TPU v7x, 256 devices: a whole 4x4x8 slice. The times are simulated.
256 devices in a mesh: row: 32 (over x, z_hi, core), col: 8 (over z_lo, y).
Axes of the slice: x: 4, y: 4, z: 8 (z_hi: 4, z_lo: 2; z = z_hi * 2 + z_lo), core: 2. Of those that a mesh axis runs over, the one named last changes fastest.
Arguments:
- src_emb: bfloat16 [32768, 1024], P(('row', 'col')), may hold values from -48 to 48
- tgt_emb: bfloat16 [8192, 1024], P(('col', 'row')), may hold values from -16 to 16
- src_lang: int32 [32768], P('row'), may hold values from 0 to 3, as said below
- tgt_lang: int32 [8192], P('col'), may hold values from 0 to 3, as said below
Outputs:
- src_pull: float32 [32768, 1024], P(('row', 'col'))
- tgt_pull: float32 [8192, 1024], P(('col', 'row'))
- row_cost: float32 [32768], P(('row', 'col'))
Inputs may be any that keep to these rules, and one draw needn't show every extreme that they name: `src_lang`: every bucket holds at least one source sentence. `tgt_lang`: every bucket holds at least one target sentence.
All inputs are finite; a program needn't handle non-finite values.
Results may differ from a plain program's by a relative error of at most 0.005.
Values may be sent and summed in bfloat16 or wider, within the bound.
No kernel may reach another device: no remote copies, remote signals or barrier semaphores. Data moves between devices by JAX's collectives and lax.ppermute only.
A program may use at most 64 MiB of HBM per device.

v0:
```python
import math

import jax
import jax.numpy as jnp
from jax import lax
from jax.sharding import PartitionSpec as P

ITERS = 3


NEG = -1e30
EPSILON = 0.5


def across_targets(logits, allowed):
    local_max = jnp.max(jnp.where(allowed, logits, NEG), axis=1)
    top = lax.pmax(local_max, "col")
    partial_sum = jnp.sum(jnp.where(allowed, jnp.exp(logits - top[:, None]), 0.0), axis=1)
    total = lax.psum(partial_sum, "col")
    return top + jnp.log(total)


def across_sources(logits, allowed):
    local_max = jnp.max(jnp.where(allowed, logits, NEG), axis=0)
    top = lax.pmax(local_max, "row")
    partial_sum = jnp.sum(jnp.where(allowed, jnp.exp(logits - top[None, :]), 0.0), axis=0)
    total = lax.psum(partial_sum, "row")
    return top + jnp.log(total)


def shards(src_emb, tgt_emb, src_lang, tgt_lang):
    root = math.sqrt(src_emb.shape[1])
    total_src = src_lang.shape[0] * lax.axis_size("row")
    total_tgt = tgt_lang.shape[0] * lax.axis_size("col")
    src_block = lax.all_gather(src_emb, "col", axis=0, tiled=True)
    tgt_block = lax.all_gather(tgt_emb, "row", axis=0, tiled=True)
    product = lax.dot_general(
        src_block, tgt_block, (((1,), (1,)), ((), ())), preferred_element_type=jnp.float32
    )
    cost = product * (-1.0 / root)
    allowed = src_lang[:, None] == tgt_lang[None, :]
    tgt_pot = jnp.zeros((cost.shape[1],), jnp.float32)
    src_pot = jnp.zeros((cost.shape[0],), jnp.float32)
    for step in range(ITERS):
        src_pot = -EPSILON * (
            across_targets((tgt_pot[None, :] - cost) / EPSILON, allowed) - math.log(total_tgt)
        )
        tgt_pot = -EPSILON * (
            across_sources((src_pot[:, None] - cost) / EPSILON, allowed) - math.log(total_src)
        )
    weight = jnp.where(
        allowed, jnp.exp((src_pot[:, None] + tgt_pot[None, :] - cost) / EPSILON), 0.0
    )
    weight_low = weight.astype(jnp.bfloat16)
    cost_terms = jnp.sum(weight * cost, axis=1) / total_tgt
    src_terms = jnp.dot(weight_low, tgt_block, preferred_element_type=jnp.float32) / total_tgt
    src_pull, row_cost = (
        lax.psum_scatter(src_terms, "col", scatter_dimension=0, tiled=True),
        lax.psum_scatter(cost_terms, "col", scatter_dimension=0, tiled=True),
    )
    tgt_terms = (
        lax.dot_general(
            weight_low, src_block, (((0,), (0,)), ((), ())), preferred_element_type=jnp.float32
        )
        / total_src
    )
    tgt_pull = lax.psum_scatter(tgt_terms, "row", scatter_dimension=0, tiled=True)
    return (src_pull, tgt_pull, row_cost)


def solution(mesh):
    return jax.shard_map(
        shards,
        mesh=mesh,
        in_specs=(P(("row", "col"), None), P(("col", "row"), None), P("row"), P("col")),
        out_specs=(P(("row", "col"), None), P(("col", "row"), None), P(("row", "col"))),
        check_vma=False,
    )
```

profile of v0, /device:TPU:2, one launch (start us, length us, event | category | flops | bytes accessed | tf_op | source)
XLA Modules:
  0.0 837.9 jit_solution(1637866949791631170)
XLA Ops:
  8.7 48.0 %all-gather.3.cloned.1.call-done = bf16[1024,1024]{1,0:T(8,128)(2,1)} async-done(((bf16[128,1024]{1,0:T(8,128)(2,1)}), bf16[1024,1024]{1,0:T(8,128)(2,1)}) %all-gather.3.cloned.1.call-update) | async-done | bytes 2097168 | tf_op jit(solution)/shard_map/all_gather | solution.py:35
  56.8 55.4 %all-gather.5.cloned.1.call-done = bf16[1024,1024]{1,0:T(8,128)(2,1)} async-done(((bf16[32,1024]{1,0:T(8,128)(2,1)}), bf16[1024,1024]{1,0:T(8,128)(2,1)}) %all-gather.5.cloned.1.call-update) | async-done | bytes 2097168 | tf_op jit(solution)/shard_map/all_gather | solution.py:36
  112.2 6.8 fusion
  119.0 18.9 %pmax.42 = f32[1024]{0:T(1024)S(1)} all-reduce(f32[1024]{0:T(1024)S(1)} %get-tuple-element.3), channel_id=1, replica_groups=mesh['row'=32,'col'=8] {'col'}, use_global_device_ids=true, to_apply=%region_1.2 | all-reduce | flops 1024 | bytes 8192 | tf_op jit(solution)/shard_map/pmax | solution.py:17
  140.8 16.0 %psum.42 = f32[1024]{0:T(1024)S(1)} all-reduce(f32[1024]{0:T(1024)S(1)} %fusion.1), channel_id=1, replica_groups=mesh['row'=32,'col'=8] {'col'}, use_global_device_ids=true, to_apply=%region_3.4 | all-reduce | flops 1024 | bytes 8192 | tf_op jit(solution)/shard_map/psum | solution.py:19
  159.8 60.2 %pmax.43 = f32[1024]{0:T(1024)S(1)} all-reduce(f32[1024]{0:T(1024)S(1)} %fusion.2), channel_id=1, replica_groups=mesh['row'=32,'col'=8] {'row'}, use_global_device_ids=true, to_apply=%region_5.6 | all-reduce | flops 1024 | bytes 8192 | tf_op jit(solution)/shard_map/pmax | solution.py:25
  220.0 3.1 fusion.3
  223.1 61.0 %psum.43 = f32[1024]{0:T(1024)S(1)} all-reduce(f32[1024]{0:T(1024)S(1)} %fusion.3), channel_id=1, replica_groups=mesh['row'=32,'col'=8] {'row'}, use_global_device_ids=true, to_apply=%region_7.8 | all-reduce | flops 1024 | bytes 8192 | tf_op jit(solution)/shard_map/psum | solution.py:27
  286.7 18.1 %pmax.44 = f32[1024]{0:T(1024)S(1)} all-reduce(f32[1024]{0:T(1024)S(1)} %fusion.4), channel_id=1, replica_groups=mesh['row'=32,'col'=8] {'col'}, use_global_device_ids=true, to_apply=%region_9.10 | all-reduce | flops 1024 | bytes 8192 | tf_op jit(solution)/shard_map/pmax | solution.py:17
  307.8 16.0 %psum.44 = f32[1024]{0:T(1024)S(1)} all-reduce(f32[1024]{0:T(1024)S(1)} %fusion.5), channel_id=1, replica_groups=mesh['row'=32,'col'=8] {'col'}, use_global_device_ids=true, to_apply=%region_11.12 | all-reduce | flops 1024 | bytes 8192 | tf_op jit(solution)/shard_map/psum | solution.py:19
  326.8 69.9 %pmax.45 = f32[1024]{0:T(1024)S(1)} all-reduce(f32[1024]{0:T(1024)S(1)} %fusion.6), channel_id=1, replica_groups=mesh['row'=32,'col'=8] {'row'}, use_global_device_ids=true, to_apply=%region_13.14 | all-reduce | flops 1024 | bytes 8192 | tf_op jit(solution)/shard_map/pmax | solution.py:25
  396.7 3.1 fusion.7
  399.8 69.9 %psum.45 = f32[1024]{0:T(1024)S(1)} all-reduce(f32[1024]{0:T(1024)S(1)} %fusion.7), channel_id=1, replica_groups=mesh['row'=32,'col'=8] {'row'}, use_global_device_ids=true, to_apply=%region_15.16 | all-reduce | flops 1024 | bytes 8192 | tf_op jit(solution)/shard_map/psum | solution.py:27
  472.3 18.0 %pmax.46 = f32[1024]{0:T(1024)S(1)} all-reduce(f32[1024]{0:T(1024)S(1)} %fusion.8), channel_id=1, replica_groups=mesh['row'=32,'col'=8] {'col'}, use_global_device_ids=true, to_apply=%region_17.18 | all-reduce | flops 1024 | bytes 8192 | tf_op jit(solution)/shard_map/pmax | solution.py:17
  493.3 16.0 %psum.46 = f32[1024]{0:T(1024)S(1)} all-reduce(f32[1024]{0:T(1024)S(1)} %fusion.9), channel_id=1, replica_groups=mesh['row'=32,'col'=8] {'col'}, use_global_device_ids=true, to_apply=%region_19.20 | all-reduce | flops 1024 | bytes 8192 | tf_op jit(solution)/shard_map/psum | solution.py:19
  509.3 3.2 fusion.10
  512.5 69.9 %pmax.47 = f32[1024]{0:T(1024)S(1)} all-reduce(f32[1024]{0:T(1024)S(1)} %fusion.10), channel_id=1, replica_groups=mesh['row'=32,'col'=8] {'row'}, use_global_device_ids=true, to_apply=%region_21.22 | all-reduce | flops 1024 | bytes 8192 | tf_op jit(solution)/shard_map/pmax | solution.py:25
  585.5 70.1 %psum.47 = f32[1024]{0:T(1024)S(1)} all-reduce(f32[1024]{0:T(1024)S(1)} %fusion.11), channel_id=1, replica_groups=mesh['row'=32,'col'=8] {'row'}, use_global_device_ids=true, to_apply=%region_23.24 | all-reduce | flops 1024 | bytes 8192 | tf_op jit(solution)/shard_map/psum | solution.py:27
  655.6 6.8 convolution_multiply_fusion
  664.0 6.8 convolution_multiply_fusion.1
  672.7 3.1 multiply_reduce_fusion
  675.9 17.9 %all-reduce = f32[1024]{0:T(1024)S(1)} all-reduce(f32[1024]{0:T(1024)S(1)} %broadcast_multiply_fusion), channel_id=4, replica_groups=mesh['row'=32,'col'=8] {'col'}, use_global_device_ids=true, to_apply=%region_27.28.clone | all-reduce | flops 1024 | bytes 8192
  694.3 79.7 %reduce-scatter.5.cloned.1.call-done = f32[32,1024]{1,0:T(8,128)} async-done(((f32[1024,1024]{1,0:T(8,128)}), f32[32,1024]{1,0:T(8,128)}) %reduce-scatter.5.cloned.1.call-update) | async-done | bytes 131088 | tf_op jit(solution)/shard_map/reduce_scatter | solution.py:67
  774.0 57.4 %reduce-scatter.3.cloned.1.call-done = f32[128,1024]{1,0:T(8,128)} async-done(((f32[1024,1024]{1,0:T(8,128)}), f32[128,1024]{1,0:T(8,128)}) %reduce-scatter.3.cloned.1.call-update) | async-done | bytes 524304 | tf_op jit(solution)/shard_map/reduce_scatter | solution.py:58
  (35 shorter events, 28.3 us)
Async XLA Ops:
  7.2 49.6 %all-gather.3.cloned.1.call-start = ((), (), s32[]{:S(2)}) async-start(), calls=%async_computation.2 | async-start | bytes 2359296 | tf_op jit(solution)/shard_map/all_gather | solution.py:35
  7.9 104.3 %all-gather.5.cloned.1.call-start = ((), (), s32[]{:S(2)}) async-start(), calls=%async_computation.3 | async-start | bytes 2162688 | tf_op jit(solution)/shard_map/all_gather | solution.py:36
  8.6 129.2 %copy-start = (s32[1024]{0:T(1024)S(1)}, s32[1024]{0:T(1024)}, u32[]{:S(2)}) copy-start(s32[1024]{0:T(1024)} %param.6) | copy-start | bytes 12292
  8.7 129.2 %copy-start.1 = (s32[1024]{0:T(1024)S(1)}, s32[1024]{0:T(1024)}, u32[]{:S(2)}) copy-start(s32[1024]{0:T(1024)} %param.7) | copy-start | bytes 12292
  8.7 765.3 %reduce-scatter.5.cloned.1.call-start = ((), (), s32[]{:S(2)}) async-start(), calls=%async_computation.5 | async-start | bytes 4325376 | tf_op jit(solution)/shard_map/reduce_scatter | solution.py:67
  509.3 146.3 %copy-start.3 = (bf16[1024,1024]{1,0:T(8,128)(2,1)S(1)}, bf16[1024,1024]{1,0:T(8,128)(2,1)}, u32[]{:S(2)}) copy-start(bf16[1024,1024]{1,0:T(8,128)(2,1)} %all-gather.3.cloned.1.call-done) | copy-start | bytes 6291460
  662.4 1.6 copy-start.2
  662.4 169.0 %reduce-scatter.3.cloned.1.call-start = ((), (), s32[]{:S(2)}) async-start(), calls=%async_computation.4 | async-start | bytes 4718592 | tf_op jit(solution)/shard_map/reduce_scatter | solution.py:58
  670.8 0.7 copy-start.4
Sparse Core Ops, SparseCore 0:
  9.8 46.9 all-gather.2
  59.3 52.8 all-gather.4
  662.5 111.4 reduce-scatter.4
  777.2 54.1 reduce-scatter.2
where the time goes:
time: 839 us; the launch traced here: 838 us
  blocking collectives  522 us (62%)
  waiting for transfers between devices  242 us (29%)
  other arithmetic  35.9 us (4%)
  matrix products  20.4 us (2%)
  between operations  14.6 us (2%)
    psum x3, blocking collectives, across_sources(): total = lax.psum(partial_sum, 'row')  201 us
    pmax x3, blocking collectives, across_sources(): top = lax.pmax(local_max, 'row')  200 us
    reduce_scatter x1, waiting for transfers between devices, shards(): lax.psum_scatter(tgt_terms, 'row', scatter_dimension=0, tiled=True)  79.7 us
    reduce_scatter x1, waiting for transfers between devices, shards(): lax.psum_scatter(src_terms, 'col', scatter_dimension=0, tiled=True)  57.4 us
    all_gather x1, waiting for transfers between devices, shards(): tgt_block = lax.all_gather(tgt_emb, 'row', axis=0, tiled=True)  55.4 us
    pmax x3, blocking collectives, across_targets(): top = lax.pmax(local_max, 'col')  54.9 us
    all_gather x1, waiting for transfers between devices, shards(): src_block = lax.all_gather(src_emb, 'col', axis=0, tiled=True)  48 us
    psum x3, blocking collectives, across_targets(): total = lax.psum(partial_sum, 'col')  47.9 us
  transfers between devices with their start and end apart: 4, of which 4 were waited for; matrix products, arithmetic and copies ran while one was open for 1% of the time, Pallas kernels for 0%

commit v1 on v0

v1 whole, which is shorter than its diff:
```python
import math

import jax
import jax.numpy as jnp
from jax import lax
from jax.sharding import Mesh, PartitionSpec as P

ITERS = 3
NEG = -1e30
EPSILON = 0.5
LOG2E = math.log2(math.e)

AXES = ("x", "zh", "core", "zl", "y")
SIZES = (4, 4, 2, 2, 4)
ROW = ("x", "zh", "core")
COL = ("zl", "y")
RING = ("zh", "zl")
PLANE = ("x", "y")
SPREAD = ("x", "y", "core")


def gather(value, axes):
    size = lax.axis_size(axes)
    return lax.all_to_all(jnp.broadcast_to(value, (size, *value.shape)), axes, 0, 0)


def shift(value, step):
    size = lax.axis_size(RING)
    return lax.ppermute(value, RING, [(i, (i + step) % size) for i in range(size)])


def ring_gather(value):
    size = lax.axis_size(RING)
    up = down = value
    found = {0: value}
    for step in range(1, size // 2):
        up, down = shift(up, 1), shift(down, -1)
        found[-step], found[step] = up, down
    half = value.shape[0] // 2
    found[size // 2] = jnp.concatenate([shift(up[:half], 1), shift(down[half:], -1)])
    return found


def log2sumexp2(values, axis):
    top = jnp.max(values, axis=axis)
    total = jnp.sum(jnp.exp2(values - jnp.expand_dims(top, axis)), axis=axis)
    return top + jnp.log2(total)


def shards(src_emb, tgt_emb, src_lang, tgt_lang):
    rows, depth = src_emb.shape
    columns = tgt_emb.shape[0]
    row, col = lax.axis_index(ROW), lax.axis_index(COL)
    ring = lax.axis_size(RING)
    place = lax.axis_index(RING)
    core = lax.axis_index("core")
    total_src = src_lang.shape[0] * lax.axis_size(ROW)
    total_tgt = tgt_lang.shape[0] * lax.axis_size(COL)

    own_src_lang = lax.dynamic_slice(src_lang, (col * rows,), (rows,))
    own_tgt_lang = lax.dynamic_slice(tgt_lang, (row * columns,), (columns,))
    src_langs = gather(own_src_lang.reshape(1, rows), RING).reshape(ring, rows)
    tgt_langs = gather(own_tgt_lang.reshape(1, columns), SPREAD).reshape(-1)

    found = ring_gather(src_emb)
    src_block = jnp.concatenate([found[k] for k in range(1 - ring // 2, ring // 2 + 1)])
    order = (place + jnp.arange(1 - ring // 2, ring // 2 + 1)) % ring
    src_block_lang = src_langs[order].reshape(-1)

    mine = gather(tgt_emb, PLANE)
    theirs = lax.ppermute(mine, "core", [(0, 1), (1, 0)])
    both = jnp.where(core == 0, jnp.stack([mine, theirs], 1), jnp.stack([theirs, mine], 1))
    tgt_block = both.reshape(-1, depth)

    product = lax.dot_general(
        src_block, tgt_block, (((1,), (1,)), ((), ())), preferred_element_type=jnp.float32
    )
    allowed = src_block_lang[:, None] == tgt_langs[None, :]
    logits = jnp.where(allowed, product * (LOG2E / (EPSILON * math.sqrt(depth))), NEG)
    tgt_pot = jnp.zeros((logits.shape[1],), jnp.float32)
    for step in range(ITERS):
        part = log2sumexp2(logits + tgt_pot[None, :], 1)
        part = jnp.zeros((ring, rows)).at[order].set(part.reshape(ring, rows))
        whole = log2sumexp2(gather(part, RING), 0)
        src_pot = math.log2(total_tgt) - whole[order].reshape(-1)
        part = log2sumexp2(logits + src_pot[:, None], 0)
        whole = log2sumexp2(gather(part.reshape(8, -1), SPREAD), 0).reshape(-1)
        tgt_pot = math.log2(total_src) - whole
    weight = jnp.exp2(logits + src_pot[:, None] + tgt_pot[None, :])
    weight_low = weight.astype(jnp.bfloat16)
    cost_terms = jnp.sum(weight * logits, axis=1) * (-EPSILON / LOG2E / total_tgt)
    src_terms = jnp.dot(weight_low, tgt_block, preferred_element_type=jnp.float32) / total_tgt
    src_terms = src_terms.reshape(ring, rows, depth)
    tgt_terms = (
        lax.dot_general(
            weight_low, src_block, (((0,), (0,)), ((), ())), preferred_element_type=jnp.float32
        )
        / total_src
    )
    tgt_terms = tgt_terms.reshape(-1, 2, columns, depth)
    keep = jnp.where(core == 0, tgt_terms[:, 0], tgt_terms[:, 1])
    give = jnp.where(core == 0, tgt_terms[:, 1], tgt_terms[:, 0]).astype(jnp.bfloat16)
    keep = keep + lax.ppermute(give, "core", [(0, 1), (1, 0)]).astype(jnp.float32)
    parts = lax.all_to_all(keep.astype(jnp.bfloat16), PLANE, 0, 0)
    tgt_pull = jnp.sum(parts.astype(jnp.float32), axis=0)
    base = ring // 2 - 1
    half = rows // 2
    up = src_terms[base + ring // 2]
    up, down = up[:half].astype(jnp.bfloat16), up[half:].astype(jnp.bfloat16)
    up = shift(up, 1).astype(jnp.float32)
    down = shift(down, -1).astype(jnp.float32)
    pad = jnp.zeros((half, depth), jnp.float32)
    up, down = jnp.concatenate([up, pad]), jnp.concatenate([pad, down])
    for distance in range(ring // 2 - 1, 0, -1):
        up = shift((up + src_terms[base + distance]).astype(jnp.bfloat16), 1).astype(jnp.float32)
        down = shift((down + src_terms[base - distance]).astype(jnp.bfloat16), -1).astype(jnp.float32)
    src_pull = src_terms[base] + up + down
    costs = jnp.zeros((ring, rows)).at[order].set(cost_terms.reshape(ring, rows))
    row_cost = jnp.sum(lax.all_to_all(costs.reshape(ring, 1, rows), RING, 0, 0), axis=0)[0]
    return (src_pull, tgt_pull, row_cost)


def solution(mesh):
    split = Mesh(mesh.devices.reshape(SIZES), AXES)
    return jax.shard_map(
        shards,
        mesh=split,
        in_specs=(P(ROW + COL, None), P(COL + ROW, None), P(ROW), P(COL)),
        out_specs=(P(ROW + COL, None), P(COL + ROW, None), P(ROW + COL)),
        check_vma=False,
    )
```

time: 839 us -> 225 us (0.27)
  blocking collectives: 522 us -> 85.9 us
  waiting for transfers between devices: 242 us -> 31.5 us
  starting transfers between devices: 0.16 us -> 47.1 us
  between operations: 14.6 us -> 1.21 us
  matrix products: 20.4 us -> 10.5 us
  local copies, waits for them, and re-layouts: 3.35 us -> 12.7 us
    pmax x6 -> x0, blocking collectives: 255 us -> none  [the longest x3 200 us: across_sources(): top = lax.pmax(local_max, 'row')]
    psum x6 -> x0, blocking collectives: 249 us -> none  [the longest x3 201 us: across_sources(): total = lax.psum(partial_sum, 'row')]
    reduce_scatter x2 -> x0, waiting for transfers between devices: 137 us -> none  [the longest x1 79.7 us: shards(): lax.psum_scatter(tgt_terms, 'row', scatter_dimension=0, tiled=True)]
    all_gather x2 -> x0, waiting for transfers between devices: 103 us -> none  [the longest x1 55.4 us: shards(): tgt_block = lax.all_gather(tgt_emb, 'row', axis=0, tiled=True)]
    all_to_all x0 -> x7, blocking collectives: none -> 85.9 us  [gather(): lax.all_to_all(jnp.broadcast_to(value, (size, *value.shape)), axes, 0, 0)]
    ppermute x0 -> x18, starting transfers between devices: none -> 25.5 us  [the longest x16 25.3 us: shift(): lax.ppermute(value, RING, [(i, (i + step) % size) for i in range(size)])]
    ppermute x0 -> x18, waiting for transfers between devices: none -> 23.6 us  [the longest x16 23.6 us: shift(): lax.ppermute(value, RING, [(i, (i + step) % size) for i in range(size)])]
    all_to_all x0 -> x4, starting transfers between devices: none -> 21.5 us  [the longest x2 12.5 us: gather(): lax.all_to_all(jnp.broadcast_to(value, (size, *value.shape)), axes, 0, 0)]
  transfers between devices with their start and end apart: 4 -> 22, of which waited for: 4 -> 9; matrix products, arithmetic and copies ran while one was open for 1% -> 6% of each run, Pallas kernels for 0% -> 0%
where the time goes in v1:
time: 225 us; the launch traced here: 224 us
  blocking collectives  85.9 us (38%)
  starting transfers between devices  47.1 us (21%)
  other arithmetic  34.8 us (15%)
  waiting for transfers between devices  31.5 us (14%)
  local copies, waits for them, and re-layouts  12.7 us (6%)
  matrix products  10.5 us (5%)
    all_to_all x7, blocking collectives, gather(): lax.all_to_all(jnp.broadcast_to(value, (size, *value.shape)), axes, 0, 0)  85.9 us
    ppermute x16, starting transfers between devices, shift(): lax.ppermute(value, RING, [(i, (i + step) % size) for i in range(size)])  25.3 us
    ppermute x16, waiting for transfers between devices, shift(): lax.ppermute(value, RING, [(i, (i + step) % size) for i in range(size)])  23.6 us
    reduce_max x11, other arithmetic, log2sumexp2(): top = jnp.max(values, axis=axis)  13.6 us
    all_to_all x2, starting transfers between devices, gather(): lax.all_to_all(jnp.broadcast_to(value, (size, *value.shape)), axes, 0, 0)  12.5 us
    reduce_sum x12, other arithmetic, log2sumexp2(): total = jnp.sum(jnp.exp2(values - jnp.expand_dims(top, axis)), axis=axis)  6.08 us
    unnamed x30, local copies, waits for them, and re-layouts  5.7 us
    dot_general x1, matrix products, shards(): lax.dot_general(weight_low, src_block, (((0,), (0,)), ((), ())), preferre...  5.43 us
  transfers between devices with their start and end apart: 22, of which 9 were waited for; matrix products, arithmetic and copies ran while one was open for 6% of the time, Pallas kernels for 0%

profile of v1, /device:TPU:2, one launch (start us, length us, event | category | flops | bytes accessed | tf_op | source)
XLA Modules:
  0.0 223.7 jit_solution(5064936084096504136)
XLA Ops:
  2.1 7.6 %all-to-all-start.1 = ((s32[32,1,32]{2,1,0:T(1,128)}), s32[32,1,32]{2,1,0:T(1,128)S(1)}, u32[]{:S(2)}, u32[]{:S(2)}) async-start(s32[32,1,32]{2,1,0:T(1,128)} %broadcast_in_dim.23), calls=%async_computation.1 | async-start | bytes 32768 | tf_op jit(solution)/shard_map/all_to_all | solution.py:24
  10.5 5.3 %all-to-all-done.1 = s32[32,1,32]{2,1,0:T(1,128)S(1)} async-done(((s32[32,1,32]{2,1,0:T(1,128)}), s32[32,1,32]{2,1,0:T(1,128)S(1)}, u32[]{:S(2)}, u32[]{:S(2)}) %all-to-all-start.1) | async-done | bytes 4128 | tf_op jit(solution)/shard_map/all_to_all | solution.py:24
  15.8 15.9 %all_to_all.55 = s32[8,1,128]{2,1,0:T(1,128)S(1)} all-to-all(s32[8,1,128]{2,1,0:T(1,128)S(1)} %broadcast_in_dim.22), channel_id=1, replica_groups=mesh['x'=4,'zh'=4,'core'=2,'zl'=2,'y'=4] {'zh','zl'}, dimensions={0} | all-to-all | bytes 8192 | tf_op jit(solution)/shard_map/all_to_all | solution.py:24
  33.7 4.9 %all-to-all-start.2 = ((bf16[16,32,1024]{2,1,0:T(8,128)(2,1)}), bf16[16,32,1024]{2,1,0:T(8,128)(2,1)S(1)}, u32[]{:S(2)}, u32[]{:S(2)}) async-start(bf16[16,32,1024]{2,1,0:T(8,128)(2,1)} %broadcast_in_dim.24), calls=%async_computation.2 | async-start | bytes 2097152 | tf_op jit(solution)/shard_map/all_to_all | solution.py:24
  41.8 4.6 %collective-permute-done = bf16[128,1024]{1,0:T(8,128)(2,1)S(1)} collective-permute-done((bf16[128,1024]{1,0:T(8,128)(2,1)}, bf16[128,1024]{1,0:T(8,128)(2,1)S(1)}, u32[]{:S(2)}, u32[]{:S(2)}) %collective-permute-start) | collective-permute-done | bytes 262176 | tf_op jit(solution)/shard_map/ppermute | solution.py:29
  46.4 3.2 %collective-permute-start.4 = (bf16[128,1024]{1,0:T(8,128)(2,1)S(1)}, bf16[128,1024]{1,0:T(8,128)(2,1)S(1)}, u32[]{:S(2)}, u32[]{:S(2)}) collective-permute-start(bf16[128,1024]{1,0:T(8,128)(2,1)S(1)} %collective-permute-done.3), channel_id=1, source_target_pairs={{0,52},{4,0},{16,4},{20,16},{32,20},{36,32},{48,36},{52,48},{1,53}... | collective-permute-start | bytes 786440 | tf_op jit(solution)/shard_map/ppermute | solution.py:29
  49.6 4.3 %collective-permute-done.1 = bf16[128,1024]{1,0:T(8,128)(2,1)S(1)} collective-permute-done((bf16[128,1024]{1,0:T(8,128)(2,1)S(1)}, bf16[128,1024]{1,0:T(8,128)(2,1)S(1)}, u32[]{:S(2)}, u32[]{:S(2)}) %collective-permute-start.1) | collective-permute-done | bytes 262176 | tf_op jit(solution)/shard_map/ppermute | solution.py:29
  54.0 3.2 %collective-permute-start.5 = (bf16[128,1024]{1,0:T(8,128)(2,1)S(1)}, bf16[128,1024]{1,0:T(8,128)(2,1)S(1)}, u32[]{:S(2)}, u32[]{:S(2)}) collective-permute-start(bf16[128,1024]{1,0:T(8,128)(2,1)S(1)} %collective-permute-done.4), channel_id=1, source_target_pairs={{0,52},{4,0},{16,4},{20,16},{32,20},{36,32},{48,36},{52,48},{1,53}... | collective-permute-start | bytes 786440 | tf_op jit(solution)/shard_map/ppermute | solution.py:29
  59.1 3.2 %collective-permute-done.2 = bf16[128,1024]{1,0:T(8,128)(2,1)S(1)} collective-permute-done((bf16[128,1024]{1,0:T(8,128)(2,1)S(1)}, bf16[128,1024]{1,0:T(8,128)(2,1)S(1)}, u32[]{:S(2)}, u32[]{:S(2)}) %collective-permute-start.2) | collective-permute-done | bytes 262176 | tf_op jit(solution)/shard_map/ppermute | solution.py:29
  62.4 3.4 %collective-permute-start.7 = (bf16[64,1024]{1,0:T(8,128)(2,1)S(1)}, bf16[64,1024]{1,0:T(8,128)(2,1)S(1)}, u32[]{:S(2)}, u32[]{:S(2)}) collective-permute-start(bf16[64,1024]{1,0:T(8,128)(2,1)S(1)} %slice.77), channel_id=1, source_target_pairs={{0,52},{4,0},{16,4},{20,16},{32,20},{36,32},{48,36},{52,48},{1,53}... | collective-permute-start | bytes 393224 | tf_op jit(solution)/shard_map/ppermute | solution.py:29
  74.6 12.5 %all_to_all.56 = f32[8,8,128]{2,1,0:T(8,128)S(1)} all-to-all(f32[8,8,128]{2,1,0:T(8,128)S(1)} %broadcast_in_dim.26), channel_id=1, replica_groups=mesh['x'=4,'zh'=4,'core'=2,'zl'=2,'y'=4] {'zh','zl'}, dimensions={0} | all-to-all | bytes 65536 | tf_op jit(solution)/shard_map/all_to_all | solution.py:24
  87.7 2.7 %add_reduce_fusion.3 = f32[1024]{0:T(1024)S(1)} fusion(f32[1024,1024]{0,1:T(8,128)} %copy-done, f32[1024]{0:T(1024)S(1)} %subtract_bitcast_fusion.5), kind=kLoop, calls=%fused_computation.20 | loop fusion | flops 2096128 | bytes 4202496 | tf_op jit(solution)/shard_map/reduce_max | solution.py:45
  92.3 14.1 %all_to_all.57 = f32[32,8,128]{2,1,0:T(8,128)S(1)} all-to-all(f32[32,8,128]{2,1,0:T(8,128)S(1)} %broadcast_in_dim.27), channel_id=1, replica_groups=mesh['x'=4,'zh'=4,'core'=2,'zl'=2,'y'=4] {'x','y','core'}, dimensions={0} | all-to-all | bytes 262144 | tf_op jit(solution)/shard_map/all_to_all | solution.py:24
  111.4 10.4 %all_to_all.58 = f32[8,8,128]{2,1,0:T(8,128)S(1)} all-to-all(f32[8,8,128]{2,1,0:T(8,128)S(1)} %broadcast_in_dim.28), channel_id=1, replica_groups=mesh['x'=4,'zh'=4,'core'=2,'zl'=2,'y'=4] {'zh','zl'}, dimensions={0} | all-to-all | bytes 65536 | tf_op jit(solution)/shard_map/all_to_all | solution.py:24
  127.1 11.3 %all_to_all.59 = f32[32,8,128]{2,1,0:T(8,128)S(1)} all-to-all(f32[32,8,128]{2,1,0:T(8,128)S(1)} %broadcast_in_dim.29), channel_id=1, replica_groups=mesh['x'=4,'zh'=4,'core'=2,'zl'=2,'y'=4] {'x','y','core'}, dimensions={0} | all-to-all | bytes 262144 | tf_op jit(solution)/shard_map/all_to_all | solution.py:24
  143.3 10.4 %all_to_all.60 = f32[8,8,128]{2,1,0:T(8,128)S(1)} all-to-all(f32[8,8,128]{2,1,0:T(8,128)S(1)} %broadcast_in_dim.30), channel_id=1, replica_groups=mesh['x'=4,'zh'=4,'core'=2,'zl'=2,'y'=4] {'zh','zl'}, dimensions={0} | all-to-all | bytes 65536 | tf_op jit(solution)/shard_map/all_to_all | solution.py:24
  158.9 11.3 %all_to_all.61 = f32[32,8,128]{2,1,0:T(8,128)S(1)} all-to-all(f32[32,8,128]{2,1,0:T(8,128)S(1)} %broadcast_in_dim.31), channel_id=1, replica_groups=mesh['x'=4,'zh'=4,'core'=2,'zl'=2,'y'=4] {'x','y','core'}, dimensions={0} | all-to-all | bytes 262144 | tf_op jit(solution)/shard_map/all_to_all | solution.py:24
  170.3 5.4 %convolution_multiply_fusion = f32[1024,1024]{1,0:T(8,128)S(1)} fusion(bf16[1024,1024]{1,0:T(8,128)(2,1)} %copy-done.10, f32[1024,1024]{0,1:T(8,128)} %copy-done, f32[1024]{0:T(1024)S(1)} %subtract_bitcast_fusion, f32[1024]{0:T(1024)S(1)} %subtract_bitcast_fusion.1), kind=kOutput, calls=%fused_computation.23 | convolution fusion | flops 2152726528 | bytes 10493952 | tf_op jit(solution)/shard_map/dot_general | solution.py:95
  180.9 3.7 %collective-permute-done.13 = bf16[64,1024]{1,0:T(8,128)(2,1)S(1)} collective-permute-done((bf16[64,1024]{1,0:T(8,128)(2,1)S(1)}, bf16[64,1024]{1,0:T(8,128)(2,1)S(1)}, u32[]{:S(2)}, u32[]{:S(2)}) %collective-permute-start.13) | collective-permute-done | bytes 131104 | tf_op jit(solution)/shard_map/ppermute | solution.py:29
  186.6 2.8 %collective-permute-start.14 = (bf16[128,1024]{1,0:T(8,128)(2,1)S(1)}, bf16[128,1024]{1,0:T(8,128)(2,1)S(1)}, u32[]{:S(2)}, u32[]{:S(2)}) collective-permute-start(bf16[128,1024]{1,0:T(8,128)(2,1)S(1)} %get-tuple-element.8), channel_id=1, source_target_pairs={{0,52},{4,0},{16,4},{20,16},{32,20},{36,32},{48,36},{52,48},{1,53}... | collective-permute-start | bytes 786440 | tf_op jit(solution)/shard_map/ppermute | solution.py:29
  191.6 4.1 %all-to-all-start.10 = ((f32[8,1,128]{2,1,0:T(1,128)}), f32[8,1,128]{2,1,0:T(1,128)S(1)}, u32[]{:S(2)}, u32[]{:S(2)}) async-start(f32[8,1,128]{2,1,0:T(1,128)} %bitcast.25), calls=%async_computation.10 | async-start | bytes 8192 | tf_op jit(solution)/shard_map/all_to_all | solution.py:119
  200.5 3.9 %fusion.3 = bf16[16,32,1024]{2,1,0:T(8,128)(2,1)} fusion(bf16[16,32,1024]{2,1,0:T(8,128)(2,1)S(1)} %collective-permute-done.17, f32[16,2,32,1024]{3,2,1,0:T(8,128)} %bitcast.68, pred[]{:T(512)S(6)} %eq.29), kind=kLoop, calls=%fused_computation.29 | loop fusion | flops 2097152 | bytes 6291457 | tf_op jit(solution)/shard_map/convert_element_type | solution.py:104
  204.4 4.9 %all-to-all-start.9 = ((bf16[16,32,1024]{2,1,0:T(8,128)(2,1)}), bf16[16,32,1024]{2,1,0:T(8,128)(2,1)S(1)}, u32[]{:S(2)}, u32[]{:S(2)}) async-start(bf16[16,32,1024]{2,1,0:T(8,128)(2,1)} %fusion.3), calls=%async_computation.9 | async-start | bytes 2097152 | tf_op jit(solution)/shard_map/all_to_all | solution.py:104
  214.6 3.8 %collective-permute-done.12 = bf16[128,1024]{1,0:T(8,128)(2,1)S(1)} collective-permute-done((bf16[128,1024]{1,0:T(8,128)(2,1)S(1)}, bf16[128,1024]{1,0:T(8,128)(2,1)S(1)}, u32[]{:S(2)}, u32[]{:S(2)}) %collective-permute-start.12) | collective-permute-done | bytes 262176 | tf_op jit(solution)/shard_map/ppermute | solution.py:29
  (133 shorter events, 65.3 us)
Async XLA Ops:
  0.6 65.3 %copy-start.9 = (bf16[128,1024]{1,0:T(8,128)(2,1)S(1)}, bf16[128,1024]{1,0:T(8,128)(2,1)}, u32[]{:S(2)}) copy-start(bf16[128,1024]{1,0:T(8,128)(2,1)} %param.4) | copy-start | bytes 786436
  2.1 13.7 %all-to-all-start.1 = ((s32[32,1,32]{2,1,0:T(1,128)}), s32[32,1,32]{2,1,0:T(1,128)S(1)}, u32[]{:S(2)}, u32[]{:S(2)}) async-start(s32[32,1,32]{2,1,0:T(1,128)} %broadcast_in_dim.23), calls=%async_computation.1 | async-start | bytes 32768 | tf_op jit(solution)/shard_map/all_to_all | solution.py:24
  33.7 32.1 %all-to-all-start.2 = ((bf16[16,32,1024]{2,1,0:T(8,128)(2,1)}), bf16[16,32,1024]{2,1,0:T(8,128)(2,1)S(1)}, u32[]{:S(2)}, u32[]{:S(2)}) async-start(bf16[16,32,1024]{2,1,0:T(8,128)(2,1)} %broadcast_in_dim.24), calls=%async_computation.2 | async-start | bytes 2097152 | tf_op jit(solution)/shard_map/all_to_all | solution.py:24
  38.6 7.8 %collective-permute-start = (bf16[128,1024]{1,0:T(8,128)(2,1)}, bf16[128,1024]{1,0:T(8,128)(2,1)S(1)}, u32[]{:S(2)}, u32[]{:S(2)}) collective-permute-start(bf16[128,1024]{1,0:T(8,128)(2,1)} %param.4), channel_id=1, source_target_pairs={{0,4},{4,16},{16,20},{20,32},{32,36},{36,48},{48,52},{52,0},{1,5},... | collective-permute-start | bytes 786440 | tf_op jit(solution)/shard_map/ppermute | solution.py:29
  39.1 7.2 %collective-permute-start.3 = (bf16[128,1024]{1,0:T(8,128)(2,1)}, bf16[128,1024]{1,0:T(8,128)(2,1)S(1)}, u32[]{:S(2)}, u32[]{:S(2)}) collective-permute-start(bf16[128,1024]{1,0:T(8,128)(2,1)} %param.4), channel_id=1, source_target_pairs={{0,52},{4,0},{16,4},{20,16},{32,20},{36,32},{48,36},{52,48},{1,53}... | collective-permute-start | bytes 786440 | tf_op jit(solution)/shard_map/ppermute | solution.py:29
  46.4 7.6 %collective-permute-start.1 = (bf16[128,1024]{1,0:T(8,128)(2,1)S(1)}, bf16[128,1024]{1,0:T(8,128)(2,1)S(1)}, u32[]{:S(2)}, u32[]{:S(2)}) collective-permute-start(bf16[128,1024]{1,0:T(8,128)(2,1)S(1)} %collective-permute-done), channel_id=1, source_target_pairs={{0,4},{4,16},{16,20},{20,32},{32,36},{36,48},{48,52},{52,0},{1,5},... | collective-permute-start | bytes 786440 | tf_op jit(solution)/shard_map/ppermute | solution.py:29
  46.4 7.6 %collective-permute-start.4 = (bf16[128,1024]{1,0:T(8,128)(2,1)S(1)}, bf16[128,1024]{1,0:T(8,128)(2,1)S(1)}, u32[]{:S(2)}, u32[]{:S(2)}) collective-permute-start(bf16[128,1024]{1,0:T(8,128)(2,1)S(1)} %collective-permute-done.3), channel_id=1, source_target_pairs={{0,52},{4,0},{16,4},{20,16},{32,20},{36,32},{48,36},{52,48},{1,53}... | collective-permute-start | bytes 786440 | tf_op jit(solution)/shard_map/ppermute | solution.py:29
  54.0 8.3 %collective-permute-start.2 = (bf16[128,1024]{1,0:T(8,128)(2,1)S(1)}, bf16[128,1024]{1,0:T(8,128)(2,1)S(1)}, u32[]{:S(2)}, u32[]{:S(2)}) collective-permute-start(bf16[128,1024]{1,0:T(8,128)(2,1)S(1)} %collective-permute-done.1), channel_id=1, source_target_pairs={{0,4},{4,16},{16,20},{20,32},{32,36},{36,48},{48,52},{52,0},{1,5},... | collective-permute-start | bytes 786440 | tf_op jit(solution)/shard_map/ppermute | solution.py:29
  54.0 8.4 %collective-permute-start.5 = (bf16[128,1024]{1,0:T(8,128)(2,1)S(1)}, bf16[128,1024]{1,0:T(8,128)(2,1)S(1)}, u32[]{:S(2)}, u32[]{:S(2)}) collective-permute-start(bf16[128,1024]{1,0:T(8,128)(2,1)S(1)} %collective-permute-done.4), channel_id=1, source_target_pairs={{0,52},{4,0},{16,4},{20,16},{32,20},{36,32},{48,36},{52,48},{1,53}... | collective-permute-start | bytes 786440 | tf_op jit(solution)/shard_map/ppermute | solution.py:29
  62.3 6.3 %collective-permute-start.6 = (bf16[64,1024]{1,0:T(8,128)(2,1)S(1)}, bf16[64,1024]{1,0:T(8,128)(2,1)S(1)}, u32[]{:S(2)}, u32[]{:S(2)}) collective-permute-start(bf16[64,1024]{1,0:T(8,128)(2,1)S(1)} %slice.76), channel_id=1, source_target_pairs={{0,4},{4,16},{16,20},{20,32},{32,36},{36,48},{48,52},{52,0},{1,5},... | collective-permute-start | bytes 393224 | tf_op jit(solution)/shard_map/ppermute | solution.py:29
  62.4 6.2 %collective-permute-start.7 = (bf16[64,1024]{1,0:T(8,128)(2,1)S(1)}, bf16[64,1024]{1,0:T(8,128)(2,1)S(1)}, u32[]{:S(2)}, u32[]{:S(2)}) collective-permute-start(bf16[64,1024]{1,0:T(8,128)(2,1)S(1)} %slice.77), channel_id=1, source_target_pairs={{0,52},{4,0},{16,4},{20,16},{32,20},{36,32},{48,36},{52,48},{1,53}... | collective-permute-start | bytes 393224 | tf_op jit(solution)/shard_map/ppermute | solution.py:29
  65.8 2.8 %collective-permute-start.8 = (bf16[16,32,1024]{2,1,0:T(8,128)(2,1)S(1)}, bf16[16,32,1024]{2,1,0:T(8,128)(2,1)S(1)}, u32[]{:S(2)}, u32[]{:S(2)}) collective-permute-start(bf16[16,32,1024]{2,1,0:T(8,128)(2,1)S(1)} %all-to-all-done.2), channel_id=1, source_target_pairs={{0,8},{8,0},{1,9},{9,1},{2,10},{10,2},{3,11},{11,3},{4,12},{12,4},... | collective-permute-start | bytes 3145736 | tf_op jit(solution)/shard_map/ppermute | solution.py:71
  178.4 7.6 %copy-start.8 = (f32[1024,1024]{1,0:T(8,128)}, f32[1024,1024]{1,0:T(8,128)S(1)}, u32[]{:S(2)}) copy-start(f32[1024,1024]{1,0:T(8,128)S(1)} %get-tuple-element.14) | copy-start | bytes 12582916
  178.6 21.9 %collective-permute-start.17 = (bf16[16,32,1024]{2,1,0:T(8,128)(2,1)S(1)}, bf16[16,32,1024]{2,1,0:T(8,128)(2,1)S(1)}, u32[]{:S(2)}, u32[]{:S(2)}) collective-permute-start(bf16[16,32,1024]{2,1,0:T(8,128)(2,1)S(1)} %fusion.4), channel_id=1, source_target_pairs={{0,8},{8,0},{1,9},{9,1},{2,10},{10,2},{3,11},{11,3},{4,12},{12,4},... | collective-permute-start | bytes 3145736 | tf_op jit(solution)/shard_map/ppermute | solution.py:103
  178.8 5.9 %collective-permute-start.13 = (bf16[64,1024]{1,0:T(8,128)(2,1)S(1)}, bf16[64,1024]{1,0:T(8,128)(2,1)S(1)}, u32[]{:S(2)}, u32[]{:S(2)}) collective-permute-start(bf16[64,1024]{1,0:T(8,128)(2,1)S(1)} %get-tuple-element.10), channel_id=1, source_target_pairs={{0,52},{4,0},{16,4},{20,16},{32,20},{36,32},{48,36},{52,48},{1,53}... | collective-permute-start | bytes 393224 | tf_op jit(solution)/shard_map/ppermute | solution.py:29
  179.3 6.7 %collective-permute-start.9 = (bf16[64,1024]{1,0:T(8,128)(2,1)S(1)}, bf16[64,1024]{1,0:T(8,128)(2,1)S(1)}, u32[]{:S(2)}, u32[]{:S(2)}) collective-permute-start(bf16[64,1024]{1,0:T(8,128)(2,1)S(1)} %get-tuple-element.9), channel_id=1, source_target_pairs={{0,4},{4,16},{16,20},{20,32},{32,36},{36,48},{48,52},{52,0},{1,5},... | collective-permute-start | bytes 393224 | tf_op jit(solution)/shard_map/ppermute | solution.py:29
  186.1 9.6 %collective-permute-start.10 = (bf16[128,1024]{1,0:T(8,128)(2,1)S(1)}, bf16[128,1024]{1,0:T(8,128)(2,1)S(1)}, u32[]{:S(2)}, u32[]{:S(2)}) collective-permute-start(bf16[128,1024]{1,0:T(8,128)(2,1)S(1)} %get-tuple-element.7), channel_id=1, source_target_pairs={{0,4},{4,16},{16,20},{20,32},{32,36},{36,48},{48,52},{52,0},{1,5},... | collective-permute-start | bytes 786440 | tf_op jit(solution)/shard_map/ppermute | solution.py:29
  186.6 9.1 %collective-permute-start.14 = (bf16[128,1024]{1,0:T(8,128)(2,1)S(1)}, bf16[128,1024]{1,0:T(8,128)(2,1)S(1)}, u32[]{:S(2)}, u32[]{:S(2)}) collective-permute-start(bf16[128,1024]{1,0:T(8,128)(2,1)S(1)} %get-tuple-element.8), channel_id=1, source_target_pairs={{0,52},{4,0},{16,4},{20,16},{32,20},{36,32},{48,36},{52,48},{1,53}... | collective-permute-start | bytes 786440 | tf_op jit(solution)/shard_map/ppermute | solution.py:29
  191.6 12.8 %all-to-all-start.10 = ((f32[8,1,128]{2,1,0:T(1,128)}), f32[8,1,128]{2,1,0:T(1,128)S(1)}, u32[]{:S(2)}, u32[]{:S(2)}) async-start(f32[8,1,128]{2,1,0:T(1,128)} %bitcast.25), calls=%async_computation.10 | async-start | bytes 8192 | tf_op jit(solution)/shard_map/all_to_all | solution.py:119
  197.1 12.2 %collective-permute-start.11 = (bf16[128,1024]{1,0:T(8,128)(2,1)S(1)}, bf16[128,1024]{1,0:T(8,128)(2,1)S(1)}, u32[]{:S(2)}, u32[]{:S(2)}) collective-permute-start(bf16[128,1024]{1,0:T(8,128)(2,1)S(1)} %get-tuple-element.5), channel_id=1, source_target_pairs={{0,4},{4,16},{16,20},{20,32},{32,36},{36,48},{48,52},{52,0},{1,5},... | collective-permute-start | bytes 786440 | tf_op jit(solution)/shard_map/ppermute | solution.py:29
  199.2 10.1 %collective-permute-start.15 = (bf16[128,1024]{1,0:T(8,128)(2,1)S(1)}, bf16[128,1024]{1,0:T(8,128)(2,1)S(1)}, u32[]{:S(2)}, u32[]{:S(2)}) collective-permute-start(bf16[128,1024]{1,0:T(8,128)(2,1)S(1)} %get-tuple-element.6), channel_id=1, source_target_pairs={{0,52},{4,0},{16,4},{20,16},{32,20},{36,32},{48,36},{52,48},{1,53}... | collective-permute-start | bytes 786440 | tf_op jit(solution)/shard_map/ppermute | solution.py:29
  204.4 18.4 %all-to-all-start.9 = ((bf16[16,32,1024]{2,1,0:T(8,128)(2,1)}), bf16[16,32,1024]{2,1,0:T(8,128)(2,1)S(1)}, u32[]{:S(2)}, u32[]{:S(2)}) async-start(bf16[16,32,1024]{2,1,0:T(8,128)(2,1)} %fusion.3), calls=%async_computation.9 | async-start | bytes 2097152 | tf_op jit(solution)/shard_map/all_to_all | solution.py:104
  210.7 7.7 %collective-permute-start.12 = (bf16[128,1024]{1,0:T(8,128)(2,1)S(1)}, bf16[128,1024]{1,0:T(8,128)(2,1)S(1)}, u32[]{:S(2)}, u32[]{:S(2)}) collective-permute-start(bf16[128,1024]{1,0:T(8,128)(2,1)S(1)} %get-tuple-element.3), channel_id=1, source_target_pairs={{0,4},{4,16},{16,20},{20,32},{32,36},{36,48},{48,52},{52,0},{1,5},... | collective-permute-start | bytes 786440 | tf_op jit(solution)/shard_map/ppermute | solution.py:29
  211.5 6.9 %collective-permute-start.16 = (bf16[128,1024]{1,0:T(8,128)(2,1)S(1)}, bf16[128,1024]{1,0:T(8,128)(2,1)S(1)}, u32[]{:S(2)}, u32[]{:S(2)}) collective-permute-start(bf16[128,1024]{1,0:T(8,128)(2,1)S(1)} %get-tuple-element.4), channel_id=1, source_target_pairs={{0,52},{4,0},{16,4},{20,16},{32,20},{36,32},{48,36},{52,48},{1,53}... | collective-permute-start | bytes 786440 | tf_op jit(solution)/shard_map/ppermute | solution.py:29
  (9 other events, 29.9 us)

commit v2 on v1

v2 whole, which is shorter than its diff:
```python
import functools
import math

import jax
import jax.numpy as jnp
from jax import lax
from jax.experimental import pallas as pl
from jax.experimental.pallas import tpu as pltpu
from jax.sharding import Mesh, PartitionSpec as P

ITERS = 3
NEG = -1e30
EPSILON = 0.5
LOG2E = math.log2(math.e)
LANES = 128

AXES = ("x", "zh", "core", "zl", "y")
SIZES = (4, 4, 2, 2, 4)
ROW = ("x", "zh", "core")
COL = ("zl", "y")
RING = ("zh", "zl")
PLANE = ("x", "y")
SPREAD = ("x", "y", "core")
SWAP = [(0, 1), (1, 0)]

VMEM = pl.BlockSpec(memory_space=pltpu.VMEM)
SMEM = pl.BlockSpec(memory_space=pltpu.SMEM)
CONTRACT_LAST = (((1,), (1,)), ((), ()))


def dot(a, b, dims=(((1,), (0,)), ((), ()))):
    return lax.dot_general(a, b, dims, preferred_element_type=jnp.float32)


def call(kernel, outs, scratch, *operands, smem=0, flops=0, bytes_accessed=0):
    specs = [SMEM] * smem + [VMEM] * (len(operands) - smem)
    return pl.pallas_call(
        kernel,
        out_shape=outs,
        in_specs=specs,
        out_specs=jax.tree.map(lambda _: VMEM, outs),
        scratch_shapes=scratch,
        compiler_params=pltpu.CompilerParams(vmem_limit_bytes=30 * 2**20),
        cost_estimate=pl.CostEstimate(
            flops=flops, bytes_accessed=bytes_accessed, transcendentals=0
        ),
    )(*operands)


def shift(value, step):
    size = lax.axis_size(RING)
    return lax.ppermute(value, RING, [(i, (i + step) % size) for i in range(size)])


def ring_gather(value):
    size = lax.axis_size(RING)
    up = down = value
    found = {0: value}
    for step in range(1, size // 2):
        up, down = shift(up, 1), shift(down, -1)
        found[-step], found[step] = up, down
    half = value.shape[0] // 2
    far = (shift(up[:half], 1), shift(down[half:], -1))
    return [found[k] for k in range(1 - size // 2, size // 2)], far


def with_language(emb, lang):
    hot = lang[:, None] == lax.broadcasted_iota(jnp.int32, (1, LANES), 1)
    return jnp.concatenate([emb, hot.astype(emb.dtype)], axis=1)


def columns_lse(table, added):
    rows, width = table.shape
    tiles = width // LANES

    def block(c, t):
        at = pl.ds(pl.multiple_of(c * LANES, LANES), LANES)
        z = table[at, t * LANES : (t + 1) * LANES]
        if added is not None:
            z = z + added[at, :]
        return z.reshape(LANES // 8, 8, LANES)

    def find_top(c, tops):
        return tuple(
            jnp.maximum(top, jnp.max(block(c, t), axis=0)) for t, top in enumerate(tops)
        )

    tops = (jnp.full((8, LANES), 2 * NEG, jnp.float32),) * tiles
    tops = lax.fori_loop(0, rows // LANES, find_top, tops)
    tops = [jnp.max(top, axis=0, keepdims=True) for top in tops]

    def add_up(c, sums):
        return tuple(
            s + jnp.sum(jnp.exp2(block(c, t) - tops[t][None]), axis=0)
            for t, s in enumerate(sums)
        )

    sums = (jnp.zeros((8, LANES), jnp.float32),) * tiles
    sums = lax.fori_loop(0, rows // LANES, add_up, sums)
    return [
        top + jnp.log2(jnp.sum(s, axis=0, keepdims=True)) for top, s in zip(tops, sums)
    ]


def send_out(parts, offset, order, out):
    for t, part in enumerate(parts):
        order[pl.ds(lax.rem(t + offset, 8), 1), :] = part
    out[...] = jnp.broadcast_to(order[...][None], out.shape)


def merge(gathered, log_count, offset, order):
    parts = gathered[...]
    top = jnp.max(parts, axis=0)
    total = jnp.sum(jnp.exp2(parts - top[None]), axis=0)
    order[...] = log_count - (top + jnp.log2(total))
    return jnp.concatenate([order[pl.ds(lax.rem(t + offset, 8), 1), :] for t in range(8)])


def spread(pots, wide):
    columns = pots.T
    for c in range(8):
        wide[c * LANES : (c + 1) * LANES, :] = jnp.broadcast_to(
            columns[:, c : c + 1], (LANES, LANES)
        )


def first_kernel(scale, offsets, *refs):
    chunks, (far_up, far_down, mine, theirs) = refs[:7], refs[7:11]
    logits, logits_t, src_block, out, order = refs[11:]
    depth = src_block.shape[1]
    half = mine.shape[0]
    parts = []
    for unit in range(4):
        if unit < 3:
            src = jnp.concatenate([chunks[2 * unit][...], chunks[2 * unit + 1][...]])
        else:
            src = jnp.concatenate([chunks[6][...], far_up[...], far_down[...]])
        src, hot = src[:, :depth], src[:, depth:]
        at = slice(unit * 256, (unit + 1) * 256)
        src_block[at, :] = src
        for side, tgt in enumerate((mine, theirs)):
            to = slice(side * half, (side + 1) * half)
            emb, tgt_hot = tgt[:, :depth], tgt[:, depth:]
            same = dot(hot, tgt_hot, CONTRACT_LAST) > 0.5
            logits[at, to] = jnp.where(same, dot(src, emb, CONTRACT_LAST) * scale, NEG)
            same = dot(tgt_hot, hot, CONTRACT_LAST) > 0.5
            logits_t[to, at] = jnp.where(same, dot(emb, src, CONTRACT_LAST) * scale, NEG)
    parts = columns_lse(logits_t, None)
    send_out(parts, offsets[0], order, out)


def half_step_kernel(log_count, enter, leave, offsets, table, gathered, out, pots, order, wide):
    local = merge(gathered, log_count, offsets[enter], order)
    pots[...] = local
    spread(local, wide)
    send_out(columns_lse(table, wide), offsets[leave], order, out)


def src_kernel(log_count, share, offsets, logits, gathered, src_pots, mine, theirs, out, order, wide):
    depth = out.shape[1]
    half = mine.shape[0]
    tgt = merge(gathered, log_count, offsets[1], order)
    spread(src_pots[...], wide)
    for unit in range(4):
        at = slice(unit * 256, (unit + 1) * 256)
        weight = [
            jnp.exp2(logits[at, t * LANES : (t + 1) * LANES] + wide[at, :] + tgt[t : t + 1, :])
            .astype(jnp.bfloat16)
            for t in range(8)
        ]
        first = jnp.concatenate(weight[:4], axis=1)
        second = jnp.concatenate(weight[4:], axis=1)
        pull = dot(first, mine[:, :depth]) + dot(second, theirs[:, :depth])
        out[at, :] = pull * share


def tgt_kernel(
    log_count, share, offsets, logits_t, gathered, src_pots, src_block, keep, give, order, wide
):
    half = keep.shape[0]
    spread(merge(gathered, log_count, offsets[1], order), wide)
    src = src_pots[...]
    for unit in range(4):
        at = slice(unit * 256, (unit + 1) * 256)
        weight = [
            jnp.exp2(logits_t[at, t * LANES : (t + 1) * LANES] + wide[at, :] + src[t : t + 1, :])
            .astype(jnp.bfloat16)
            for t in range(8)
        ]
        pull = dot(jnp.concatenate(weight, axis=1), src_block[...]) * share
        to = slice((unit % 2) * 256, (unit % 2 + 1) * 256)
        if unit < 2:
            keep[to, :] = pull
        else:
            give[to, :] = pull.astype(give.dtype)


def shards(src_emb, tgt_emb, src_lang, tgt_lang):
    f32, bf16 = jnp.float32, jnp.bfloat16
    rows, depth = src_emb.shape
    columns = tgt_emb.shape[0]
    row, col = lax.axis_index(ROW), lax.axis_index(COL)
    ring, plane = lax.axis_size(RING), lax.axis_size(PLANE)
    spread_size = lax.axis_size(SPREAD)
    n_src, n_tgt = rows * ring, columns * spread_size
    place, core = lax.axis_index(RING), lax.axis_index("core")
    total_src = src_lang.shape[0] * lax.axis_size(ROW)
    total_tgt = tgt_lang.shape[0] * lax.axis_size(COL)
    offsets = jnp.stack([(place + ring // 2 + 1) % ring, 4 * core]).astype(jnp.int32)

    own_src_lang = lax.dynamic_slice(src_lang, (col * rows,), (rows,))
    own_tgt_lang = lax.dynamic_slice(tgt_lang, (row * columns,), (columns,))
    chunks, far = ring_gather(with_language(src_emb, own_src_lang))
    tgt = with_language(tgt_emb, own_tgt_lang)
    mine = lax.all_to_all(jnp.broadcast_to(tgt, (plane, *tgt.shape)), PLANE, 0, 0)
    theirs = lax.ppermute(mine, "core", SWAP)
    mine, theirs = (v.reshape(plane * columns, -1) for v in (mine, theirs))

    order = pltpu.VMEM((8, LANES), f32)
    table = jax.ShapeDtypeStruct((n_src, n_tgt), f32)
    table_t = jax.ShapeDtypeStruct((n_tgt, n_src), f32)
    pots = jax.ShapeDtypeStruct((8, LANES), f32)
    to_ring = jax.ShapeDtypeStruct((ring, 8, LANES), f32)
    to_spread = jax.ShapeDtypeStruct((spread_size, 8, LANES), f32)
    logits, logits_t, src_block, part = call(
        functools.partial(first_kernel, LOG2E / (EPSILON * math.sqrt(depth))),
        (table, table_t, jax.ShapeDtypeStruct((n_src, depth), bf16), to_ring),
        [order],
        offsets, *chunks, *far, mine, theirs,
        smem=1, flops=4 * n_src * n_tgt * depth, bytes_accessed=2**23,
    )
    wide_src = pltpu.VMEM((n_src, LANES), f32)
    wide_tgt = pltpu.VMEM((n_tgt, LANES), f32)
    for step in range(ITERS):
        gathered = lax.all_to_all(part, RING, 0, 0)
        part, src_pots = call(
            functools.partial(half_step_kernel, math.log2(total_tgt), 0, 1),
            (to_spread, pots), [order, wide_src],
            offsets, logits, gathered, smem=1, flops=8 * n_src * n_tgt, bytes_accessed=2**22,
        )
        gathered = lax.all_to_all(part, SPREAD, 0, 0)
        if step < ITERS - 1:
            part, _ = call(
                functools.partial(half_step_kernel, math.log2(total_src), 1, 0),
                (to_ring, pots), [order, wide_tgt],
                offsets, logits_t, gathered, smem=1, flops=8 * n_src * n_tgt, bytes_accessed=2**22,
            )
    src_terms = call(
        functools.partial(src_kernel, math.log2(total_src), 1.0 / total_tgt),
        jax.ShapeDtypeStruct((n_src, depth), f32),
        [order, wide_src],
        offsets, logits, gathered, src_pots, mine, theirs,
        smem=1, flops=2 * n_src * n_tgt * depth, bytes_accessed=2**23,
    )
    keep, give = call(
        functools.partial(tgt_kernel, math.log2(total_src), 1.0 / total_src),
        (jax.ShapeDtypeStruct((n_tgt // 2, depth), f32), jax.ShapeDtypeStruct((n_tgt // 2, depth), bf16)),
        [order, wide_tgt],
        offsets, logits_t, gathered, src_pots, src_block,
        smem=1, flops=2 * n_src * n_tgt * depth, bytes_accessed=2**23,
    )
    keep = keep + lax.ppermute(give, "core", SWAP).astype(f32)
    parts = lax.all_to_all(keep.astype(bf16).reshape(plane, columns, depth), PLANE, 0, 0)
    tgt_pull = jnp.sum(parts.astype(f32), axis=0)
    src_terms = src_terms.reshape(ring, rows, depth)
    base = ring // 2 - 1
    half = rows // 2
    far = src_terms[base + ring // 2].astype(bf16)
    pad = jnp.zeros((half, depth), f32)
    up = jnp.concatenate([shift(far[:half], 1).astype(f32), pad])
    down = jnp.concatenate([pad, shift(far[half:], -1).astype(f32)])
    for distance in range(ring // 2 - 1, 0, -1):
        up = shift((up + src_terms[base + distance]).astype(bf16), 1).astype(f32)
        down = shift((down + src_terms[base - distance]).astype(bf16), -1).astype(f32)
    src_pull = src_terms[base] + up + down
    row_cost = jnp.sum(src_pull * src_emb.astype(f32), axis=1) * (-1.0 / math.sqrt(depth))
    return (src_pull, tgt_pull, row_cost)


def solution(mesh):
    split = Mesh(mesh.devices.reshape(SIZES), AXES)
    return jax.shard_map(
        shards,
        mesh=split,
        in_specs=(P(ROW + COL, None), P(COL + ROW, None), P(ROW), P(COL)),
        out_specs=(P(ROW + COL, None), P(COL + ROW, None), P(ROW + COL)),
        check_vma=False,
    )
```

time: 225 us -> 210 us (0.933)
  other arithmetic: 34.8 us -> 7.73 us
  Pallas kernels: 0 us -> 26.2 us
  waiting for transfers between devices: 31.5 us -> 55.4 us
  blocking collectives: 85.9 us -> 67 us
  matrix products: 10.5 us -> 0 us
  local copies, waits for them, and re-layouts: 12.7 us -> 8.34 us
  starting transfers between devices: 47.1 us -> 43.2 us
    pallas_call x0 -> x8, Pallas kernels: none -> 26.2 us  [call(): pl.pallas_call(kernel, out_shape=outs, in_specs=specs, out_specs=jax.tree...]
    all_to_all x7 -> x6, blocking collectives: 85.9 us -> 67 us  [the longest x3 35.2 us: shards(): gathered = lax.all_to_all(part, SPREAD, 0, 0)]
    ppermute x16, waiting for transfers between devices: 23.6 us -> 37.5 us  [shift(): lax.ppermute(value, RING, [(i, (i + step) % size) for i in range(size)])]
    reduce_max x11 -> x0, other arithmetic: 13.6 us -> none  [log2sumexp2(): top = jnp.max(values, axis=axis)]
    dot_general x3 -> x0, matrix products: 10.5 us -> none  [the longest x1 5.43 us: shards(): lax.dot_general(weight_low, src_block, (((0,), (0,)), ((), ())), preferre...]
    all_to_all x4 -> x2, waiting for transfers between devices: 7.88 us -> 17.9 us  [the longest x1 15.6 us: shards(): lax.all_to_all(jnp.broadcast_to(tgt, (plane, *tgt.shape)), PLANE, 0, 0)]
    all_to_all x4 -> x2, starting transfers between devices: 21.5 us -> 12.5 us  [the longest x1 7.48 us: shards(): lax.all_to_all(jnp.broadcast_to(tgt, (plane, *tgt.shape)), PLANE, 0, 0)]
    reduce_sum x15 -> x2, other arithmetic: 8.47 us -> 2.8 us  [the longest x1 1.96 us: shards(): jnp.sum(src_pull * src_emb.astype(f32), axis=1) * (-1.0 / math.sqrt(depth))]
  transfers between devices with their start and end apart: 22 -> 20, of which waited for: 9 -> 10; matrix products, arithmetic and copies ran while one was open for 6% -> 4% of each run, Pallas kernels for 0% -> 1%
where the time goes in v2:
time: 210 us; the launch traced here: 209 us
  blocking collectives  67 us (32%)
  waiting for transfers between devices  55.4 us (26%)
  starting transfers between devices  43.2 us (21%)
  Pallas kernels  26.2 us (12%)
  local copies, waits for them, and re-layouts  8.34 us (4%)
  other arithmetic  7.73 us (4%)
    ppermute x16, waiting for transfers between devices, shift(): lax.ppermute(value, RING, [(i, (i + step) % size) for i in range(size)])  37.5 us
    all_to_all x3, blocking collectives, shards(): gathered = lax.all_to_all(part, SPREAD, 0, 0)  35.2 us
    all_to_all x3, blocking collectives, shards(): gathered = lax.all_to_all(part, RING, 0, 0)  31.7 us
    ppermute x16, starting transfers between devices, shift(): lax.ppermute(value, RING, [(i, (i + step) % size) for i in range(size)])  30.3 us
    pallas_call x8, Pallas kernels, call(): pl.pallas_call(kernel, out_shape=outs, in_specs=specs, out_specs=jax.tree...  26.2 us
    all_to_all x1, waiting for transfers between devices, shards(): lax.all_to_all(jnp.broadcast_to(tgt, (plane, *tgt.shape)), PLANE, 0, 0)  15.6 us
    all_to_all x1, starting transfers between devices, shards(): lax.all_to_all(jnp.broadcast_to(tgt, (plane, *tgt.shape)), PLANE, 0, 0)  7.48 us
    all_to_all x1, starting transfers between devices, shards(): lax.all_to_all(keep.astype(bf16).reshape(plane, columns, depth), PLANE, 0...  5.05 us
  transfers between devices with their start and end apart: 20, of which 10 were waited for; matrix products, arithmetic and copies ran while one was open for 4% of the time, Pallas kernels for 1%

profile of v2, /device:TPU:2, one launch (start us, length us, event | category | flops | bytes accessed | tf_op | source)
XLA Modules:
  0.0 208.6 jit_solution(12054527634790835674)
XLA Ops:
  3.5 7.5 %all-to-all-start = ((bf16[16,32,1152]{2,1,0:T(8,128)(2,1)}), bf16[16,32,1152]{2,1,0:T(8,128)(2,1)S(1)}, u32[]{:S(2)}, u32[]{:S(2)}) async-start(bf16[16,32,1152]{2,1,0:T(8,128)(2,1)} %broadcast_in_dim.2), calls=%async_computation | async-start | bytes 2359296 | tf_op jit(solution)/shard_map/all_to_all | solution.py:215
  11.8 15.6 %all-to-all-done = bf16[16,32,1152]{2,1,0:T(8,128)(2,1)S(1)} async-done(((bf16[16,32,1152]{2,1,0:T(8,128)(2,1)}), bf16[16,32,1152]{2,1,0:T(8,128)(2,1)S(1)}, u32[]{:S(2)}, u32[]{:S(2)}) %all-to-all-start) | async-done | bytes 1179680 | tf_op jit(solution)/shard_map/all_to_all | solution.py:215
  27.5 5.9 %collective-permute-start.3 = (bf16[128,1152]{1,0:T(8,128)(2,1)S(1)}, bf16[128,1152]{1,0:T(8,128)(2,1)S(1)}, u32[]{:S(2)}, u32[]{:S(2)}) collective-permute-start(bf16[128,1152]{1,0:T(8,128)(2,1)S(1)} %pad_maximum_fusion.refs_3_), channel_id=1, source_target_pairs={{0,52},{4,0},{16,4},{20,16},{32,20},{36,32},{48,36},{52,48},{1,53}... | collective-permute-start | bytes 884744 | tf_op jit(solution)/shard_map/ppermute | solution.py:52
  33.4 6.9 %collective-permute-done.3.refs_4_ = bf16[128,1152]{1,0:T(8,128)(2,1)S(1)} collective-permute-done((bf16[128,1152]{1,0:T(8,128)(2,1)S(1)}, bf16[128,1152]{1,0:T(8,128)(2,1)S(1)}, u32[]{:S(2)}, u32[]{:S(2)}) %collective-permute-start.3) | collective-permute-done | bytes 294944 | tf_op jit(solution)/shard_map/ppermute | solution.py:52
  40.4 3.7 %collective-permute-start.4 = (bf16[128,1152]{1,0:T(8,128)(2,1)S(1)}, bf16[128,1152]{1,0:T(8,128)(2,1)S(1)}, u32[]{:S(2)}, u32[]{:S(2)}) collective-permute-start(bf16[128,1152]{1,0:T(8,128)(2,1)S(1)} %collective-permute-done.3.refs_4_), channel_id=1, source_target_pairs={{0,52},{4,0},{16,4},{20,16},{32,20},{36,32},{48,36},{52,48},{1,53}... | collective-permute-start | bytes 884744 | tf_op jit(solution)/shard_map/ppermute | solution.py:52
  44.8 5.4 %collective-permute-done.4.refs_5_ = bf16[128,1152]{1,0:T(8,128)(2,1)S(1)} collective-permute-done((bf16[128,1152]{1,0:T(8,128)(2,1)S(1)}, bf16[128,1152]{1,0:T(8,128)(2,1)S(1)}, u32[]{:S(2)}, u32[]{:S(2)}) %collective-permute-start.4) | collective-permute-done | bytes 294944 | tf_op jit(solution)/shard_map/ppermute | solution.py:52
  50.2 3.7 %collective-permute-start.5 = (bf16[128,1152]{1,0:T(8,128)(2,1)S(1)}, bf16[128,1152]{1,0:T(8,128)(2,1)S(1)}, u32[]{:S(2)}, u32[]{:S(2)}) collective-permute-start(bf16[128,1152]{1,0:T(8,128)(2,1)S(1)} %collective-permute-done.4.refs_5_), channel_id=1, source_target_pairs={{0,52},{4,0},{16,4},{20,16},{32,20},{36,32},{48,36},{52,48},{1,53}... | collective-permute-start | bytes 884744 | tf_op jit(solution)/shard_map/ppermute | solution.py:52
  54.6 4.6 %collective-permute-done.5.refs_6_ = bf16[128,1152]{1,0:T(8,128)(2,1)S(1)} collective-permute-done((bf16[128,1152]{1,0:T(8,128)(2,1)S(1)}, bf16[128,1152]{1,0:T(8,128)(2,1)S(1)}, u32[]{:S(2)}, u32[]{:S(2)}) %collective-permute-start.5) | collective-permute-done | bytes 294944 | tf_op jit(solution)/shard_map/ppermute | solution.py:52
  59.8 3.7 %collective-permute-start.7 = (bf16[64,1152]{1,0:T(8,128)(2,1)}, bf16[64,1152]{1,0:T(8,128)(2,1)}, u32[]{:S(2)}, u32[]{:S(2)}) collective-permute-start(bf16[64,1152]{1,0:T(8,128)(2,1)} %slice.57), channel_id=1, source_target_pairs={{0,52},{4,0},{16,4},{20,16},{32,20},{36,32},{48,36},{52,48},{1,53}... | collective-permute-start | bytes 442376 | tf_op jit(solution)/shard_map/ppermute | solution.py:52
  66.5 4.4 %collective-permute-done.6.refs_7_ = bf16[64,1152]{1,0:T(8,128)(2,1)} collective-permute-done((bf16[64,1152]{1,0:T(8,128)(2,1)}, bf16[64,1152]{1,0:T(8,128)(2,1)}, u32[]{:S(2)}, u32[]{:S(2)}) %collective-permute-start.6) | collective-permute-done | bytes 147488 | tf_op jit(solution)/shard_map/ppermute | solution.py:52
  73.8 7.7 %shard_map.67 = (f32[1024,1024]{1,0:T(8,128)S(1)}, f32[1024,1024]{1,0:T(8,128)S(1)}, bf16[1024,1024]{1,0:T(8,128)(2,1)S(1)}, f32[8,8,128]{2,1,0:T(8,128)S(1)}) custom-call(s32[2]{0:T(128)S(1)} %pad_add_fusion.offsets, bf16[128,1152]{1,0:T(8,128)(2,1)S(1)} %collective-permute-done.2.refs_0_, bf16[128,1152]{1,0:T(8,128)(2,1)S(1)} %copy-done.6, ...), custom_call_target="tpu_custom_call" | custom-call | flops 4294967296 | bytes 8388608 | tf_op jit(solution)/shard_map/pallas_call | solution.py:37
  81.5 10.9 %all_to_all.40.gathered = f32[8,8,128]{2,1,0:T(8,128)S(1)} all-to-all(f32[8,8,128]{2,1,0:T(8,128)S(1)} %get-tuple-element.17), channel_id=1, replica_groups=mesh['x'=4,'zh'=4,'core'=2,'zl'=2,'y'=4] {'zh','zl'}, dimensions={0} | all-to-all | bytes 65536 | tf_op jit(solution)/shard_map/all_to_all | solution.py:235
  95.0 12.7 %all_to_all.41.gathered = f32[32,8,128]{2,1,0:T(8,128)S(1)} all-to-all(f32[32,8,128]{2,1,0:T(8,128)S(1)} %get-tuple-element.18), channel_id=1, replica_groups=mesh['x'=4,'zh'=4,'core'=2,'zl'=2,'y'=4] {'x','y','core'}, dimensions={0} | all-to-all | bytes 262144 | tf_op jit(solution)/shard_map/all_to_all | solution.py:241
  110.2 10.4 %all_to_all.42.gathered = f32[8,8,128]{2,1,0:T(8,128)S(1)} all-to-all(f32[8,8,128]{2,1,0:T(8,128)S(1)} %get-tuple-element.19), channel_id=1, replica_groups=mesh['x'=4,'zh'=4,'core'=2,'zl'=2,'y'=4] {'zh','zl'}, dimensions={0} | all-to-all | bytes 65536 | tf_op jit(solution)/shard_map/all_to_all | solution.py:235
  123.1 11.3 %all_to_all.43.gathered = f32[32,8,128]{2,1,0:T(8,128)S(1)} all-to-all(f32[32,8,128]{2,1,0:T(8,128)S(1)} %get-tuple-element.20), channel_id=1, replica_groups=mesh['x'=4,'zh'=4,'core'=2,'zl'=2,'y'=4] {'x','y','core'}, dimensions={0} | all-to-all | bytes 262144 | tf_op jit(solution)/shard_map/all_to_all | solution.py:241
  136.9 10.4 %all_to_all.44.gathered = f32[8,8,128]{2,1,0:T(8,128)S(1)} all-to-all(f32[8,8,128]{2,1,0:T(8,128)S(1)} %get-tuple-element.21), channel_id=1, replica_groups=mesh['x'=4,'zh'=4,'core'=2,'zl'=2,'y'=4] {'zh','zl'}, dimensions={0} | all-to-all | bytes 65536 | tf_op jit(solution)/shard_map/all_to_all | solution.py:235
  149.3 11.3 %all_to_all.45.gathered = f32[32,8,128]{2,1,0:T(8,128)S(1)} all-to-all(f32[32,8,128]{2,1,0:T(8,128)S(1)} %get-tuple-element.22), channel_id=1, replica_groups=mesh['x'=4,'zh'=4,'core'=2,'zl'=2,'y'=4] {'x','y','core'}, dimensions={0} | all-to-all | bytes 262144 | tf_op jit(solution)/shard_map/all_to_all | solution.py:241
  171.0 3.8 %collective-permute-done.9 = bf16[64,1024]{1,0:T(8,128)(2,1)S(1)} collective-permute-done((bf16[64,1024]{1,0:T(8,128)(2,1)S(1)}, bf16[64,1024]{1,0:T(8,128)(2,1)S(1)}, u32[]{:S(2)}, u32[]{:S(2)}) %collective-permute-start.9) | collective-permute-done | bytes 131104 | tf_op jit(solution)/shard_map/ppermute | solution.py:52
  175.0 3.2 %collective-permute-start.14 = (bf16[128,1024]{1,0:T(8,128)(2,1)S(1)}, bf16[128,1024]{1,0:T(8,128)(2,1)S(1)}, u32[]{:S(2)}, u32[]{:S(2)}) collective-permute-start(bf16[128,1024]{1,0:T(8,128)(2,1)S(1)} %get-tuple-element.34), channel_id=1, source_target_pairs={{0,52},{4,0},{16,4},{20,16},{32,20},{36,32},{48,36},{52,48},{1,53}... | collective-permute-start | bytes 786440 | tf_op jit(solution)/shard_map/ppermute | solution.py:52
  178.3 5.8 %collective-permute-done.10 = bf16[128,1024]{1,0:T(8,128)(2,1)S(1)} collective-permute-done((bf16[128,1024]{1,0:T(8,128)(2,1)S(1)}, bf16[128,1024]{1,0:T(8,128)(2,1)S(1)}, u32[]{:S(2)}, u32[]{:S(2)}) %collective-permute-start.10) | collective-permute-done | bytes 262176 | tf_op jit(solution)/shard_map/ppermute | solution.py:52
  184.3 3.2 %collective-permute-start.15 = (bf16[128,1024]{1,0:T(8,128)(2,1)S(1)}, bf16[128,1024]{1,0:T(8,128)(2,1)S(1)}, u32[]{:S(2)}, u32[]{:S(2)}) collective-permute-start(bf16[128,1024]{1,0:T(8,128)(2,1)S(1)} %get-tuple-element.32), channel_id=1, source_target_pairs={{0,52},{4,0},{16,4},{20,16},{32,20},{36,32},{48,36},{52,48},{1,53}... | collective-permute-start | bytes 786440 | tf_op jit(solution)/shard_map/ppermute | solution.py:52
  189.0 5.0 %all-to-all-start.7 = ((bf16[16,32,1024]{2,1,0:T(8,128)(2,1)}), bf16[16,32,1024]{2,1,0:T(8,128)(2,1)S(1)}, u32[]{:S(2)}, u32[]{:S(2)}) async-start(bf16[16,32,1024]{2,1,0:T(8,128)(2,1)} %bitcast.4), calls=%async_computation.7 | async-start | bytes 2097152 | tf_op jit(solution)/shard_map/all_to_all | solution.py:263
  195.5 3.2 %collective-permute-start.16 = (bf16[128,1024]{1,0:T(8,128)(2,1)S(1)}, bf16[128,1024]{1,0:T(8,128)(2,1)S(1)}, u32[]{:S(2)}, u32[]{:S(2)}) collective-permute-start(bf16[128,1024]{1,0:T(8,128)(2,1)S(1)} %get-tuple-element.30), channel_id=1, source_target_pairs={{0,52},{4,0},{16,4},{20,16},{32,20},{36,32},{48,36},{52,48},{1,53}... | collective-permute-start | bytes 786440 | tf_op jit(solution)/shard_map/ppermute | solution.py:52
  198.7 4.3 %collective-permute-done.12 = bf16[128,1024]{1,0:T(8,128)(2,1)S(1)} collective-permute-done((bf16[128,1024]{1,0:T(8,128)(2,1)S(1)}, bf16[128,1024]{1,0:T(8,128)(2,1)S(1)}, u32[]{:S(2)}, u32[]{:S(2)}) %collective-permute-start.12) | collective-permute-done | bytes 262176 | tf_op jit(solution)/shard_map/ppermute | solution.py:52
  (67 shorter events, 43.0 us)
Async XLA Ops:
  0.6 26.8 %copy-start.7 = (bf16[128,1024]{1,0:T(8,128)(2,1)S(1)}, bf16[128,1024]{1,0:T(8,128)(2,1)}, u32[]{:S(2)}) copy-start(bf16[128,1024]{1,0:T(8,128)(2,1)} %param.4) | copy-start | bytes 786436
  3.5 24.0 %all-to-all-start = ((bf16[16,32,1152]{2,1,0:T(8,128)(2,1)}), bf16[16,32,1152]{2,1,0:T(8,128)(2,1)S(1)}, u32[]{:S(2)}, u32[]{:S(2)}) async-start(bf16[16,32,1152]{2,1,0:T(8,128)(2,1)} %broadcast_in_dim.2), calls=%async_computation | async-start | bytes 2359296 | tf_op jit(solution)/shard_map/all_to_all | solution.py:215
  27.5 43.4 %collective-permute-start.8 = (bf16[16,32,1152]{2,1,0:T(8,128)(2,1)S(1)}, bf16[16,32,1152]{2,1,0:T(8,128)(2,1)S(1)}, u32[]{:S(2)}, u32[]{:S(2)}) collective-permute-start(bf16[16,32,1152]{2,1,0:T(8,128)(2,1)S(1)} %all-to-all-done), channel_id=1, source_target_pairs={{0,8},{8,0},{1,9},{9,1},{2,10},{10,2},{3,11},{11,3},{4,12},{12,4},... | collective-permute-start | bytes 3538952 | tf_op jit(solution)/shard_map/ppermute | solution.py:216
  27.5 12.9 %collective-permute-start.3 = (bf16[128,1152]{1,0:T(8,128)(2,1)S(1)}, bf16[128,1152]{1,0:T(8,128)(2,1)S(1)}, u32[]{:S(2)}, u32[]{:S(2)}) collective-permute-start(bf16[128,1152]{1,0:T(8,128)(2,1)S(1)} %pad_maximum_fusion.refs_3_), channel_id=1, source_target_pairs={{0,52},{4,0},{16,4},{20,16},{32,20},{36,32},{48,36},{52,48},{1,53}... | collective-permute-start | bytes 884744 | tf_op jit(solution)/shard_map/ppermute | solution.py:52
  33.4 10.6 %collective-permute-start = (bf16[128,1152]{1,0:T(8,128)(2,1)S(1)}, bf16[128,1152]{1,0:T(8,128)(2,1)S(1)}, u32[]{:S(2)}, u32[]{:S(2)}) collective-permute-start(bf16[128,1152]{1,0:T(8,128)(2,1)S(1)} %pad_maximum_fusion.refs_3_), channel_id=1, source_target_pairs={{0,4},{4,16},{16,20},{20,32},{32,36},{36,48},{48,52},{52,0},{1,5},... | collective-permute-start | bytes 884744 | tf_op jit(solution)/shard_map/ppermute | solution.py:52
  40.4 9.8 %collective-permute-start.4 = (bf16[128,1152]{1,0:T(8,128)(2,1)S(1)}, bf16[128,1152]{1,0:T(8,128)(2,1)S(1)}, u32[]{:S(2)}, u32[]{:S(2)}) collective-permute-start(bf16[128,1152]{1,0:T(8,128)(2,1)S(1)} %collective-permute-done.3.refs_4_), channel_id=1, source_target_pairs={{0,52},{4,0},{16,4},{20,16},{32,20},{36,32},{48,36},{52,48},{1,53}... | collective-permute-start | bytes 884744 | tf_op jit(solution)/shard_map/ppermute | solution.py:52
  44.1 10.6 %collective-permute-start.1 = (bf16[128,1152]{1,0:T(8,128)(2,1)S(1)}, bf16[128,1152]{1,0:T(8,128)(2,1)S(1)}, u32[]{:S(2)}, u32[]{:S(2)}) collective-permute-start(bf16[128,1152]{1,0:T(8,128)(2,1)S(1)} %collective-permute-done.refs_2_), channel_id=1, source_target_pairs={{0,4},{4,16},{16,20},{20,32},{32,36},{36,48},{48,52},{52,0},{1,5},... | collective-permute-start | bytes 884744 | tf_op jit(solution)/shard_map/ppermute | solution.py:52
  50.2 9.0 %collective-permute-start.5 = (bf16[128,1152]{1,0:T(8,128)(2,1)S(1)}, bf16[128,1152]{1,0:T(8,128)(2,1)S(1)}, u32[]{:S(2)}, u32[]{:S(2)}) collective-permute-start(bf16[128,1152]{1,0:T(8,128)(2,1)S(1)} %collective-permute-done.4.refs_5_), channel_id=1, source_target_pairs={{0,52},{4,0},{16,4},{20,16},{32,20},{36,32},{48,36},{52,48},{1,53}... | collective-permute-start | bytes 884744 | tf_op jit(solution)/shard_map/ppermute | solution.py:52
  54.6 8.9 %copy-start.5 = (bf16[128,1152]{1,0:T(8,128)(2,1)}, bf16[128,1152]{1,0:T(8,128)(2,1)S(1)}, u32[]{:S(2)}) copy-start(bf16[128,1152]{1,0:T(8,128)(2,1)S(1)} %collective-permute-done.1.refs_1_) | copy-start | bytes 884740
  54.6 8.9 %collective-permute-start.2 = (bf16[128,1152]{1,0:T(8,128)(2,1)S(1)}, bf16[128,1152]{1,0:T(8,128)(2,1)S(1)}, u32[]{:S(2)}, u32[]{:S(2)}) collective-permute-start(bf16[128,1152]{1,0:T(8,128)(2,1)S(1)} %collective-permute-done.1.refs_1_), channel_id=1, source_target_pairs={{0,4},{4,16},{16,20},{20,32},{32,36},{36,48},{48,52},{52,0},{1,5},... | collective-permute-start | bytes 884744 | tf_op jit(solution)/shard_map/ppermute | solution.py:52
  59.8 6.7 %collective-permute-start.7 = (bf16[64,1152]{1,0:T(8,128)(2,1)}, bf16[64,1152]{1,0:T(8,128)(2,1)}, u32[]{:S(2)}, u32[]{:S(2)}) collective-permute-start(bf16[64,1152]{1,0:T(8,128)(2,1)} %slice.57), channel_id=1, source_target_pairs={{0,52},{4,0},{16,4},{20,16},{32,20},{36,32},{48,36},{52,48},{1,53}... | collective-permute-start | bytes 442376 | tf_op jit(solution)/shard_map/ppermute | solution.py:52
  64.2 6.7 %collective-permute-start.6 = (bf16[64,1152]{1,0:T(8,128)(2,1)}, bf16[64,1152]{1,0:T(8,128)(2,1)}, u32[]{:S(2)}, u32[]{:S(2)}) collective-permute-start(bf16[64,1152]{1,0:T(8,128)(2,1)} %slice.56), channel_id=1, source_target_pairs={{0,4},{4,16},{16,20},{20,32},{32,36},{36,48},{48,52},{52,0},{1,5},... | collective-permute-start | bytes 442376 | tf_op jit(solution)/shard_map/ppermute | solution.py:52
  163.8 23.7 %collective-permute-start.17 = (bf16[512,1024]{1,0:T(8,128)(2,1)S(1)}, bf16[512,1024]{1,0:T(8,128)(2,1)S(1)}, u32[]{:S(2)}, u32[]{:S(2)}) collective-permute-start(bf16[512,1024]{1,0:T(8,128)(2,1)S(1)} %get-tuple-element.26), channel_id=1, source_target_pairs={{0,8},{8,0},{1,9},{9,1},{2,10},{10,2},{3,11},{11,3},{4,12},{12,4},... | collective-permute-start | bytes 3145736 | tf_op jit(solution)/shard_map/ppermute | solution.py:262
  167.3 16.7 %copy-start = (f32[1024,1024]{1,0:T(8,128)}, f32[1024,1024]{1,0:T(8,128)S(1)}, u32[]{:S(2)}) copy-start(f32[1024,1024]{1,0:T(8,128)S(1)} %shard_map.73) | copy-start | bytes 12582916
  167.7 7.1 %collective-permute-start.9 = (bf16[64,1024]{1,0:T(8,128)(2,1)S(1)}, bf16[64,1024]{1,0:T(8,128)(2,1)S(1)}, u32[]{:S(2)}, u32[]{:S(2)}) collective-permute-start(bf16[64,1024]{1,0:T(8,128)(2,1)S(1)} %get-tuple-element.35), channel_id=1, source_target_pairs={{0,4},{4,16},{16,20},{20,32},{32,36},{36,48},{48,52},{52,0},{1,5},... | collective-permute-start | bytes 393224 | tf_op jit(solution)/shard_map/ppermute | solution.py:52
  168.4 6.4 %collective-permute-start.13 = (bf16[64,1024]{1,0:T(8,128)(2,1)S(1)}, bf16[64,1024]{1,0:T(8,128)(2,1)S(1)}, u32[]{:S(2)}, u32[]{:S(2)}) collective-permute-start(bf16[64,1024]{1,0:T(8,128)(2,1)S(1)} %get-tuple-element.36), channel_id=1, source_target_pairs={{0,52},{4,0},{16,4},{20,16},{32,20},{36,32},{48,36},{52,48},{1,53}... | collective-permute-start | bytes 393224 | tf_op jit(solution)/shard_map/ppermute | solution.py:52
  174.9 9.1 %collective-permute-start.10 = (bf16[128,1024]{1,0:T(8,128)(2,1)S(1)}, bf16[128,1024]{1,0:T(8,128)(2,1)S(1)}, u32[]{:S(2)}, u32[]{:S(2)}) collective-permute-start(bf16[128,1024]{1,0:T(8,128)(2,1)S(1)} %get-tuple-element.33), channel_id=1, source_target_pairs={{0,4},{4,16},{16,20},{20,32},{32,36},{36,48},{48,52},{52,0},{1,5},... | collective-permute-start | bytes 786440 | tf_op jit(solution)/shard_map/ppermute | solution.py:52
  175.0 9.0 %collective-permute-start.14 = (bf16[128,1024]{1,0:T(8,128)(2,1)S(1)}, bf16[128,1024]{1,0:T(8,128)(2,1)S(1)}, u32[]{:S(2)}, u32[]{:S(2)}) collective-permute-start(bf16[128,1024]{1,0:T(8,128)(2,1)S(1)} %get-tuple-element.34), channel_id=1, source_target_pairs={{0,52},{4,0},{16,4},{20,16},{32,20},{36,32},{48,36},{52,48},{1,53}... | collective-permute-start | bytes 786440 | tf_op jit(solution)/shard_map/ppermute | solution.py:52
  184.2 9.8 %collective-permute-start.11 = (bf16[128,1024]{1,0:T(8,128)(2,1)S(1)}, bf16[128,1024]{1,0:T(8,128)(2,1)S(1)}, u32[]{:S(2)}, u32[]{:S(2)}) collective-permute-start(bf16[128,1024]{1,0:T(8,128)(2,1)S(1)} %get-tuple-element.31), channel_id=1, source_target_pairs={{0,4},{4,16},{16,20},{20,32},{32,36},{36,48},{48,52},{52,0},{1,5},... | collective-permute-start | bytes 786440 | tf_op jit(solution)/shard_map/ppermute | solution.py:52
  184.3 9.7 %collective-permute-start.15 = (bf16[128,1024]{1,0:T(8,128)(2,1)S(1)}, bf16[128,1024]{1,0:T(8,128)(2,1)S(1)}, u32[]{:S(2)}, u32[]{:S(2)}) collective-permute-start(bf16[128,1024]{1,0:T(8,128)(2,1)S(1)} %get-tuple-element.32), channel_id=1, source_target_pairs={{0,52},{4,0},{16,4},{20,16},{32,20},{36,32},{48,36},{52,48},{1,53}... | collective-permute-start | bytes 786440 | tf_op jit(solution)/shard_map/ppermute | solution.py:52
  189.0 14.1 %copy-start.8 = (bf16[128,1024]{1,0:T(8,128)(2,1)S(1)}, bf16[128,1024]{1,0:T(8,128)(2,1)}, u32[]{:S(2)}) copy-start(bf16[128,1024]{1,0:T(8,128)(2,1)} %param.4) | copy-start | bytes 786436
  189.0 18.8 %all-to-all-start.7 = ((bf16[16,32,1024]{2,1,0:T(8,128)(2,1)}), bf16[16,32,1024]{2,1,0:T(8,128)(2,1)S(1)}, u32[]{:S(2)}, u32[]{:S(2)}) async-start(bf16[16,32,1024]{2,1,0:T(8,128)(2,1)} %bitcast.4), calls=%async_computation.7 | async-start | bytes 2097152 | tf_op jit(solution)/shard_map/all_to_all | solution.py:263
  195.4 7.7 %collective-permute-start.12 = (bf16[128,1024]{1,0:T(8,128)(2,1)S(1)}, bf16[128,1024]{1,0:T(8,128)(2,1)S(1)}, u32[]{:S(2)}, u32[]{:S(2)}) collective-permute-start(bf16[128,1024]{1,0:T(8,128)(2,1)S(1)} %get-tuple-element.29), channel_id=1, source_target_pairs={{0,4},{4,16},{16,20},{20,32},{32,36},{36,48},{48,52},{52,0},{1,5},... | collective-permute-start | bytes 786440 | tf_op jit(solution)/shard_map/ppermute | solution.py:52
  195.5 7.6 %collective-permute-start.16 = (bf16[128,1024]{1,0:T(8,128)(2,1)S(1)}, bf16[128,1024]{1,0:T(8,128)(2,1)S(1)}, u32[]{:S(2)}, u32[]{:S(2)}) collective-permute-start(bf16[128,1024]{1,0:T(8,128)(2,1)S(1)} %get-tuple-element.30), channel_id=1, source_target_pairs={{0,52},{4,0},{16,4},{20,16},{32,20},{36,32},{48,36},{52,48},{1,53}... | collective-permute-start | bytes 786440 | tf_op jit(solution)/shard_map/ppermute | solution.py:52
  (5 other events, 4.3 us)

commit v3 on v2

v3 whole, which is shorter than its diff:
```python
import functools
import math

import jax
import jax.numpy as jnp
from jax import lax
from jax.experimental import pallas as pl
from jax.experimental.pallas import tpu as pltpu
from jax.sharding import Mesh, PartitionSpec as P

ITERS = 3
NEG = -1e30
EPSILON = 0.5
LOG2E = math.log2(math.e)
LANES = 128
DISTANCES = (1, 7, 2, 6, 3, 5, 0, 4)

AXES = ("x", "zh", "core", "zl", "y")
SIZES = (4, 4, 2, 2, 4)
ROW = ("x", "zh", "core")
COL = ("zl", "y")
RING = ("zh", "zl")
PLANE = ("x", "y")
SPREAD = ("x", "y", "core")
SWAP = [(0, 1), (1, 0)]

VMEM = pl.BlockSpec(memory_space=pltpu.VMEM)
SMEM = pl.BlockSpec(memory_space=pltpu.SMEM)
CONTRACT_LAST = (((1,), (1,)), ((), ()))


def dot(a, b, dims=(((1,), (0,)), ((), ()))):
    return lax.dot_general(a, b, dims, preferred_element_type=jnp.float32)


def call(kernel, outs, scratch, *operands, smem=0, flops=0, bytes_accessed=0):
    specs = [SMEM] * smem + [VMEM] * (len(operands) - smem)
    return pl.pallas_call(
        kernel,
        out_shape=outs,
        in_specs=specs,
        out_specs=jax.tree.map(lambda _: VMEM, outs),
        scratch_shapes=scratch,
        compiler_params=pltpu.CompilerParams(vmem_limit_bytes=30 * 2**20),
        cost_estimate=pl.CostEstimate(
            flops=flops, bytes_accessed=bytes_accessed, transcendentals=0
        ),
    )(*operands)


def shift(value, step):
    size = lax.axis_size(RING)
    return lax.ppermute(value, RING, [(i, (i + step) % size) for i in range(size)])


def with_language(emb, lang):
    hot = lang[:, None] == lax.broadcasted_iota(jnp.int32, (1, LANES), 1)
    return jnp.concatenate([emb, hot.astype(emb.dtype)], axis=1)


def columns_lse(tables, added):
    tiles = tables[0].shape[1] // LANES

    def blocks(t):
        start = 0
        for table in tables:
            for c in range(table.shape[0] // LANES):
                z = table[c * LANES : (c + 1) * LANES, t * LANES : (t + 1) * LANES]
                if added is not None:
                    z = z + added[start : start + LANES, :]
                start += LANES
                yield z.reshape(LANES // 8, 8, LANES)

    results = []
    for t in range(tiles):
        top = functools.reduce(jnp.maximum, (jnp.max(z, axis=0) for z in blocks(t)))
        top = jnp.max(top, axis=0, keepdims=True)
        total = functools.reduce(
            jnp.add, (jnp.sum(jnp.exp2(z - top[None]), axis=0) for z in blocks(t))
        )
        results.append(top + jnp.log2(jnp.sum(total, axis=0, keepdims=True)))
    return results


def send_out(parts, offset, table, order, out):
    for part, at in zip(parts, table):
        order[pl.ds(lax.rem(at + offset, 8), 1), :] = part
    out[...] = jnp.broadcast_to(order[...][None], out.shape)


def merge(gathered, log_count, offset, table, order):
    parts = gathered[...]
    top = jnp.max(parts, axis=0)
    total = jnp.sum(jnp.exp2(parts - top[None]), axis=0)
    order[...] = log_count - (top + jnp.log2(total))
    return jnp.concatenate([order[pl.ds(lax.rem(at + offset, 8), 1), :] for at in table])


def spread(pots, wide):
    columns = pots.T
    for c in range(8):
        wide[c * LANES : (c + 1) * LANES, :] = jnp.broadcast_to(
            columns[:, c : c + 1], (LANES, LANES)
        )


def make_logits(scale, src, mine, theirs, logits, logits_t, src_block):
    depth = src_block.shape[1]
    half = mine.shape[0]
    src, hot = src[:, :depth], src[:, depth:]
    src_block[...] = src
    for side, tgt in enumerate((mine, theirs)):
        to = slice(side * half, (side + 1) * half)
        emb, tgt_hot = tgt[:, :depth], tgt[:, depth:]
        same = dot(hot, tgt_hot, CONTRACT_LAST) > 0.5
        logits[:, to] = jnp.where(same, dot(src, emb, CONTRACT_LAST) * scale, NEG)
        same = dot(tgt_hot, hot, CONTRACT_LAST) > 0.5
        logits_t[to, :] = jnp.where(same, dot(emb, src, CONTRACT_LAST) * scale, NEG)


def pair_kernel(scale, near, other, mine, theirs, logits, logits_t, src_block, part):
    src = jnp.concatenate([near[...], other[...]])
    make_logits(scale, src, mine, theirs, logits, logits_t, src_block)
    part[...] = jnp.concatenate(columns_lse([logits_t], None))


def last_pair_kernel(
    scale, offsets, own, far_up, far_down, mine, theirs, *refs
):
    parts, (logits, logits_t, src_block, out, order) = refs[:3], refs[3:]
    src = jnp.concatenate([own[...], far_up[...], far_down[...]])
    make_logits(scale, src, mine, theirs, logits, logits_t, src_block)
    parts = [part[r : r + 1, :] for part in parts for r in range(2)]
    send_out(parts + columns_lse([logits_t], None), offsets[0], DISTANCES, order, out)


def src_pots_kernel(log_count, offsets, *refs):
    tables, (gathered, out, pots, order, wide) = refs[:4], refs[4:]
    local = merge(gathered, log_count, offsets[0], DISTANCES, order)
    pots[...] = local
    spread(local, wide)
    send_out(columns_lse(tables, wide), offsets[1], range(8), order, out)


def tgt_pots_kernel(log_count, offsets, *refs):
    tables, (gathered, out, order, wide) = refs[:4], refs[4:]
    spread(merge(gathered, log_count, offsets[1], range(8), order), wide)
    parts = [part for table in tables for part in columns_lse([table], wide)]
    send_out(parts, offsets[0], DISTANCES, order, out)


def src_kernel(log_count, share, units, offsets, *refs):
    n = len(units)
    tables, (gathered, src_pots, mine, theirs), outs = refs[:n], refs[n : n + 4], refs[n + 4 : -2]
    order, wide = refs[-2:]
    depth = outs[0].shape[1]
    tgt = merge(gathered, log_count, offsets[1], range(8), order)
    spread(src_pots[...], wide)
    for k, (unit, table) in enumerate(zip(units, tables)):
        at = slice(unit * 256, (unit + 1) * 256)
        weight = [
            jnp.exp2(table[:, t * LANES : (t + 1) * LANES] + wide[at, :] + tgt[t : t + 1, :])
            .astype(jnp.bfloat16)
            for t in range(8)
        ]
        first = jnp.concatenate(weight[:4], axis=1)
        second = jnp.concatenate(weight[4:], axis=1)
        pull = (dot(first, mine[:, :depth]) + dot(second, theirs[:, :depth])) * share
        for out, value in zip(outs[2 * k : 2 * k + 2], (pull[:LANES], pull[LANES:])):
            out[...] = value.astype(out.dtype)


def tgt_kernel(log_count, share, offsets, *refs):
    tables, (gathered, src_pots), blocks = refs[:4], refs[4:6], refs[6:10]
    keep, give, order, wide = refs[10:]
    spread(merge(gathered, log_count, offsets[1], range(8), order), wide)
    src = src_pots[...]
    for unit in (2, 3, 0, 1):
        at = slice(unit * 256, (unit + 1) * 256)
        pull = 0.0
        for k, (table, block) in enumerate(zip(tables, blocks)):
            weight = [
                jnp.exp2(table[at, t * LANES : (t + 1) * LANES] + wide[at, :] + src[2 * k + t : 2 * k + t + 1, :])
                .astype(jnp.bfloat16)
                for t in range(2)
            ]
            pull = pull + dot(jnp.concatenate(weight, axis=1), block[...])
        to = slice((unit % 2) * 256, (unit % 2 + 1) * 256)
        if unit < 2:
            keep[to, :] = pull * share
        else:
            give[to, :] = (pull * share).astype(give.dtype)


def shards(src_emb, tgt_emb, src_lang, tgt_lang):
    f32, bf16 = jnp.float32, jnp.bfloat16
    rows, depth = src_emb.shape
    columns = tgt_emb.shape[0]
    row, col = lax.axis_index(ROW), lax.axis_index(COL)
    ring, plane = lax.axis_size(RING), lax.axis_size(PLANE)
    spread_size = lax.axis_size(SPREAD)
    n_src, n_tgt = rows * ring, columns * spread_size
    place, core = lax.axis_index(RING), lax.axis_index("core")
    total_src = src_lang.shape[0] * lax.axis_size(ROW)
    total_tgt = tgt_lang.shape[0] * lax.axis_size(COL)
    offsets = jnp.stack([place, 4 * core]).astype(jnp.int32)

    own_src_lang = lax.dynamic_slice(src_lang, (col * rows,), (rows,))
    own_tgt_lang = lax.dynamic_slice(tgt_lang, (row * columns,), (columns,))
    own = with_language(src_emb, own_src_lang)
    tgt = with_language(tgt_emb, own_tgt_lang)
    mine = lax.all_to_all(jnp.broadcast_to(tgt, (plane, *tgt.shape)), PLANE, 0, 0)
    up, down = shift(own, 1), shift(own, -1)
    pairs = [(down, up)]
    up, down = shift(up, 1), shift(down, -1)
    mine, up, down = lax.optimization_barrier((mine, up, down))
    pairs.append((down, up))
    theirs = lax.ppermute(mine, "core", SWAP)
    mine, theirs = (v.reshape(plane * columns, -1) for v in (mine, theirs))
    up, down = shift(up, 1), shift(down, -1)
    pairs.append((down, up))
    far = (shift(up[: rows // 2], 1), shift(down[rows // 2 :], -1))

    order = pltpu.VMEM((8, LANES), f32)
    pots = jax.ShapeDtypeStruct((8, LANES), f32)
    to_ring = jax.ShapeDtypeStruct((ring, 8, LANES), f32)
    to_spread = jax.ShapeDtypeStruct((spread_size, 8, LANES), f32)
    pair = (
        jax.ShapeDtypeStruct((2 * rows, n_tgt), f32),
        jax.ShapeDtypeStruct((n_tgt, 2 * rows), f32),
        jax.ShapeDtypeStruct((2 * rows, depth), bf16),
    )
    matmul = 2 * n_src * n_tgt * depth
    scale = LOG2E / (EPSILON * math.sqrt(depth))
    made = [
        call(
            functools.partial(pair_kernel, scale),
            (*pair, jax.ShapeDtypeStruct((2, LANES), f32)), [],
            near, other, mine, theirs,
            flops=matmul // 2, bytes_accessed=2**22,
        )
        for near, other in pairs
    ]
    *last, part = call(
        functools.partial(last_pair_kernel, scale),
        (*pair, to_ring), [order],
        offsets, own, *far, mine, theirs, *(m[3] for m in made),
        smem=1, flops=matmul // 2, bytes_accessed=2**22,
    )
    made.append(last)
    logits, logits_t, src_blocks = ([m[k] for m in made] for k in range(3))
    wide_src = pltpu.VMEM((n_src, LANES), f32)
    wide_tgt = pltpu.VMEM((n_tgt, LANES), f32)
    for step in range(ITERS):
        gathered = lax.all_to_all(part, RING, 0, 0)
        part, src_pots = call(
            functools.partial(src_pots_kernel, math.log2(total_tgt)),
            (to_spread, pots), [order, wide_src],
            offsets, *logits, gathered, smem=1, flops=8 * n_src * n_tgt, bytes_accessed=2**22,
        )
        gathered = lax.all_to_all(part, SPREAD, 0, 0)
        if step < ITERS - 1:
            (part,) = call(
                functools.partial(tgt_pots_kernel, math.log2(total_src)),
                (to_ring,), [order, wide_tgt],
                offsets, *logits_t, gathered, smem=1, flops=8 * n_src * n_tgt, bytes_accessed=2**22,
            )
    term = jax.ShapeDtypeStruct((rows, depth), f32)
    own_term, far_term = call(
        functools.partial(src_kernel, math.log2(total_src), 1.0 / total_tgt, (3,)),
        (term, jax.ShapeDtypeStruct((rows, depth), bf16)), [order, wide_src],
        offsets, logits[3], gathered, src_pots, mine, theirs,
        smem=1, flops=matmul // 4, bytes_accessed=2**22,
    )
    half = rows // 2
    up, down = shift(far_term[:half], 1), shift(far_term[half:], -1)
    gathered, own_term = lax.optimization_barrier((gathered, own_term))
    terms = call(
        functools.partial(src_kernel, math.log2(total_src), 1.0 / total_tgt, (0, 1, 2)),
        (term,) * 6, [order, wide_src],
        offsets, *logits[:3], gathered, src_pots, mine, theirs,
        smem=1, flops=3 * matmul // 4, bytes_accessed=2**23,
    )
    gathered, *terms = lax.optimization_barrier((gathered, *terms))
    keep, give = call(
        functools.partial(tgt_kernel, math.log2(total_src), 1.0 / total_src),
        (jax.ShapeDtypeStruct((n_tgt // 2, depth), f32), jax.ShapeDtypeStruct((n_tgt // 2, depth), bf16)),
        [order, wide_tgt],
        offsets, *logits_t, gathered, src_pots, *src_blocks,
        smem=1, flops=matmul, bytes_accessed=2**23,
    )
    keep = keep + lax.ppermute(give, "core", SWAP).astype(f32)
    parts = lax.all_to_all(keep.astype(bf16).reshape(plane, columns, depth), PLANE, 0, 0)
    tgt_pull = jnp.sum(parts.astype(f32), axis=0)
    pad = jnp.zeros((half, depth), f32)
    up = jnp.concatenate([up.astype(f32), pad])
    down = jnp.concatenate([pad, down.astype(f32)])
    for k in (2, 1, 0):
        up = shift((up + terms[2 * k]).astype(bf16), 1).astype(f32)
        down = shift((down + terms[2 * k + 1]).astype(bf16), -1).astype(f32)
    src_pull = own_term + up + down
    row_cost = jnp.sum(src_pull * src_emb.astype(f32), axis=1) * (-1.0 / math.sqrt(depth))
    return (src_pull, tgt_pull, row_cost)


def solution(mesh):
    split = Mesh(mesh.devices.reshape(SIZES), AXES)
    return jax.shard_map(
        shards,
        mesh=split,
        in_specs=(P(ROW + COL, None), P(COL + ROW, None), P(ROW), P(COL)),
        out_specs=(P(ROW + COL, None), P(COL + ROW, None), P(ROW + COL)),
        check_vma=False,
    )
```

time: 210 us -> 188 us (0.90)
  waiting for transfers between devices: 55.4 us -> 39.3 us
  blocking collectives: 67 us -> 70.7 us
  local copies, waits for them, and re-layouts: 8.34 us -> 5.14 us
  starting transfers between devices: 43.2 us -> 40.3 us
  other arithmetic: 7.73 us -> 5.08 us
    all_to_all x1, waiting for transfers between devices: 15.6 us -> 0.01 us  [shards(): lax.all_to_all(jnp.broadcast_to(tgt, (plane, *tgt.shape)), PLANE, 0, 0)]
    all_to_all x3, blocking collectives: 31.7 us -> 34.4 us  [shards(): gathered = lax.all_to_all(part, RING, 0, 0)]
    ppermute x16, starting transfers between devices: 30.3 us -> 27.7 us  [shift(): lax.ppermute(value, RING, [(i, (i + step) % size) for i in range(size)])]
    unnamed x18 -> x12, local copies, waits for them, and re-layouts: 4.31 us -> 2.41 us
    pallas_call x8 -> x12, Pallas kernels: 26.2 us -> 25.1 us  [call(): pl.pallas_call(kernel, out_shape=outs, in_specs=specs, out_specs=jax.tree...]
  transfers between devices with their start and end apart: 20 -> 20, of which waited for: 10 -> 7; matrix products, arithmetic and copies ran while one was open for 4% -> 2% of each run, Pallas kernels for 1% -> 5%
where the time goes in v3:
time: 188 us; the launch traced here: 187 us
  blocking collectives  70.7 us (38%)
  starting transfers between devices  40.3 us (21%)
  waiting for transfers between devices  39.3 us (21%)
  Pallas kernels  25.1 us (13%)
  local copies, waits for them, and re-layouts  5.14 us (3%)
  other arithmetic  5.08 us (3%)
    all_to_all x3, blocking collectives, shards(): gathered = lax.all_to_all(part, SPREAD, 0, 0)  36.3 us
    ppermute x16, waiting for transfers between devices, shift(): lax.ppermute(value, RING, [(i, (i + step) % size) for i in range(size)])  36.3 us
    all_to_all x3, blocking collectives, shards(): gathered = lax.all_to_all(part, RING, 0, 0)  34.4 us
    ppermute x16, starting transfers between devices, shift(): lax.ppermute(value, RING, [(i, (i + step) % size) for i in range(size)])  27.7 us
    pallas_call x12, Pallas kernels, call(): pl.pallas_call(kernel, out_shape=outs, in_specs=specs, out_specs=jax.tree...  25.1 us
    all_to_all x1, starting transfers between devices, shards(): lax.all_to_all(jnp.broadcast_to(tgt, (plane, *tgt.shape)), PLANE, 0, 0)  7.48 us
    all_to_all x1, starting transfers between devices, shards(): lax.all_to_all(keep.astype(bf16).reshape(plane, columns, depth), PLANE, 0...  5.04 us
  transfers between devices with their start and end apart: 20, of which 7 were waited for; matrix products, arithmetic and copies ran while one was open for 2% of the time, Pallas kernels for 5%

profile of v3, /device:TPU:2, one launch (start us, length us, event | category | flops | bytes accessed | tf_op | source)
XLA Modules:
  0.0 186.5 jit_solution(11918767264152085850)
XLA Ops:
  3.5 7.5 %all-to-all-start = ((bf16[16,32,1152]{2,1,0:T(8,128)(2,1)}), bf16[16,32,1152]{2,1,0:T(8,128)(2,1)S(1)}, u32[]{:S(2)}, u32[]{:S(2)}) async-start(bf16[16,32,1152]{2,1,0:T(8,128)(2,1)} %broadcast_in_dim.2), calls=%async_computation | async-start | bytes 2359296 | tf_op jit(solution)/shard_map/all_to_all | solution.py:212
  13.9 4.0 %collective-permute-start = (bf16[128,1152]{1,0:T(8,128)(2,1)S(1)}, bf16[128,1152]{1,0:T(8,128)(2,1)S(1)}, u32[]{:S(2)}, u32[]{:S(2)}) collective-permute-start(bf16[128,1152]{1,0:T(8,128)(2,1)S(1)} %pad_maximum_fusion.own), channel_id=1, source_target_pairs={{0,52},{4,0},{16,4},{20,16},{32,20},{36,32},{48,36},{52,48},{1,53}... | collective-permute-start | bytes 884744 | tf_op jit(solution)/shard_map/ppermute | solution.py:53
  17.9 6.4 %collective-permute-done.1.other = bf16[128,1152]{1,0:T(8,128)(2,1)S(1)} collective-permute-done((bf16[128,1152]{1,0:T(8,128)(2,1)S(1)}, bf16[128,1152]{1,0:T(8,128)(2,1)S(1)}, u32[]{:S(2)}, u32[]{:S(2)}) %collective-permute-start.1) | collective-permute-done | bytes 294944 | tf_op jit(solution)/shard_map/ppermute | solution.py:53
  24.3 3.2 %collective-permute-start.3 = (bf16[128,1152]{1,0:T(8,128)(2,1)S(1)}, bf16[128,1152]{1,0:T(8,128)(2,1)}, u32[]{:S(2)}, u32[]{:S(2)}) collective-permute-start(bf16[128,1152]{1,0:T(8,128)(2,1)S(1)} %collective-permute-done.near), channel_id=1, source_target_pairs={{0,52},{4,0},{16,4},{20,16},{32,20},{36,32},{48,36},{52,48},{1,53}... | collective-permute-start | bytes 884744 | tf_op jit(solution)/shard_map/ppermute | solution.py:53
  28.2 4.8 %collective-permute-done.2.other = bf16[128,1152]{1,0:T(8,128)(2,1)S(1)} collective-permute-done((bf16[128,1152]{1,0:T(8,128)(2,1)S(1)}, bf16[128,1152]{1,0:T(8,128)(2,1)S(1)}, u32[]{:S(2)}, u32[]{:S(2)}) %collective-permute-start.2) | collective-permute-done | bytes 294944 | tf_op jit(solution)/shard_map/ppermute | solution.py:53
  36.3 7.1 %collective-permute-done.5.near = bf16[128,1152]{1,0:T(8,128)(2,1)S(1)} collective-permute-done((bf16[128,1152]{1,0:T(8,128)(2,1)}, bf16[128,1152]{1,0:T(8,128)(2,1)S(1)}, u32[]{:S(2)}, u32[]{:S(2)}) %collective-permute-start.5) | collective-permute-done | bytes 294944 | tf_op jit(solution)/shard_map/ppermute | solution.py:53
  43.4 3.6 %collective-permute-start.8 = (bf16[64,1152]{1,0:T(8,128)(2,1)S(1)}, bf16[64,1152]{1,0:T(8,128)(2,1)S(1)}, u32[]{:S(2)}, u32[]{:S(2)}) collective-permute-start(bf16[64,1152]{1,0:T(8,128)(2,1)S(1)} %slice.17), channel_id=1, source_target_pairs={{0,52},{4,0},{16,4},{20,16},{32,20},{36,32},{48,36},{52,48},{1,53}... | collective-permute-start | bytes 442376 | tf_op jit(solution)/shard_map/ppermute | solution.py:53
  48.3 2.7 %shard_map.68 = (f32[256,1024]{1,0:T(8,128)S(1)}, f32[1024,256]{1,0:T(8,128)S(1)}, bf16[256,1024]{1,0:T(8,128)(2,1)S(1)}, f32[2,128]{1,0:T(2,128)S(1)}) custom-call(bf16[128,1152]{1,0:T(8,128)(2,1)} %collective-permute-done.3.near, bf16[128,1152]{1,0:T(8,128)(2,1)S(1)} %copy-done.3, bf16[512,1152]{1,0:T(8,128)(2,1)S(1)} %bitcast.5, ...), custom_call_target="tpu_custom_call" | custom-call | flops 1073741824 | bytes 4194304 | tf_op jit(solution)/shard_map/pallas_call | solution.py:38
  56.8 13.6 %all_to_all.40.refs_4_ = f32[8,8,128]{2,1,0:T(8,128)S(1)} all-to-all(f32[8,8,128]{2,1,0:T(8,128)S(1)} %get-tuple-element.59), channel_id=1, replica_groups=mesh['x'=4,'zh'=4,'core'=2,'zl'=2,'y'=4] {'zh','zl'}, dimensions={0} | all-to-all | bytes 65536 | tf_op jit(solution)/shard_map/all_to_all | solution.py:255
  72.6 13.8 %all_to_all.41.refs_4_ = f32[32,8,128]{2,1,0:T(8,128)S(1)} all-to-all(f32[32,8,128]{2,1,0:T(8,128)S(1)} %get-tuple-element.60), channel_id=1, replica_groups=mesh['x'=4,'zh'=4,'core'=2,'zl'=2,'y'=4] {'x','y','core'}, dimensions={0} | all-to-all | bytes 262144 | tf_op jit(solution)/shard_map/all_to_all | solution.py:261
  88.1 10.4 %all_to_all.42.refs_4_ = f32[8,8,128]{2,1,0:T(8,128)S(1)} all-to-all(f32[8,8,128]{2,1,0:T(8,128)S(1)} %shard_map.72), channel_id=1, replica_groups=mesh['x'=4,'zh'=4,'core'=2,'zl'=2,'y'=4] {'zh','zl'}, dimensions={0} | all-to-all | bytes 65536 | tf_op jit(solution)/shard_map/all_to_all | solution.py:255
  100.6 11.3 %all_to_all.43.refs_4_ = f32[32,8,128]{2,1,0:T(8,128)S(1)} all-to-all(f32[32,8,128]{2,1,0:T(8,128)S(1)} %get-tuple-element.61), channel_id=1, replica_groups=mesh['x'=4,'zh'=4,'core'=2,'zl'=2,'y'=4] {'x','y','core'}, dimensions={0} | all-to-all | bytes 262144 | tf_op jit(solution)/shard_map/all_to_all | solution.py:261
  113.6 10.4 %all_to_all.44.refs_4_ = f32[8,8,128]{2,1,0:T(8,128)S(1)} all-to-all(f32[8,8,128]{2,1,0:T(8,128)S(1)} %shard_map.74), channel_id=1, replica_groups=mesh['x'=4,'zh'=4,'core'=2,'zl'=2,'y'=4] {'zh','zl'}, dimensions={0} | all-to-all | bytes 65536 | tf_op jit(solution)/shard_map/all_to_all | solution.py:255
  125.7 11.3 %all_to_all.45.refs_1_.refs_3_.refs_4_ = f32[32,8,128]{2,1,0:T(8,128)S(1)} all-to-all(f32[32,8,128]{2,1,0:T(8,128)S(1)} %get-tuple-element.62), channel_id=1, replica_groups=mesh['x'=4,'zh'=4,'core'=2,'zl'=2,'y'=4] {'x','y','core'}, dimensions={0} | all-to-all | bytes 262144 | tf_op jit(solution)/shard_map/all_to_all | solution.py:261
  138.4 2.6 %shard_map.77 = (f32[128,1024]{1,0:T(8,128)S(1)}, f32[128,1024]{1,0:T(8,128)S(1)}, f32[128,1024]{1,0:T(8,128)S(1)}, f32[128,1024]{1,0:T(8,128)S(1)}, f32[128,1024]{1,0:T(8,128)S(1)}, /*index=5*/f32[128,1024]{1,0:T(8,128)S(1)}) custom-call(s32[2]{0:T(128)S(1)} %pad_add_fusion.offsets, f32[256,1024]{1,0:T(8,128)S(1)} %get-tuple-element.46.refs_0_, ...), custom_call_target="tpu_custom_call" | custom-call | flops 1610612736 | bytes 8388608 | tf_op jit(solution)/shard_map/pallas_call | solution.py:38
  141.7 2.7 %collective-permute-start.13 = (bf16[64,1024]{1,0:T(8,128)(2,1)S(1)}, bf16[64,1024]{1,0:T(8,128)(2,1)S(1)}, u32[]{:S(2)}, u32[]{:S(2)}) collective-permute-start(bf16[64,1024]{1,0:T(8,128)(2,1)S(1)} %get-tuple-element.90), channel_id=1, source_target_pairs={{0,52},{4,0},{16,4},{20,16},{32,20},{36,32},{48,36},{52,48},{1,53}... | collective-permute-start | bytes 393224 | tf_op jit(solution)/shard_map/ppermute | solution.py:53
  144.3 3.2 %shard_map.78 = (f32[512,1024]{1,0:T(8,128)S(1)}, bf16[512,1024]{1,0:T(8,128)(2,1)S(1)}) custom-call(s32[2]{0:T(128)S(1)} %pad_add_fusion.offsets, f32[1024,256]{1,0:T(8,128)S(1)} %get-tuple-element.55.refs_0_, f32[1024,256]{1,0:T(8,128)S(1)} %get-tuple-element.56.refs_1_, f32[1024,256]{1,0:T(8,128)S(1)} %get-tuple-element.57.refs_2_, ...), custom_call_target="tpu_custom_call" | custom-call | flops 2147483648 | bytes 8388608 | tf_op jit(solution)/shard_map/pallas_call | solution.py:38
  147.7 3.2 %collective-permute-start.14 = (bf16[128,1024]{1,0:T(8,128)(2,1)S(1)}, bf16[128,1024]{1,0:T(8,128)(2,1)S(1)}, u32[]{:S(2)}, u32[]{:S(2)}) collective-permute-start(bf16[128,1024]{1,0:T(8,128)(2,1)S(1)} %add_convert_fusion.3), channel_id=1, source_target_pairs={{0,52},{4,0},{16,4},{20,16},{32,20},{36,32},{48,36},{52,48},{1,53}... | collective-permute-start | bytes 786440 | tf_op jit(solution)/shard_map/ppermute | solution.py:53
  151.1 5.5 %collective-permute-done.14 = bf16[128,1024]{1,0:T(8,128)(2,1)S(1)} collective-permute-done((bf16[128,1024]{1,0:T(8,128)(2,1)S(1)}, bf16[128,1024]{1,0:T(8,128)(2,1)S(1)}, u32[]{:S(2)}, u32[]{:S(2)}) %collective-permute-start.14) | collective-permute-done | bytes 262176 | tf_op jit(solution)/shard_map/ppermute | solution.py:53
  156.6 2.9 %collective-permute-start.15 = (bf16[128,1024]{1,0:T(8,128)(2,1)S(1)}, bf16[128,1024]{1,0:T(8,128)(2,1)S(1)}, u32[]{:S(2)}, u32[]{:S(2)}) collective-permute-start(bf16[128,1024]{1,0:T(8,128)(2,1)S(1)} %add_convert_fusion.2), channel_id=1, source_target_pairs={{0,52},{4,0},{16,4},{20,16},{32,20},{36,32},{48,36},{52,48},{1,53}... | collective-permute-start | bytes 786440 | tf_op jit(solution)/shard_map/ppermute | solution.py:53
  159.6 5.0 %collective-permute-done.15 = bf16[128,1024]{1,0:T(8,128)(2,1)S(1)} collective-permute-done((bf16[128,1024]{1,0:T(8,128)(2,1)S(1)}, bf16[128,1024]{1,0:T(8,128)(2,1)S(1)}, u32[]{:S(2)}, u32[]{:S(2)}) %collective-permute-start.15) | collective-permute-done | bytes 262176 | tf_op jit(solution)/shard_map/ppermute | solution.py:53
  168.5 5.0 %all-to-all-start.7 = ((bf16[16,32,1024]{2,1,0:T(8,128)(2,1)}), bf16[16,32,1024]{2,1,0:T(8,128)(2,1)S(1)}, u32[]{:S(2)}, u32[]{:S(2)}) async-start(bf16[16,32,1024]{2,1,0:T(8,128)(2,1)} %bitcast.4), calls=%async_computation.7 | async-start | bytes 2097152 | tf_op jit(solution)/shard_map/all_to_all | solution.py:293
  173.8 7.6 %collective-permute-done.12 = bf16[128,1024]{1,0:T(8,128)(2,1)S(1)} collective-permute-done((bf16[128,1024]{1,0:T(8,128)(2,1)S(1)}, bf16[128,1024]{1,0:T(8,128)(2,1)S(1)}, u32[]{:S(2)}, u32[]{:S(2)}) %collective-permute-start.12) | collective-permute-done | bytes 262176 | tf_op jit(solution)/shard_map/ppermute | solution.py:53
  182.7 2.9 %all-to-all-done.7 = bf16[16,32,1024]{2,1,0:T(8,128)(2,1)S(1)} async-done(((bf16[16,32,1024]{2,1,0:T(8,128)(2,1)}), bf16[16,32,1024]{2,1,0:T(8,128)(2,1)S(1)}, u32[]{:S(2)}, u32[]{:S(2)}) %all-to-all-start.7) | async-done | bytes 1048608 | tf_op jit(solution)/shard_map/all_to_all | solution.py:293
  (67 shorter events, 35.0 us)
Async XLA Ops:
  0.6 11.2 %copy-start.4 = (bf16[128,1024]{1,0:T(8,128)(2,1)S(1)}, bf16[128,1024]{1,0:T(8,128)(2,1)}, u32[]{:S(2)}) copy-start(bf16[128,1024]{1,0:T(8,128)(2,1)} %param.4) | copy-start | bytes 786436
  3.5 30.3 %all-to-all-start = ((bf16[16,32,1152]{2,1,0:T(8,128)(2,1)}), bf16[16,32,1152]{2,1,0:T(8,128)(2,1)S(1)}, u32[]{:S(2)}, u32[]{:S(2)}) async-start(bf16[16,32,1152]{2,1,0:T(8,128)(2,1)} %broadcast_in_dim.2), calls=%async_computation | async-start | bytes 2359296 | tf_op jit(solution)/shard_map/all_to_all | solution.py:212
  11.9 12.4 %collective-permute-start.1 = (bf16[128,1152]{1,0:T(8,128)(2,1)S(1)}, bf16[128,1152]{1,0:T(8,128)(2,1)S(1)}, u32[]{:S(2)}, u32[]{:S(2)}) collective-permute-start(bf16[128,1152]{1,0:T(8,128)(2,1)S(1)} %pad_maximum_fusion.own), channel_id=1, source_target_pairs={{0,4},{4,16},{16,20},{20,32},{32,36},{36,48},{48,52},{52,0},{1,5},... | collective-permute-start | bytes 884744 | tf_op jit(solution)/shard_map/ppermute | solution.py:53
  13.9 10.4 %collective-permute-start = (bf16[128,1152]{1,0:T(8,128)(2,1)S(1)}, bf16[128,1152]{1,0:T(8,128)(2,1)S(1)}, u32[]{:S(2)}, u32[]{:S(2)}) collective-permute-start(bf16[128,1152]{1,0:T(8,128)(2,1)S(1)} %pad_maximum_fusion.own), channel_id=1, source_target_pairs={{0,52},{4,0},{16,4},{20,16},{32,20},{36,32},{48,36},{52,48},{1,53}... | collective-permute-start | bytes 884744 | tf_op jit(solution)/shard_map/ppermute | solution.py:53
  24.3 8.8 %collective-permute-start.2 = (bf16[128,1152]{1,0:T(8,128)(2,1)S(1)}, bf16[128,1152]{1,0:T(8,128)(2,1)S(1)}, u32[]{:S(2)}, u32[]{:S(2)}) collective-permute-start(bf16[128,1152]{1,0:T(8,128)(2,1)S(1)} %collective-permute-done.1.other), channel_id=1, source_target_pairs={{0,4},{4,16},{16,20},{20,32},{32,36},{36,48},{48,52},{52,0},{1,5},... | collective-permute-start | bytes 884744 | tf_op jit(solution)/shard_map/ppermute | solution.py:53
  24.3 8.8 %collective-permute-start.3 = (bf16[128,1152]{1,0:T(8,128)(2,1)S(1)}, bf16[128,1152]{1,0:T(8,128)(2,1)}, u32[]{:S(2)}, u32[]{:S(2)}) collective-permute-start(bf16[128,1152]{1,0:T(8,128)(2,1)S(1)} %collective-permute-done.near), channel_id=1, source_target_pairs={{0,52},{4,0},{16,4},{20,16},{32,20},{36,32},{48,36},{52,48},{1,53}... | collective-permute-start | bytes 884744 | tf_op jit(solution)/shard_map/ppermute | solution.py:53
  33.8 13.6 %collective-permute-start.4 = (bf16[16,32,1152]{2,1,0:T(8,128)(2,1)S(1)}, bf16[16,32,1152]{2,1,0:T(8,128)(2,1)S(1)}, u32[]{:S(2)}, u32[]{:S(2)}) collective-permute-start(bf16[16,32,1152]{2,1,0:T(8,128)(2,1)S(1)} %all-to-all-done), channel_id=1, source_target_pairs={{0,8},{8,0},{1,9},{9,1},{2,10},{10,2},{3,11},{11,3},{4,12},{12,4},... | collective-permute-start | bytes 3538952 | tf_op jit(solution)/shard_map/ppermute | solution.py:218
  33.8 9.6 %collective-permute-start.5 = (bf16[128,1152]{1,0:T(8,128)(2,1)}, bf16[128,1152]{1,0:T(8,128)(2,1)S(1)}, u32[]{:S(2)}, u32[]{:S(2)}) collective-permute-start(bf16[128,1152]{1,0:T(8,128)(2,1)} %collective-permute-done.3.near), channel_id=1, source_target_pairs={{0,52},{4,0},{16,4},{20,16},{32,20},{36,32},{48,36},{52,48},{1,53}... | collective-permute-start | bytes 884744 | tf_op jit(solution)/shard_map/ppermute | solution.py:53
  36.2 10.9 %collective-permute-start.6 = (bf16[128,1152]{1,0:T(8,128)(2,1)}, bf16[128,1152]{1,0:T(8,128)(2,1)S(1)}, u32[]{:S(2)}, u32[]{:S(2)}) collective-permute-start(bf16[128,1152]{1,0:T(8,128)(2,1)} %copy-done.2), channel_id=1, source_target_pairs={{0,4},{4,16},{16,20},{20,32},{32,36},{36,48},{48,52},{52,0},{1,5},... | collective-permute-start | bytes 884744 | tf_op jit(solution)/shard_map/ppermute | solution.py:53
  43.4 11.1 %collective-permute-start.8 = (bf16[64,1152]{1,0:T(8,128)(2,1)S(1)}, bf16[64,1152]{1,0:T(8,128)(2,1)S(1)}, u32[]{:S(2)}, u32[]{:S(2)}) collective-permute-start(bf16[64,1152]{1,0:T(8,128)(2,1)S(1)} %slice.17), channel_id=1, source_target_pairs={{0,52},{4,0},{16,4},{20,16},{32,20},{36,32},{48,36},{52,48},{1,53}... | collective-permute-start | bytes 442376 | tf_op jit(solution)/shard_map/ppermute | solution.py:53
  47.1 7.5 %collective-permute-start.7 = (bf16[64,1152]{1,0:T(8,128)(2,1)S(1)}, bf16[64,1152]{1,0:T(8,128)(2,1)S(1)}, u32[]{:S(2)}, u32[]{:S(2)}) collective-permute-start(bf16[64,1152]{1,0:T(8,128)(2,1)S(1)} %slice.16), channel_id=1, source_target_pairs={{0,4},{4,16},{16,20},{20,32},{32,36},{36,48},{48,52},{52,0},{1,5},... | collective-permute-start | bytes 442376 | tf_op jit(solution)/shard_map/ppermute | solution.py:53
  47.3 1.0 copy-start.3
  51.0 1.8 copy-start.1
  141.0 9.9 %collective-permute-start.9 = (bf16[64,1024]{1,0:T(8,128)(2,1)S(1)}, bf16[64,1024]{1,0:T(8,128)(2,1)S(1)}, u32[]{:S(2)}, u32[]{:S(2)}) collective-permute-start(bf16[64,1024]{1,0:T(8,128)(2,1)S(1)} %get-tuple-element.89), channel_id=1, source_target_pairs={{0,4},{4,16},{16,20},{20,32},{32,36},{36,48},{48,52},{52,0},{1,5},... | collective-permute-start | bytes 393224 | tf_op jit(solution)/shard_map/ppermute | solution.py:53
  141.7 6.0 %collective-permute-start.13 = (bf16[64,1024]{1,0:T(8,128)(2,1)S(1)}, bf16[64,1024]{1,0:T(8,128)(2,1)S(1)}, u32[]{:S(2)}, u32[]{:S(2)}) collective-permute-start(bf16[64,1024]{1,0:T(8,128)(2,1)S(1)} %get-tuple-element.90), channel_id=1, source_target_pairs={{0,52},{4,0},{16,4},{20,16},{32,20},{36,32},{48,36},{52,48},{1,53}... | collective-permute-start | bytes 393224 | tf_op jit(solution)/shard_map/ppermute | solution.py:53
  147.6 19.6 %collective-permute-start.17 = (bf16[512,1024]{1,0:T(8,128)(2,1)S(1)}, bf16[512,1024]{1,0:T(8,128)(2,1)S(1)}, u32[]{:S(2)}, u32[]{:S(2)}) collective-permute-start(bf16[512,1024]{1,0:T(8,128)(2,1)S(1)} %get-tuple-element.86), channel_id=1, source_target_pairs={{0,8},{8,0},{1,9},{9,1},{2,10},{10,2},{3,11},{11,3},{4,12},{12,4},... | collective-permute-start | bytes 3145736 | tf_op jit(solution)/shard_map/ppermute | solution.py:292
  147.7 8.8 %collective-permute-start.14 = (bf16[128,1024]{1,0:T(8,128)(2,1)S(1)}, bf16[128,1024]{1,0:T(8,128)(2,1)S(1)}, u32[]{:S(2)}, u32[]{:S(2)}) collective-permute-start(bf16[128,1024]{1,0:T(8,128)(2,1)S(1)} %add_convert_fusion.3), channel_id=1, source_target_pairs={{0,52},{4,0},{16,4},{20,16},{32,20},{36,32},{48,36},{52,48},{1,53}... | collective-permute-start | bytes 786440 | tf_op jit(solution)/shard_map/ppermute | solution.py:53
  151.0 8.5 %collective-permute-start.10 = (bf16[128,1024]{1,0:T(8,128)(2,1)S(1)}, bf16[128,1024]{1,0:T(8,128)(2,1)S(1)}, u32[]{:S(2)}, u32[]{:S(2)}) collective-permute-start(bf16[128,1024]{1,0:T(8,128)(2,1)S(1)} %add_convert_fusion.6), channel_id=1, source_target_pairs={{0,4},{4,16},{16,20},{20,32},{32,36},{36,48},{48,52},{52,0},{1,5},... | collective-permute-start | bytes 786440 | tf_op jit(solution)/shard_map/ppermute | solution.py:53
  156.6 8.0 %collective-permute-start.15 = (bf16[128,1024]{1,0:T(8,128)(2,1)S(1)}, bf16[128,1024]{1,0:T(8,128)(2,1)S(1)}, u32[]{:S(2)}, u32[]{:S(2)}) collective-permute-start(bf16[128,1024]{1,0:T(8,128)(2,1)S(1)} %add_convert_fusion.2), channel_id=1, source_target_pairs={{0,52},{4,0},{16,4},{20,16},{32,20},{36,32},{48,36},{52,48},{1,53}... | collective-permute-start | bytes 786440 | tf_op jit(solution)/shard_map/ppermute | solution.py:53
  159.5 14.1 %collective-permute-start.11 = (bf16[128,1024]{1,0:T(8,128)(2,1)S(1)}, bf16[128,1024]{1,0:T(8,128)(2,1)S(1)}, u32[]{:S(2)}, u32[]{:S(2)}) collective-permute-start(bf16[128,1024]{1,0:T(8,128)(2,1)S(1)} %add_convert_fusion.5), channel_id=1, source_target_pairs={{0,4},{4,16},{16,20},{20,32},{32,36},{36,48},{48,52},{52,0},{1,5},... | collective-permute-start | bytes 786440 | tf_op jit(solution)/shard_map/ppermute | solution.py:53
  164.6 9.1 %collective-permute-start.16 = (bf16[128,1024]{1,0:T(8,128)(2,1)S(1)}, bf16[128,1024]{1,0:T(8,128)(2,1)S(1)}, u32[]{:S(2)}, u32[]{:S(2)}) collective-permute-start(bf16[128,1024]{1,0:T(8,128)(2,1)S(1)} %add_convert_fusion.1), channel_id=1, source_target_pairs={{0,52},{4,0},{16,4},{20,16},{32,20},{36,32},{48,36},{52,48},{1,53}... | collective-permute-start | bytes 786440 | tf_op jit(solution)/shard_map/ppermute | solution.py:53
  168.5 12.8 %copy-start.5 = (bf16[128,1024]{1,0:T(8,128)(2,1)S(1)}, bf16[128,1024]{1,0:T(8,128)(2,1)}, u32[]{:S(2)}) copy-start(bf16[128,1024]{1,0:T(8,128)(2,1)} %param.4) | copy-start | bytes 786436
  168.5 17.1 %all-to-all-start.7 = ((bf16[16,32,1024]{2,1,0:T(8,128)(2,1)}), bf16[16,32,1024]{2,1,0:T(8,128)(2,1)S(1)}, u32[]{:S(2)}, u32[]{:S(2)}) async-start(bf16[16,32,1024]{2,1,0:T(8,128)(2,1)} %bitcast.4), calls=%async_computation.7 | async-start | bytes 2097152 | tf_op jit(solution)/shard_map/all_to_all | solution.py:293
  173.7 7.7 %collective-permute-start.12 = (bf16[128,1024]{1,0:T(8,128)(2,1)S(1)}, bf16[128,1024]{1,0:T(8,128)(2,1)S(1)}, u32[]{:S(2)}, u32[]{:S(2)}) collective-permute-start(bf16[128,1024]{1,0:T(8,128)(2,1)S(1)} %add_convert_fusion.4), channel_id=1, source_target_pairs={{0,4},{4,16},{16,20},{20,32},{32,36},{36,48},{48,52},{52,0},{1,5},... | collective-permute-start | bytes 786440 | tf_op jit(solution)/shard_map/ppermute | solution.py:53
  (2 other events, 1.4 us)

commit v4 on v3

v4 whole, which is shorter than its diff:
```python
import functools
import math

import jax
import jax.numpy as jnp
from jax import lax
from jax.experimental import pallas as pl
from jax.experimental.pallas import tpu as pltpu
from jax.sharding import Mesh, PartitionSpec as P

ITERS = 3
NEG = -1e30
EPSILON = 0.5
LOG2E = math.log2(math.e)
LANES = 128
DISTANCES = (1, 7, 2, 6, 3, 5, 0, 4)

AXES = ("x", "zh", "core", "zl", "y")
SIZES = (4, 4, 2, 2, 4)
ROW = ("x", "zh", "core")
COL = ("zl", "y")
RING = ("zh", "zl")
PLANE = ("x", "y")
SPREAD = ("x", "y", "core")
SWAP = [(0, 1), (1, 0)]

VMEM = pl.BlockSpec(memory_space=pltpu.VMEM)
SMEM = pl.BlockSpec(memory_space=pltpu.SMEM)
IN_HBM = pl.BlockSpec(memory_space=pl.ANY)
CONTRACT_LAST = (((1,), (1,)), ((), ()))


def dot(a, b, dims=(((1,), (0,)), ((), ()))):
    return lax.dot_general(a, b, dims, preferred_element_type=jnp.float32)


def call(kernel, outs, scratch, *operands, smem=0, in_hbm=(), outs_in_hbm=(), flops=0, bytes_accessed=0):
    specs = [
        SMEM if k < smem else IN_HBM if k in in_hbm else VMEM for k in range(len(operands))
    ]
    operands = [
        pltpu.with_memory_space_constraint(v, pltpu.HBM) if k in in_hbm else v
        for k, v in enumerate(operands)
    ]
    outs = [
        pltpu.HBM(out.shape, out.dtype) if k in outs_in_hbm else out for k, out in enumerate(outs)
    ]
    return pl.pallas_call(
        kernel,
        out_shape=outs,
        in_specs=specs,
        out_specs=[IN_HBM if k in outs_in_hbm else VMEM for k in range(len(outs))],
        scratch_shapes=scratch,
        compiler_params=pltpu.CompilerParams(vmem_limit_bytes=16 * 2**20),
        cost_estimate=pl.CostEstimate(
            flops=flops, bytes_accessed=bytes_accessed, transcendentals=0
        ),
    )(*operands)


def shift(value, step):
    size = lax.axis_size(RING)
    return lax.ppermute(value, RING, [(i, (i + step) % size) for i in range(size)])


def copy_all(pairs, sems):
    copies = [pltpu.make_async_copy(a, b, sems.at[k]) for k, (a, b) in enumerate(pairs)]
    for copy in copies:
        copy.start()
    for copy in copies:
        copy.wait()


def one_hot(line, dtype):
    labels = jnp.broadcast_to(line.astype(jnp.float32), (LANES, LANES)).T
    lanes = lax.broadcasted_iota(jnp.int32, (LANES, LANES), 1).astype(jnp.float32)
    return (labels == lanes).astype(dtype)


def label_kernel(offsets, src_lang, tgt_lang, src, tgt, src_out, tgt_out, src_labels, tgt_labels, hot, one, sems):
    columns, depth = tgt.shape
    copy_all([(tgt_lang, tgt_labels), (tgt, one.at[:, :depth]), (src_lang, src_labels)], sems)
    bulk = pltpu.make_async_copy(src, src_out.at[:, :depth], sems.at[0])
    bulk.start()
    here = offsets[3] * columns
    hot[...] = one_hot(tgt_labels[pl.ds(here // LANES, 1), :], jnp.float32)
    one[:, depth:] = hot[pl.ds(pl.multiple_of(lax.rem(here, LANES), columns), columns), :].astype(one.dtype)
    bulk.wait()
    copies = [
        pltpu.make_async_copy(one, tgt_out.at[k], sems.at[k]) for k in range(tgt_out.shape[0])
    ]
    for copy in copies:
        copy.start()
    src_out[:, depth:] = one_hot(src_labels[pl.ds(offsets[2], 1), :], src_out.dtype)
    for copy in copies:
        copy.wait()


def columns_sums(tables, added):
    tiles = tables[0].shape[1] // LANES

    def blocks(t):
        start = 0
        for table in tables:
            for c in range(table.shape[0] // LANES):
                z = table[c * LANES : (c + 1) * LANES, t * LANES : (t + 1) * LANES]
                if added is not None:
                    z = z + added[start : start + LANES, :]
                start += LANES
                yield z.reshape(LANES // 8, 8, LANES)

    tops, totals = [], []
    for t in range(tiles):
        top = functools.reduce(jnp.maximum, (jnp.max(z, axis=0) for z in blocks(t)))
        top = jnp.max(top, axis=0, keepdims=True)
        total = functools.reduce(
            jnp.add, (jnp.sum(jnp.exp2(z - top[None]), axis=0) for z in blocks(t))
        )
        tops.append(top)
        totals.append(jnp.sum(total, axis=0, keepdims=True))
    return tops, totals


def columns_lse(tables, added):
    return [top + jnp.log2(total) for top, total in zip(*columns_sums(tables, added))]


def send_out(parts, offset, table, order, out):
    for part, at in zip(parts, table):
        order[pl.ds(lax.rem(at + offset, 8), 1), :] = part
    out[...] = jnp.broadcast_to(order[...][None], out.shape)


def merge(gathered, log_count, offset, table, order):
    parts = gathered[...]
    top = jnp.max(parts, axis=0)
    total = jnp.sum(jnp.exp2(parts - top[None]), axis=0)
    order[...] = log_count - (top + jnp.log2(total))
    return jnp.concatenate([order[pl.ds(lax.rem(at + offset, 8), 1), :] for at in table])


def spread(pots, wide):
    columns = pots.T
    for c in range(8):
        wide[c * LANES : (c + 1) * LANES, :] = jnp.broadcast_to(
            columns[:, c : c + 1], (LANES, LANES)
        )


def make_logits(scale, src, tgt, logits, logits_t):
    depth = src.shape[1] - LANES
    half = tgt.shape[0] // 2
    emb, hot = src[:, :depth], src[:, depth:]
    for side in range(2):
        to = slice(side * half, (side + 1) * half)
        tgt_emb, tgt_hot = tgt[to, :depth], tgt[to, depth:]
        same = dot(tgt_hot, hot, CONTRACT_LAST) > 0.5
        logits_t[to, :] = jnp.where(same, dot(tgt_emb, emb, CONTRACT_LAST) * scale, NEG)
        same = dot(hot, tgt_hot, CONTRACT_LAST) > 0.5
        logits[:, to] = jnp.where(same, dot(emb, tgt_emb, CONTRACT_LAST) * scale, NEG)


def first_pair_kernel(scale, near, other, mine, theirs, src, logits, logits_t, part, tgt, sems):
    half = mine.shape[0]
    copy_all(
        [
            (mine, tgt.at[:half]),
            (theirs, tgt.at[half:]),
            (near, src.at[: near.shape[0]]),
            (other, src.at[near.shape[0] :]),
        ],
        sems,
    )
    make_logits(scale, src, tgt, logits, logits_t)
    part[...] = jnp.concatenate(columns_lse([logits_t], None))


def halves_kernel(up, down, up_out, down_out, sems):
    half = up_out.shape[0]
    copy_all([(up.at[:half], up_out), (down.at[half:], down_out)], sems)


def pair_kernel(scale, near, other, tgt, src, logits, logits_t, part, sems):
    copy_all([(near, src.at[: near.shape[0]]), (other, src.at[near.shape[0] :])], sems)
    make_logits(scale, src, tgt, logits, logits_t)
    part[...] = jnp.concatenate(columns_lse([logits_t], None))


def last_pair_kernel(scale, offsets, own, far_up, far_down, tgt, *refs):
    parts, (src, logits, logits_t, out, order, sems) = refs[:3], refs[3:]
    rows, half = own.shape[0], far_up.shape[0]
    copy_all(
        [
            (own, src.at[:rows]),
            (far_up, src.at[rows : rows + half]),
            (far_down, src.at[rows + half :]),
        ],
        sems,
    )
    make_logits(scale, src, tgt, logits, logits_t)
    parts = [part[r : r + 1, :] for part in parts for r in range(2)]
    send_out(parts + columns_lse([logits_t], None), offsets[0], DISTANCES, order, out)


def src_pots_kernel(log_count, offsets, *refs):
    tables, (gathered, out, pots, order, wide) = refs[:4], refs[4:]
    local = merge(gathered, log_count, offsets[0], DISTANCES, order)
    pots[...] = local
    spread(local, wide)
    send_out(columns_lse(tables, wide), offsets[1], range(8), order, out)


def tgt_pots_kernel(log_count, offsets, *refs):
    tables, (gathered, out, order, wide) = refs[:4], refs[4:]
    spread(merge(gathered, log_count, offsets[1], range(8), order), wide)
    parts = [part for table in tables for part in columns_lse([table], wide)]
    send_out(parts, offsets[0], DISTANCES, order, out)


def src_kernel(log_count, share, units, offsets, *refs):
    n = len(units)
    tables, (tgt_pots, src_pots, block), outs = refs[:n], refs[n : n + 3], refs[n + 3 : -2]
    order, wide = refs[-2:]
    depth, half = outs[0].shape[1], block.shape[0] // 2
    if log_count is None:
        tgt = tgt_pots[...]
    else:
        tgt = merge(tgt_pots, log_count, offsets[1], range(8), order)
        outs[-1][...] = tgt
        outs = outs[:-1]
    spread(src_pots[...], wide)
    for k, (unit, table) in enumerate(zip(units, tables)):
        at = slice(unit * 256, (unit + 1) * 256)
        weight = [
            jnp.exp2(table[:, t * LANES : (t + 1) * LANES] + wide[at, :] + tgt[t : t + 1, :])
            .astype(jnp.bfloat16)
            for t in range(8)
        ]
        first = jnp.concatenate(weight[:4], axis=1)
        second = jnp.concatenate(weight[4:], axis=1)
        pull = (dot(first, block[:half, :depth]) + dot(second, block[half:, :depth])) * share
        start = 0
        for out in outs[2 * k : 2 * k + 2 + len(outs) % 2]:
            out[...] = pull[start : start + out.shape[0]].astype(out.dtype)
            start += out.shape[0]


def tgt_kernel(share, *refs):
    tables, (tgt_pots, src_pots), blocks = refs[:4], refs[4:6], refs[6:10]
    keep, give, wide = refs[10:]
    spread(tgt_pots[...], wide)
    src = src_pots[...]
    for unit in (2, 3, 0, 1):
        at = slice(unit * 256, (unit + 1) * 256)
        pull = 0.0
        for k, (table, block) in enumerate(zip(tables, blocks)):
            weight = [
                jnp.exp2(table[at, t * LANES : (t + 1) * LANES] + src[2 * k + t : 2 * k + t + 1, :] + wide[at, :])
                .astype(jnp.bfloat16)
                for t in range(2)
            ]
            pull = pull + dot(jnp.concatenate(weight, axis=1), block[:, : keep.shape[1]])
        to = slice((unit % 2) * 256, (unit % 2 + 1) * 256)
        if unit < 2:
            keep[to, :] = pull * share
        else:
            give[to, :] = (pull * share).astype(give.dtype)


def add_cores_kernel(keep, taken, out, total, sems):
    rows = keep.shape[0] // sems.shape[0]
    copies = []
    for c in range(sems.shape[0]):
        at = slice(c * rows, (c + 1) * rows)
        total[at, :] = (keep[at, :] + taken[at, :].astype(jnp.float32)).astype(total.dtype)
        copies.append(pltpu.make_async_copy(total.at[at], out.at[at], sems.at[c]))
        copies[-1].start()
    for copy in copies:
        copy.wait()


def first_add_kernel(up, up_term, down, down_term, up_out, down_out):
    half = up.shape[0]
    up_out[:half, :] = (up_term[:half, :] + up[...].astype(jnp.float32)).astype(up_out.dtype)
    up_out[half:, :] = up_term[half:, :].astype(up_out.dtype)
    down_out[:half, :] = down_term[:half, :].astype(down_out.dtype)
    down_out[half:, :] = (down_term[half:, :] + down[...].astype(jnp.float32)).astype(down_out.dtype)


def add_kernel(up, up_term, down, down_term, up_out, down_out):
    for out, term, add in ((up_out, up_term, up), (down_out, down_term, down)):
        out[...] = (term[...] + add[...].astype(jnp.float32)).astype(out.dtype)


def shards(src_emb, tgt_emb, src_lang, tgt_lang):
    f32, bf16 = jnp.float32, jnp.bfloat16
    rows, depth = src_emb.shape
    columns = tgt_emb.shape[0]
    row, col = lax.axis_index(ROW), lax.axis_index(COL)
    ring, plane = lax.axis_size(RING), lax.axis_size(PLANE)
    spread_size = lax.axis_size(SPREAD)
    n_src, n_tgt = rows * ring, columns * spread_size
    place, core = lax.axis_index(RING), lax.axis_index("core")
    total_src = src_lang.shape[0] * lax.axis_size(ROW)
    total_tgt = tgt_lang.shape[0] * lax.axis_size(COL)
    offsets = jnp.stack([place, 4 * core, col, row]).astype(jnp.int32)

    n_label = depth + LANES
    dma = pltpu.SemaphoreType.DMA
    own, tgt = call(
        label_kernel,
        [jax.ShapeDtypeStruct((rows, n_label), bf16), jax.ShapeDtypeStruct((plane, columns, n_label), bf16)],
        [
            pltpu.VMEM((src_lang.shape[0] // LANES, LANES), jnp.int32),
            pltpu.VMEM((tgt_lang.shape[0] // LANES, LANES), jnp.int32),
            pltpu.VMEM((LANES, LANES), f32), pltpu.VMEM((columns, n_label), bf16), dma((plane,)),
        ],
        offsets, src_lang.reshape(-1, LANES), tgt_lang.reshape(-1, LANES), src_emb, tgt_emb,
        smem=1, in_hbm=range(1, 5), outs_in_hbm=(1,), flops=1, bytes_accessed=2**20,
    )
    mine = lax.all_to_all(tgt, PLANE, 0, 0)
    up, down = shift(own, 1), shift(own, -1)
    pairs = [(down, up)]
    up, down = shift(up, 1), shift(down, -1)
    mine, up, down = lax.optimization_barrier((mine, up, down))
    pairs.append((down, up))
    theirs = lax.ppermute(mine, "core", SWAP)
    mine, theirs = (v.reshape(plane * columns, -1) for v in (mine, theirs))
    up, down = shift(up, 1), shift(down, -1)

    order = pltpu.VMEM((8, LANES), f32)
    pots = jax.ShapeDtypeStruct((8, LANES), f32)
    to_ring = jax.ShapeDtypeStruct((ring, 8, LANES), f32)
    to_spread = jax.ShapeDtypeStruct((spread_size, 8, LANES), f32)
    pair = [
        jax.ShapeDtypeStruct((2 * rows, n_label), bf16),
        jax.ShapeDtypeStruct((2 * rows, n_tgt), f32),
        jax.ShapeDtypeStruct((n_tgt, 2 * rows), f32),
    ]
    pair_part = jax.ShapeDtypeStruct((2, LANES), f32)
    matmul = 2 * n_src * n_tgt * depth
    scale = LOG2E / (EPSILON * math.sqrt(depth))
    cost = dict(flops=matmul // 2, bytes_accessed=2**22)
    *first, tgt_block = call(
        functools.partial(first_pair_kernel, scale),
        [*pair, pair_part, jax.ShapeDtypeStruct((n_tgt, n_label), bf16)], [dma((4,))],
        *pairs[0], mine, theirs, in_hbm=range(3), **cost,
    )

    def pair_logits(near, other, in_hbm):
        return call(
            functools.partial(pair_kernel, scale),
            [*pair, pair_part], [dma((2,))],
            near, other, tgt_block, in_hbm=in_hbm, **cost,
        )

    made = [list(first), list(pair_logits(*pairs[1], range(2)))]
    made[0][3], made[1][3], up, down = lax.optimization_barrier((made[0][3], made[1][3], up, down))
    made.append(pair_logits(down, up, ()))
    half = rows // 2
    far = [jax.ShapeDtypeStruct((half, n_label), bf16)] * 2
    up, down = call(halves_kernel, far, [dma((2,))], up, down, flops=1, bytes_accessed=1)
    far = shift(up, 1), shift(down, -1)
    *last, part = call(
        functools.partial(last_pair_kernel, scale),
        [*pair, to_ring], [order, dma((3,))],
        offsets, own, *far, tgt_block, *(m[3] for m in made),
        smem=1, in_hbm=(1,), **cost,
    )
    made.append(last)
    src_blocks, logits, logits_t = ([m[k] for m in made] for k in range(3))
    wide_src = pltpu.VMEM((n_src, LANES), f32)
    wide_tgt = pltpu.VMEM((n_tgt, LANES), f32)
    for step in range(ITERS):
        gathered = lax.all_to_all(part, RING, 0, 0)
        part, src_pots = call(
            functools.partial(src_pots_kernel, math.log2(total_tgt)),
            [to_spread, pots], [order, wide_src],
            offsets, *logits, gathered, smem=1, flops=8 * n_src * n_tgt, bytes_accessed=2**22,
        )
        gathered = lax.all_to_all(part, SPREAD, 0, 0)
        if step < ITERS - 1:
            (part,) = call(
                functools.partial(tgt_pots_kernel, math.log2(total_src)),
                [to_ring], [order, wide_tgt],
                offsets, *logits_t, gathered, smem=1, flops=8 * n_src * n_tgt, bytes_accessed=2**22,
            )
    term = jax.ShapeDtypeStruct((rows, depth), f32)

    def src_terms(log_count, units, tgt_pots, kinds):
        return call(
            functools.partial(src_kernel, log_count, 1.0 / total_tgt, units),
            kinds, [order, wide_src],
            offsets, *(logits[u] for u in units), tgt_pots, src_pots, tgt_block,
            smem=1, flops=len(units) * matmul // 4, bytes_accessed=2**22,
        )

    low = jax.ShapeDtypeStruct((rows, depth), bf16)
    far = [jax.ShapeDtypeStruct((half, depth), bf16)] * 2
    own_term, up, down, tgt_pots = src_terms(math.log2(total_src), (3,), gathered, [term, *far, pots])
    up, down = shift(up, 1), shift(down, -1)
    terms = src_terms(None, (0, 1, 2), tgt_pots, [term] * 6)
    keep, give = call(
        functools.partial(tgt_kernel, 1.0 / total_src),
        [jax.ShapeDtypeStruct((n_tgt // 2, depth), f32), jax.ShapeDtypeStruct((n_tgt // 2, depth), bf16)],
        [wide_tgt],
        *logits_t, tgt_pots, src_pots, *src_blocks,
        flops=matmul, bytes_accessed=2**23,
    )
    taken = lax.ppermute(give, "core", SWAP)
    keep, taken, up, down, *terms = lax.optimization_barrier((keep, taken, up, down, *terms))
    shares = jax.ShapeDtypeStruct((n_tgt // 2, depth), bf16)
    (sent,) = call(
        add_cores_kernel, [shares], [pltpu.VMEM(shares.shape, bf16), dma((4,))],
        keep, taken, outs_in_hbm=(0,), flops=n_tgt * depth, bytes_accessed=2**22,
    )
    parts = lax.all_to_all(sent.reshape(plane, columns, depth), PLANE, 0, 0)
    for k in (2, 1, 0):
        up, down = call(
            first_add_kernel if k == 2 else add_kernel, [low] * 2, [],
            up, terms[2 * k], down, terms[2 * k + 1], flops=1, bytes_accessed=2**20,
        )
        if k == 0:
            parts, up, down = lax.optimization_barrier((parts, up, down))
        up, down = shift(up, 1), shift(down, -1)
    tgt_pull = jnp.sum(parts.astype(f32), axis=0)
    src_pull = own_term + up.astype(f32) + down.astype(f32)
    row_cost = jnp.sum(src_pull * src_emb.astype(f32), axis=1) * (-1.0 / math.sqrt(depth))
    return (src_pull, tgt_pull, row_cost)


def solution(mesh):
    split = Mesh(mesh.devices.reshape(SIZES), AXES)
    return jax.shard_map(
        shards,
        mesh=split,
        in_specs=(P(ROW + COL, None), P(COL + ROW, None), P(ROW), P(COL)),
        out_specs=(P(ROW + COL, None), P(COL + ROW, None), P(ROW + COL)),
        check_vma=False,
    )
```

time: 188 us -> 181 us (0.963)
  waiting for transfers between devices: 39.3 us -> 31 us
  Pallas kernels: 25.1 us -> 31.8 us
  local copies, waits for them, and re-layouts: 5.14 us -> 0.83 us
    pallas_call x12 -> x18, Pallas kernels: 25.1 us -> 31.8 us  [call(): pl.pallas_call(kernel, out_shape=outs, in_specs=specs, out_specs=[IN_HBM...]
    ppermute x16, waiting for transfers between devices: 36.3 us -> 31 us  [shift(): lax.ppermute(value, RING, [(i, (i + step) % size) for i in range(size)])]
    all_to_all x2, waiting for transfers between devices: 2.95 us -> 0.01 us  [the longest x1 0.01 us: shards(): mine = lax.all_to_all(tgt, PLANE, 0, 0)]
  transfers between devices with their start and end apart: 20 -> 20, of which waited for: 7 -> 9; matrix products, arithmetic and copies ran while one was open for 2% -> 1% of each run, Pallas kernels for 5% -> 6%
where the time goes in v4:
time: 181 us
  blocking collectives  70.8 us (39%)
  starting transfers between devices  41.9 us (23%)
  Pallas kernels  31.8 us (18%)
  waiting for transfers between devices  31 us (17%)
  other arithmetic  3.58 us (2%)
    all_to_all x3, blocking collectives, shards(): gathered = lax.all_to_all(part, SPREAD, 0, 0)  36.3 us
    all_to_all x3, blocking collectives, shards(): gathered = lax.all_to_all(part, RING, 0, 0)  34.4 us
    pallas_call x18, Pallas kernels, call(): pl.pallas_call(kernel, out_shape=outs, in_specs=specs, out_specs=[IN_HBM...  31.8 us
    ppermute x16, waiting for transfers between devices, shift(): lax.ppermute(value, RING, [(i, (i + step) % size) for i in range(size)])  31 us
    ppermute x16, starting transfers between devices, shift(): lax.ppermute(value, RING, [(i, (i + step) % size) for i in range(size)])  28.6 us
    all_to_all x1, starting transfers between devices, shards(): mine = lax.all_to_all(tgt, PLANE, 0, 0)  7.49 us
    all_to_all x1, starting transfers between devices, shards(): parts = lax.all_to_all(sent.reshape(plane, columns, depth), PLANE, 0, 0)  5.5 us
  transfers between devices with their start and end apart: 20, of which 9 were waited for; matrix products, arithmetic and copies ran while one was open for 1% of the time, Pallas kernels for 6%

profile of v4, /device:TPU:2, one launch (start us, length us, event | category | flops | bytes accessed | tf_op | source)
XLA Modules:
  0.0 180.8 jit_solution(3790724322260900563)
XLA Ops:
  0.7 3.5 %shard_map.67 = (bf16[128,1152]{1,0:T(8,128)(2,1)S(1)}, bf16[16,32,1152]{2,1,0:T(8,128)(2,1)}) custom-call(s32[4]{0:T(128)S(1)} %pad_add_fusion.offsets, s32[8,128]{1,0:T(8,128)} %bitcast.12, s32[8,128]{1,0:T(8,128)} %bitcast.13, bf16[128,1024]{1,0:T(8,128)(2,1)} %src.1, bf16[32,1024]{1,0:T(8,128)(2,1)} %tgt.1), custom_call_target="tpu_custom_call" | custom-call | flops 1 | bytes 1048576 | tf_op jit(solution)/shard_map/pallas_call | solution.py:48
  4.3 7.5 %all-to-all-start = ((bf16[16,32,1152]{2,1,0:T(8,128)(2,1)}), bf16[16,32,1152]{2,1,0:T(8,128)(2,1)S(1)}, u32[]{:S(2)}, u32[]{:S(2)}) async-start(bf16[16,32,1152]{2,1,0:T(8,128)(2,1)} %get-tuple-element.67), calls=%async_computation | async-start | bytes 2359296 | tf_op jit(solution)/shard_map/all_to_all | solution.py:321
  13.7 4.0 %collective-permute-start = (bf16[128,1152]{1,0:T(8,128)(2,1)S(1)}, bf16[128,1152]{1,0:T(8,128)(2,1)S(1)}, u32[]{:S(2)}, u32[]{:S(2)}) collective-permute-start(bf16[128,1152]{1,0:T(8,128)(2,1)S(1)} %get-tuple-element.66.own), channel_id=1, source_target_pairs={{0,52},{4,0},{16,4},{20,16},{32,20},{36,32},{48,36},{52,48},{1,53}... | collective-permute-start | bytes 884744 | tf_op jit(solution)/shard_map/ppermute | solution.py:63
  17.7 6.4 %collective-permute-done.1.other = bf16[128,1152]{1,0:T(8,128)(2,1)S(1)} collective-permute-done((bf16[128,1152]{1,0:T(8,128)(2,1)S(1)}, bf16[128,1152]{1,0:T(8,128)(2,1)S(1)}, u32[]{:S(2)}, u32[]{:S(2)}) %collective-permute-start.1) | collective-permute-done | bytes 294944 | tf_op jit(solution)/shard_map/ppermute | solution.py:63
  24.1 3.2 %collective-permute-start.3 = (bf16[128,1152]{1,0:T(8,128)(2,1)S(1)}, bf16[128,1152]{1,0:T(8,128)(2,1)S(1)}, u32[]{:S(2)}, u32[]{:S(2)}) collective-permute-start(bf16[128,1152]{1,0:T(8,128)(2,1)S(1)} %collective-permute-done.near), channel_id=1, source_target_pairs={{0,52},{4,0},{16,4},{20,16},{32,20},{36,32},{48,36},{52,48},{1,53}... | collective-permute-start | bytes 884744 | tf_op jit(solution)/shard_map/ppermute | solution.py:63
  27.3 5.5 %collective-permute-done.2.other = bf16[128,1152]{1,0:T(8,128)(2,1)S(1)} collective-permute-done((bf16[128,1152]{1,0:T(8,128)(2,1)S(1)}, bf16[128,1152]{1,0:T(8,128)(2,1)S(1)}, u32[]{:S(2)}, u32[]{:S(2)}) %collective-permute-start.2) | collective-permute-done | bytes 294944 | tf_op jit(solution)/shard_map/ppermute | solution.py:63
  33.0 3.0 %collective-permute-start.6 = (bf16[128,1152]{1,0:T(8,128)(2,1)S(1)}, bf16[128,1152]{1,0:T(8,128)(2,1)S(1)}, u32[]{:S(2)}, u32[]{:S(2)}) collective-permute-start(bf16[128,1152]{1,0:T(8,128)(2,1)S(1)} %collective-permute-done.3.near), channel_id=1, source_target_pairs={{0,52},{4,0},{16,4},{20,16},{32,20},{36,32},{48,36},{52,48},{1,53}... | collective-permute-start | bytes 884744 | tf_op jit(solution)/shard_map/ppermute | solution.py:63
  36.0 3.2 %shard_map.68 = (bf16[256,1152]{1,0:T(8,128)(2,1)S(1)}, f32[256,1024]{1,0:T(8,128)S(1)}, f32[1024,256]{1,0:T(8,128)S(1)}, f32[2,128]{1,0:T(2,128)S(1)}, bf16[1024,1152]{1,0:T(8,128)(2,1)S(1)}) custom-call(bf16[128,1152]{1,0:T(8,128)(2,1)} %copy-done.7, bf16[128,1152]{1,0:T(8,128)(2,1)} %copy-done.6, bf16[512,1152]{1,0:T(8,128)(2,1)} %bitcast.11, ...), custom_call_target="tpu_custom_call" | custom-call | flops 1073741824 | bytes 4194304 | tf_op jit(solution)/shard_map/pallas_call | solution.py:48
  39.3 2.8 %shard_map.69 = (bf16[256,1152]{1,0:T(8,128)(2,1)S(1)}, f32[256,1024]{1,0:T(8,128)S(1)}, f32[1024,256]{1,0:T(8,128)S(1)}, f32[2,128]{1,0:T(2,128)S(1)}) custom-call(bf16[128,1152]{1,0:T(8,128)(2,1)} %copy-done.8, bf16[128,1152]{1,0:T(8,128)(2,1)} %copy-done.5, bf16[1024,1152]{1,0:T(8,128)(2,1)S(1)} %get-tuple-element.72.tgt.refs_3_.refs_5_), custom_call_target="tpu_custom_call" | custom-call | flops 1073741824 | bytes 4194304 | tf_op jit(solution)/shard_map/pallas_call | solution.py:48
  42.8 3.4 %collective-permute-done.5.up.other = bf16[128,1152]{1,0:T(8,128)(2,1)S(1)} collective-permute-done((bf16[128,1152]{1,0:T(8,128)(2,1)S(1)}, bf16[128,1152]{1,0:T(8,128)(2,1)S(1)}, u32[]{:S(2)}, u32[]{:S(2)}) %collective-permute-start.5) | collective-permute-done | bytes 294944 | tf_op jit(solution)/shard_map/ppermute | solution.py:63
  46.7 3.2 %collective-permute-start.8 = (bf16[64,1152]{1,0:T(8,128)(2,1)S(1)}, bf16[64,1152]{1,0:T(8,128)(2,1)S(1)}, u32[]{:S(2)}, u32[]{:S(2)}) collective-permute-start(bf16[64,1152]{1,0:T(8,128)(2,1)S(1)} %get-tuple-element.77), channel_id=1, source_target_pairs={{0,52},{4,0},{16,4},{20,16},{32,20},{36,32},{48,36},{52,48},{1,53}... | collective-permute-start | bytes 442376 | tf_op jit(solution)/shard_map/ppermute | solution.py:63
  53.1 3.3 %shard_map.72 = (bf16[256,1152]{1,0:T(8,128)(2,1)S(1)}, f32[256,1024]{1,0:T(8,128)S(1)}, f32[1024,256]{1,0:T(8,128)S(1)}, f32[8,8,128]{2,1,0:T(8,128)S(1)}) custom-call(s32[4]{0:T(128)S(1)} %pad_add_fusion.offsets, bf16[128,1152]{1,0:T(8,128)(2,1)} %copy-done.2, bf16[64,1152]{1,0:T(8,128)(2,1)S(1)} %collective-permute-done.7.far_up, ...), custom_call_target="tpu_custom_call" | custom-call | flops 1073741824 | bytes 4194304 | tf_op jit(solution)/shard_map/pallas_call | solution.py:48
  56.3 13.7 %all_to_all.40.refs_4_ = f32[8,8,128]{2,1,0:T(8,128)S(1)} all-to-all(f32[8,8,128]{2,1,0:T(8,128)S(1)} %get-tuple-element.89), channel_id=1, replica_groups=mesh['x'=4,'zh'=4,'core'=2,'zl'=2,'y'=4] {'zh','zl'}, dimensions={0} | all-to-all | bytes 65536 | tf_op jit(solution)/shard_map/all_to_all | solution.py:375
  72.1 13.8 %all_to_all.41.refs_4_ = f32[32,8,128]{2,1,0:T(8,128)S(1)} all-to-all(f32[32,8,128]{2,1,0:T(8,128)S(1)} %get-tuple-element.90), channel_id=1, replica_groups=mesh['x'=4,'zh'=4,'core'=2,'zl'=2,'y'=4] {'x','y','core'}, dimensions={0} | all-to-all | bytes 262144 | tf_op jit(solution)/shard_map/all_to_all | solution.py:381
  87.5 10.4 %all_to_all.42.refs_4_ = f32[8,8,128]{2,1,0:T(8,128)S(1)} all-to-all(f32[8,8,128]{2,1,0:T(8,128)S(1)} %shard_map.74), channel_id=1, replica_groups=mesh['x'=4,'zh'=4,'core'=2,'zl'=2,'y'=4] {'zh','zl'}, dimensions={0} | all-to-all | bytes 65536 | tf_op jit(solution)/shard_map/all_to_all | solution.py:375
  100.0 11.3 %all_to_all.43.refs_4_ = f32[32,8,128]{2,1,0:T(8,128)S(1)} all-to-all(f32[32,8,128]{2,1,0:T(8,128)S(1)} %get-tuple-element.91), channel_id=1, replica_groups=mesh['x'=4,'zh'=4,'core'=2,'zl'=2,'y'=4] {'x','y','core'}, dimensions={0} | all-to-all | bytes 262144 | tf_op jit(solution)/shard_map/all_to_all | solution.py:381
  112.9 10.4 %all_to_all.44.refs_4_ = f32[8,8,128]{2,1,0:T(8,128)S(1)} all-to-all(f32[8,8,128]{2,1,0:T(8,128)S(1)} %shard_map.76), channel_id=1, replica_groups=mesh['x'=4,'zh'=4,'core'=2,'zl'=2,'y'=4] {'zh','zl'}, dimensions={0} | all-to-all | bytes 65536 | tf_op jit(solution)/shard_map/all_to_all | solution.py:375
  124.9 11.3 %all_to_all.45.refs_1_ = f32[32,8,128]{2,1,0:T(8,128)S(1)} all-to-all(f32[32,8,128]{2,1,0:T(8,128)S(1)} %get-tuple-element.92), channel_id=1, replica_groups=mesh['x'=4,'zh'=4,'core'=2,'zl'=2,'y'=4] {'x','y','core'}, dimensions={0} | all-to-all | bytes 262144 | tf_op jit(solution)/shard_map/all_to_all | solution.py:381
  149.2 5.5 %all-to-all-start.7 = ((bf16[16,32,1024]{2,1,0:T(8,128)(2,1)}), bf16[16,32,1024]{2,1,0:T(8,128)(2,1)}, u32[]{:S(2)}, u32[]{:S(2)}) async-start(bf16[16,32,1024]{2,1,0:T(8,128)(2,1)} %bitcast.10), calls=%async_computation.7 | async-start | bytes 2097152 | tf_op jit(solution)/shard_map/all_to_all | solution.py:417
  154.9 3.2 %collective-permute-start.13 = (bf16[128,1024]{1,0:T(8,128)(2,1)S(1)}, bf16[128,1024]{1,0:T(8,128)(2,1)S(1)}, u32[]{:S(2)}, u32[]{:S(2)}) collective-permute-start(bf16[128,1024]{1,0:T(8,128)(2,1)S(1)} %get-tuple-element.118), channel_id=1, source_target_pairs={{0,52},{4,0},{16,4},{20,16},{32,20},{36,32},{48,36},{52,48},{1,53}... | collective-permute-start | bytes 786440 | tf_op jit(solution)/shard_map/ppermute | solution.py:63
  158.1 5.5 %collective-permute-done.12.up = bf16[128,1024]{1,0:T(8,128)(2,1)S(1)} collective-permute-done((bf16[128,1024]{1,0:T(8,128)(2,1)S(1)}, bf16[128,1024]{1,0:T(8,128)(2,1)S(1)}, u32[]{:S(2)}, u32[]{:S(2)}) %collective-permute-start.12) | collective-permute-done | bytes 262176 | tf_op jit(solution)/shard_map/ppermute | solution.py:63
  163.7 3.2 %collective-permute-start.15 = (bf16[128,1024]{1,0:T(8,128)(2,1)S(1)}, bf16[128,1024]{1,0:T(8,128)(2,1)S(1)}, u32[]{:S(2)}, u32[]{:S(2)}) collective-permute-start(bf16[128,1024]{1,0:T(8,128)(2,1)S(1)} %get-tuple-element.122), channel_id=1, source_target_pairs={{0,52},{4,0},{16,4},{20,16},{32,20},{36,32},{48,36},{52,48},{1,53}... | collective-permute-start | bytes 786440 | tf_op jit(solution)/shard_map/ppermute | solution.py:63
  166.9 4.6 %collective-permute-done.14.up = bf16[128,1024]{1,0:T(8,128)(2,1)S(1)} collective-permute-done((bf16[128,1024]{1,0:T(8,128)(2,1)S(1)}, bf16[128,1024]{1,0:T(8,128)(2,1)S(1)}, u32[]{:S(2)}, u32[]{:S(2)}) %collective-permute-start.14) | collective-permute-done | bytes 262176 | tf_op jit(solution)/shard_map/ppermute | solution.py:63
  171.8 3.2 %collective-permute-start.17 = (bf16[128,1024]{1,0:T(8,128)(2,1)S(1)}, bf16[128,1024]{1,0:T(8,128)(2,1)S(1)}, u32[]{:S(2)}, u32[]{:S(2)}) collective-permute-start(bf16[128,1024]{1,0:T(8,128)(2,1)S(1)} %get-tuple-element.127), channel_id=1, source_target_pairs={{0,52},{4,0},{16,4},{20,16},{32,20},{36,32},{48,36},{52,48},{1,53}... | collective-permute-start | bytes 786440 | tf_op jit(solution)/shard_map/ppermute | solution.py:63
  (62 shorter events, 34.8 us)
Async XLA Ops:
  4.3 35.0 %copy-start.2 = (bf16[128,1152]{1,0:T(8,128)(2,1)}, bf16[128,1152]{1,0:T(8,128)(2,1)S(1)}, u32[]{:S(2)}) copy-start(bf16[128,1152]{1,0:T(8,128)(2,1)S(1)} %get-tuple-element.66.own) | copy-start | bytes 884740
  4.3 28.6 %all-to-all-start = ((bf16[16,32,1152]{2,1,0:T(8,128)(2,1)}), bf16[16,32,1152]{2,1,0:T(8,128)(2,1)S(1)}, u32[]{:S(2)}, u32[]{:S(2)}) async-start(bf16[16,32,1152]{2,1,0:T(8,128)(2,1)} %get-tuple-element.67), calls=%async_computation | async-start | bytes 2359296 | tf_op jit(solution)/shard_map/all_to_all | solution.py:321
  11.8 12.3 %collective-permute-start.1 = (bf16[128,1152]{1,0:T(8,128)(2,1)S(1)}, bf16[128,1152]{1,0:T(8,128)(2,1)S(1)}, u32[]{:S(2)}, u32[]{:S(2)}) collective-permute-start(bf16[128,1152]{1,0:T(8,128)(2,1)S(1)} %get-tuple-element.66.own), channel_id=1, source_target_pairs={{0,4},{4,16},{16,20},{20,32},{32,36},{36,48},{48,52},{52,0},{1,5},... | collective-permute-start | bytes 884744 | tf_op jit(solution)/shard_map/ppermute | solution.py:63
  13.7 10.4 %collective-permute-start = (bf16[128,1152]{1,0:T(8,128)(2,1)S(1)}, bf16[128,1152]{1,0:T(8,128)(2,1)S(1)}, u32[]{:S(2)}, u32[]{:S(2)}) collective-permute-start(bf16[128,1152]{1,0:T(8,128)(2,1)S(1)} %get-tuple-element.66.own), channel_id=1, source_target_pairs={{0,52},{4,0},{16,4},{20,16},{32,20},{36,32},{48,36},{52,48},{1,53}... | collective-permute-start | bytes 884744 | tf_op jit(solution)/shard_map/ppermute | solution.py:63
  24.1 11.9 %copy-start.6 = (bf16[128,1152]{1,0:T(8,128)(2,1)}, bf16[128,1152]{1,0:T(8,128)(2,1)S(1)}, u32[]{:S(2)}) copy-start(bf16[128,1152]{1,0:T(8,128)(2,1)S(1)} %collective-permute-done.1.other) | copy-start | bytes 884740
  24.1 8.8 %collective-permute-start.2 = (bf16[128,1152]{1,0:T(8,128)(2,1)S(1)}, bf16[128,1152]{1,0:T(8,128)(2,1)S(1)}, u32[]{:S(2)}, u32[]{:S(2)}) collective-permute-start(bf16[128,1152]{1,0:T(8,128)(2,1)S(1)} %collective-permute-done.1.other), channel_id=1, source_target_pairs={{0,4},{4,16},{16,20},{20,32},{32,36},{36,48},{48,52},{52,0},{1,5},... | collective-permute-start | bytes 884744 | tf_op jit(solution)/shard_map/ppermute | solution.py:63
  24.1 8.8 %collective-permute-start.3 = (bf16[128,1152]{1,0:T(8,128)(2,1)S(1)}, bf16[128,1152]{1,0:T(8,128)(2,1)S(1)}, u32[]{:S(2)}, u32[]{:S(2)}) collective-permute-start(bf16[128,1152]{1,0:T(8,128)(2,1)S(1)} %collective-permute-done.near), channel_id=1, source_target_pairs={{0,52},{4,0},{16,4},{20,16},{32,20},{36,32},{48,36},{52,48},{1,53}... | collective-permute-start | bytes 884744 | tf_op jit(solution)/shard_map/ppermute | solution.py:63
  32.9 3.1 %collective-permute-start.4 = (bf16[16,32,1152]{2,1,0:T(8,128)(2,1)S(1)}, bf16[16,32,1152]{2,1,0:T(8,128)(2,1)S(1)}, u32[]{:S(2)}, u32[]{:S(2)}) collective-permute-start(bf16[16,32,1152]{2,1,0:T(8,128)(2,1)S(1)} %all-to-all-done), channel_id=1, source_target_pairs={{0,8},{8,0},{1,9},{9,1},{2,10},{10,2},{3,11},{11,3},{4,12},{12,4},... | collective-permute-start | bytes 3538952 | tf_op jit(solution)/shard_map/ppermute | solution.py:327
  33.0 9.9 %collective-permute-start.6 = (bf16[128,1152]{1,0:T(8,128)(2,1)S(1)}, bf16[128,1152]{1,0:T(8,128)(2,1)S(1)}, u32[]{:S(2)}, u32[]{:S(2)}) collective-permute-start(bf16[128,1152]{1,0:T(8,128)(2,1)S(1)} %collective-permute-done.3.near), channel_id=1, source_target_pairs={{0,52},{4,0},{16,4},{20,16},{32,20},{36,32},{48,36},{52,48},{1,53}... | collective-permute-start | bytes 884744 | tf_op jit(solution)/shard_map/ppermute | solution.py:63
  36.0 10.3 %collective-permute-start.5 = (bf16[128,1152]{1,0:T(8,128)(2,1)S(1)}, bf16[128,1152]{1,0:T(8,128)(2,1)S(1)}, u32[]{:S(2)}, u32[]{:S(2)}) collective-permute-start(bf16[128,1152]{1,0:T(8,128)(2,1)S(1)} %collective-permute-done.2.other), channel_id=1, source_target_pairs={{0,4},{4,16},{16,20},{20,32},{32,36},{36,48},{48,52},{52,0},{1,5},... | collective-permute-start | bytes 884744 | tf_op jit(solution)/shard_map/ppermute | solution.py:63
  46.6 6.4 %collective-permute-start.7 = (bf16[64,1152]{1,0:T(8,128)(2,1)S(1)}, bf16[64,1152]{1,0:T(8,128)(2,1)S(1)}, u32[]{:S(2)}, u32[]{:S(2)}) collective-permute-start(bf16[64,1152]{1,0:T(8,128)(2,1)S(1)} %get-tuple-element.76), channel_id=1, source_target_pairs={{0,4},{4,16},{16,20},{20,32},{32,36},{36,48},{48,52},{52,0},{1,5},... | collective-permute-start | bytes 442376 | tf_op jit(solution)/shard_map/ppermute | solution.py:63
  46.7 6.3 %collective-permute-start.8 = (bf16[64,1152]{1,0:T(8,128)(2,1)S(1)}, bf16[64,1152]{1,0:T(8,128)(2,1)S(1)}, u32[]{:S(2)}, u32[]{:S(2)}) collective-permute-start(bf16[64,1152]{1,0:T(8,128)(2,1)S(1)} %get-tuple-element.77), channel_id=1, source_target_pairs={{0,52},{4,0},{16,4},{20,16},{32,20},{36,32},{48,36},{52,48},{1,53}... | collective-permute-start | bytes 442376 | tf_op jit(solution)/shard_map/ppermute | solution.py:63
  140.9 7.2 %collective-permute-start.9 = (bf16[512,1024]{1,0:T(8,128)(2,1)S(1)}, bf16[512,1024]{1,0:T(8,128)(2,1)S(1)}, u32[]{:S(2)}, u32[]{:S(2)}) collective-permute-start(bf16[512,1024]{1,0:T(8,128)(2,1)S(1)} %get-tuple-element.101), channel_id=1, source_target_pairs={{0,8},{8,0},{1,9},{9,1},{2,10},{10,2},{3,11},{11,3},{4,12},{12,4},... | collective-permute-start | bytes 3145736 | tf_op jit(solution)/shard_map/ppermute | solution.py:410
  141.1 7.0 %collective-permute-start.10 = (bf16[64,1024]{1,0:T(8,128)(2,1)S(1)}, bf16[64,1024]{1,0:T(8,128)(2,1)S(1)}, u32[]{:S(2)}, u32[]{:S(2)}) collective-permute-start(bf16[64,1024]{1,0:T(8,128)(2,1)S(1)} %get-tuple-element.102), channel_id=1, source_target_pairs={{0,4},{4,16},{16,20},{20,32},{32,36},{36,48},{48,52},{52,0},{1,5},... | collective-permute-start | bytes 393224 | tf_op jit(solution)/shard_map/ppermute | solution.py:63
  141.6 6.5 %collective-permute-start.11 = (bf16[64,1024]{1,0:T(8,128)(2,1)S(1)}, bf16[64,1024]{1,0:T(8,128)(2,1)S(1)}, u32[]{:S(2)}, u32[]{:S(2)}) collective-permute-start(bf16[64,1024]{1,0:T(8,128)(2,1)S(1)} %get-tuple-element.103), channel_id=1, source_target_pairs={{0,52},{4,0},{16,4},{20,16},{32,20},{36,32},{48,36},{52,48},{1,53}... | collective-permute-start | bytes 393224 | tf_op jit(solution)/shard_map/ppermute | solution.py:63
  149.2 22.5 %all-to-all-start.7 = ((bf16[16,32,1024]{2,1,0:T(8,128)(2,1)}), bf16[16,32,1024]{2,1,0:T(8,128)(2,1)}, u32[]{:S(2)}, u32[]{:S(2)}) async-start(bf16[16,32,1024]{2,1,0:T(8,128)(2,1)} %bitcast.10), calls=%async_computation.7 | async-start | bytes 2097152 | tf_op jit(solution)/shard_map/all_to_all | solution.py:417
  154.7 8.8 %collective-permute-start.12 = (bf16[128,1024]{1,0:T(8,128)(2,1)S(1)}, bf16[128,1024]{1,0:T(8,128)(2,1)S(1)}, u32[]{:S(2)}, u32[]{:S(2)}) collective-permute-start(bf16[128,1024]{1,0:T(8,128)(2,1)S(1)} %get-tuple-element.116), channel_id=1, source_target_pairs={{0,4},{4,16},{16,20},{20,32},{32,36},{36,48},{48,52},{52,0},{1,5},... | collective-permute-start | bytes 786440 | tf_op jit(solution)/shard_map/ppermute | solution.py:63
  154.8 24.5 %copy-start.1 = (f32[128,1024]{1,0:T(8,128)S(1)}, f32[128,1024]{1,0:T(8,128)}, u32[]{:S(2)}) copy-start(f32[128,1024]{1,0:T(8,128)} %copy-done) | copy-start | bytes 1572868
  154.8 24.5 %copy-start.4 = (bf16[128,1024]{1,0:T(8,128)(2,1)S(1)}, bf16[128,1024]{1,0:T(8,128)(2,1)}, u32[]{:S(2)}) copy-start(bf16[128,1024]{1,0:T(8,128)(2,1)} %src.1) | copy-start | bytes 786436
  154.9 8.7 %collective-permute-start.13 = (bf16[128,1024]{1,0:T(8,128)(2,1)S(1)}, bf16[128,1024]{1,0:T(8,128)(2,1)S(1)}, u32[]{:S(2)}, u32[]{:S(2)}) collective-permute-start(bf16[128,1024]{1,0:T(8,128)(2,1)S(1)} %get-tuple-element.118), channel_id=1, source_target_pairs={{0,52},{4,0},{16,4},{20,16},{32,20},{36,32},{48,36},{52,48},{1,53}... | collective-permute-start | bytes 786440 | tf_op jit(solution)/shard_map/ppermute | solution.py:63
  163.6 8.0 %collective-permute-start.14 = (bf16[128,1024]{1,0:T(8,128)(2,1)S(1)}, bf16[128,1024]{1,0:T(8,128)(2,1)S(1)}, u32[]{:S(2)}, u32[]{:S(2)}) collective-permute-start(bf16[128,1024]{1,0:T(8,128)(2,1)S(1)} %get-tuple-element.120), channel_id=1, source_target_pairs={{0,4},{4,16},{16,20},{20,32},{32,36},{36,48},{48,52},{52,0},{1,5},... | collective-permute-start | bytes 786440 | tf_op jit(solution)/shard_map/ppermute | solution.py:63
  163.7 7.9 %collective-permute-start.15 = (bf16[128,1024]{1,0:T(8,128)(2,1)S(1)}, bf16[128,1024]{1,0:T(8,128)(2,1)S(1)}, u32[]{:S(2)}, u32[]{:S(2)}) collective-permute-start(bf16[128,1024]{1,0:T(8,128)(2,1)S(1)} %get-tuple-element.122), channel_id=1, source_target_pairs={{0,52},{4,0},{16,4},{20,16},{32,20},{36,32},{48,36},{52,48},{1,53}... | collective-permute-start | bytes 786440 | tf_op jit(solution)/shard_map/ppermute | solution.py:63
  171.7 7.7 %collective-permute-start.16 = (bf16[128,1024]{1,0:T(8,128)(2,1)S(1)}, bf16[128,1024]{1,0:T(8,128)(2,1)S(1)}, u32[]{:S(2)}, u32[]{:S(2)}) collective-permute-start(bf16[128,1024]{1,0:T(8,128)(2,1)S(1)} %get-tuple-element.126), channel_id=1, source_target_pairs={{0,4},{4,16},{16,20},{20,32},{32,36},{36,48},{48,52},{52,0},{1,5},... | collective-permute-start | bytes 786440 | tf_op jit(solution)/shard_map/ppermute | solution.py:63
  171.8 7.6 %collective-permute-start.17 = (bf16[128,1024]{1,0:T(8,128)(2,1)S(1)}, bf16[128,1024]{1,0:T(8,128)(2,1)S(1)}, u32[]{:S(2)}, u32[]{:S(2)}) collective-permute-start(bf16[128,1024]{1,0:T(8,128)(2,1)S(1)} %get-tuple-element.127), channel_id=1, source_target_pairs={{0,52},{4,0},{16,4},{20,16},{32,20},{36,32},{48,36},{52,48},{1,53}... | collective-permute-start | bytes 786440 | tf_op jit(solution)/shard_map/ppermute | solution.py:63
  (5 other events, 28.7 us)

commit v5 on v4

--- a/solution.py
+++ b/solution.py
@@ -77,23 +77,39 @@
     return (labels == lanes).astype(dtype)
 
 
-def label_kernel(offsets, src_lang, tgt_lang, src, tgt, src_out, tgt_out, src_labels, tgt_labels, hot, one, sems):
+def label_kernel(offsets, src_lang, tgt_lang, src, tgt, src_out, tgt_out, src_labels, tgt_labels, hot, sems):
     columns, depth = tgt.shape
-    copy_all([(tgt_lang, tgt_labels), (tgt, one.at[:, :depth]), (src_lang, src_labels)], sems)
-    bulk = pltpu.make_async_copy(src, src_out.at[:, :depth], sems.at[0])
-    bulk.start()
+    copies = [
+        pltpu.make_async_copy(a, b, sems.at[k])
+        for k, (a, b) in enumerate(
+            [
+                (tgt_lang, tgt_labels),
+                (src_lang, src_labels),
+                (tgt, tgt_out.at[:, :depth]),
+                (src, src_out.at[:, :depth]),
+            ]
+        )
+    ]
+    for copy in copies:
+        copy.start()
+    copies[0].wait()
     here = offsets[3] * columns
     hot[...] = one_hot(tgt_labels[pl.ds(here // LANES, 1), :], jnp.float32)
-    one[:, depth:] = hot[pl.ds(pl.multiple_of(lax.rem(here, LANES), columns), columns), :].astype(one.dtype)
-    bulk.wait()
-    copies = [
-        pltpu.make_async_copy(one, tgt_out.at[k], sems.at[k]) for k in range(tgt_out.shape[0])
-    ]
-    for copy in copies:
-        copy.start()
+    tgt_out[:, depth:] = hot[pl.ds(pl.multiple_of(lax.rem(here, LANES), columns), columns), :].astype(tgt_out.dtype)
+    copies[1].wait()
     src_out[:, depth:] = one_hot(src_labels[pl.ds(offsets[2], 1), :], src_out.dtype)
-    for copy in copies:
-        copy.wait()
+    copies[2].wait()
+    copies[3].wait()
+
+
+def assemble_kernel(axis, offsets, *refs):
+    (*blocks, out, sems), n = refs, len(refs) - 2
+    rows = blocks[0].shape[0]
+    places = [lax.rem(offsets[axis] + k, n) * rows for k in range(n)]
+    copy_all(
+        [(block, out.at[pl.ds(pl.multiple_of(at, rows), rows)]) for block, at in zip(blocks, places)],
+        sems,
+    )
 
 
 def columns_sums(tables, added):
@@ -149,15 +165,14 @@
 
 def make_logits(scale, src, tgt, logits, logits_t):
     depth = src.shape[1] - LANES
-    half = tgt.shape[0] // 2
     emb, hot = src[:, :depth], src[:, depth:]
-    for side in range(2):
-        to = slice(side * half, (side + 1) * half)
-        tgt_emb, tgt_hot = tgt[to, :depth], tgt[to, depth:]
-        same = dot(tgt_hot, hot, CONTRACT_LAST) > 0.5
-        logits_t[to, :] = jnp.where(same, dot(tgt_emb, emb, CONTRACT_LAST) * scale, NEG)
-        same = dot(hot, tgt_hot, CONTRACT_LAST) > 0.5
-        logits[:, to] = jnp.where(same, dot(emb, tgt_emb, CONTRACT_LAST) * scale, NEG)
+    step = 256
+    for start in range(0, tgt.shape[0], step):
+        to = slice(start, start + step)
+        same = dot(tgt[to, depth:], hot, CONTRACT_LAST) > 0.5
+        value = jnp.where(same, dot(tgt[to, :depth], emb, CONTRACT_LAST) * scale, NEG)
+        logits_t[to, :] = value
+        logits[:, to] = value.T
 
 
 def first_pair_kernel(scale, near, other, mine, theirs, src, logits, logits_t, part, tgt, sems):
@@ -186,24 +201,23 @@
     part[...] = jnp.concatenate(columns_lse([logits_t], None))
 
 
-def last_pair_kernel(scale, offsets, own, far_up, far_down, tgt, *refs):
-    parts, (src, logits, logits_t, out, order, sems) = refs[:3], refs[3:]
-    rows, half = own.shape[0], far_up.shape[0]
-    copy_all(
-        [
-            (own, src.at[:rows]),
-            (far_up, src.at[rows : rows + half]),
-            (far_down, src.at[rows + half :]),
-        ],
-        sems,
-    )
+def own_kernel(scale, own, tgt, src, logits, logits_t, part, sems):
+    copy_all([(own, src)], sems)
     make_logits(scale, src, tgt, logits, logits_t)
-    parts = [part[r : r + 1, :] for part in parts for r in range(2)]
+    part[...] = jnp.concatenate(columns_lse([logits_t], None))
+
+
+def far_kernel(scale, offsets, far_up, far_down, tgt, *refs):
+    parts, (src, logits, logits_t, out, order, sems) = refs[:4], refs[4:]
+    half = far_up.shape[0]
+    copy_all([(far_up, src.at[:half]), (far_down, src.at[half:])], sems)
+    make_logits(scale, src, tgt, logits, logits_t)
+    parts = [part[r : r + 1, :] for part in parts for r in range(part.shape[0])]
     send_out(parts + columns_lse([logits_t], None), offsets[0], DISTANCES, order, out)
 
 
 def src_pots_kernel(log_count, offsets, *refs):
-    tables, (gathered, out, pots, order, wide) = refs[:4], refs[4:]
+    tables, (gathered, out, pots, order, wide) = refs[:5], refs[5:]
     local = merge(gathered, log_count, offsets[0], DISTANCES, order)
     pots[...] = local
     spread(local, wide)
@@ -211,14 +225,14 @@
 
 
 def tgt_pots_kernel(log_count, offsets, *refs):
-    tables, (gathered, out, order, wide) = refs[:4], refs[4:]
+    tables, (gathered, out, order, wide) = refs[:5], refs[5:]
     spread(merge(gathered, log_count, offsets[1], range(8), order), wide)
     parts = [part for table in tables for part in columns_lse([table], wide)]
     send_out(parts, offsets[0], DISTANCES, order, out)
 
 
-def src_kernel(log_count, share, units, offsets, *refs):
-    n = len(units)
+def src_kernel(log_count, share, pieces, offsets, *refs):
+    n = len(pieces)
     tables, (tgt_pots, src_pots, block), outs = refs[:n], refs[n : n + 3], refs[n + 3 : -2]
     order, wide = refs[-2:]
     depth, half = outs[0].shape[1], block.shape[0] // 2
@@ -229,37 +243,43 @@
         outs[-1][...] = tgt
         outs = outs[:-1]
     spread(src_pots[...], wide)
-    for k, (unit, table) in enumerate(zip(units, tables)):
-        at = slice(unit * 256, (unit + 1) * 256)
+    outs = list(outs)
+    for (first, rows, place), table in zip(pieces, tables):
+        at = slice(place, place + rows)
         weight = [
-            jnp.exp2(table[:, t * LANES : (t + 1) * LANES] + wide[at, :] + tgt[t : t + 1, :])
+            jnp.exp2(table[first : first + rows, t * LANES : (t + 1) * LANES] + wide[at, :] + tgt[t : t + 1, :])
             .astype(jnp.bfloat16)
             for t in range(8)
         ]
-        first = jnp.concatenate(weight[:4], axis=1)
-        second = jnp.concatenate(weight[4:], axis=1)
-        pull = (dot(first, block[:half, :depth]) + dot(second, block[half:, :depth])) * share
+        left = jnp.concatenate(weight[:4], axis=1)
+        right = jnp.concatenate(weight[4:], axis=1)
+        pull = (dot(left, block[:half, :depth]) + dot(right, block[half:, :depth])) * share
         start = 0
-        for out in outs[2 * k : 2 * k + 2 + len(outs) % 2]:
+        while start < rows:
+            out = outs.pop(0)
             out[...] = pull[start : start + out.shape[0]].astype(out.dtype)
             start += out.shape[0]
 
 
 def tgt_kernel(share, *refs):
-    tables, (tgt_pots, src_pots), blocks = refs[:4], refs[4:6], refs[6:10]
-    keep, give, wide = refs[10:]
+    tables, (tgt_pots, src_pots), blocks = refs[:5], refs[5:7], refs[7:12]
+    keep, give, wide = refs[12:]
     spread(tgt_pots[...], wide)
     src = src_pots[...]
+    depth = keep.shape[1]
     for unit in (2, 3, 0, 1):
         at = slice(unit * 256, (unit + 1) * 256)
+        weight, line = [], 0
+        for table in tables:
+            for t in range(table.shape[1] // LANES):
+                z = table[at, t * LANES : (t + 1) * LANES] + src[line : line + 1, :] + wide[at, :]
+                weight.append(jnp.exp2(z).astype(jnp.bfloat16))
+                line += 1
         pull = 0.0
-        for k, (table, block) in enumerate(zip(tables, blocks)):
-            weight = [
-                jnp.exp2(table[at, t * LANES : (t + 1) * LANES] + src[2 * k + t : 2 * k + t + 1, :] + wide[at, :])
-                .astype(jnp.bfloat16)
-                for t in range(2)
-            ]
-            pull = pull + dot(jnp.concatenate(weight, axis=1), block[:, : keep.shape[1]])
+        for k in range(3):
+            pull = pull + dot(jnp.concatenate(weight[2 * k : 2 * k + 2], axis=1), blocks[k][:, :depth])
+        last = jnp.concatenate([blocks[3][:, :depth], blocks[4][:, :depth]])
+        pull = pull + dot(jnp.concatenate(weight[6:], axis=1), last)
         to = slice((unit % 2) * 256, (unit % 2 + 1) * 256)
         if unit < 2:
             keep[to, :] = pull * share
@@ -303,30 +323,45 @@
     place, core = lax.axis_index(RING), lax.axis_index("core")
     total_src = src_lang.shape[0] * lax.axis_size(ROW)
     total_tgt = tgt_lang.shape[0] * lax.axis_size(COL)
-    offsets = jnp.stack([place, 4 * core, col, row]).astype(jnp.int32)
+    offsets = jnp.stack(
+        [place, 4 * core, col, row, lax.axis_index("x"), lax.axis_index("y")]
+    ).astype(jnp.int32)
 
     n_label = depth + LANES
     dma = pltpu.SemaphoreType.DMA
     own, tgt = call(
         label_kernel,
-        [jax.ShapeDtypeStruct((rows, n_label), bf16), jax.ShapeDtypeStruct((plane, columns, n_label), bf16)],
+        [jax.ShapeDtypeStruct((rows, n_label), bf16), jax.ShapeDtypeStruct((columns, n_label), bf16)],
         [
             pltpu.VMEM((src_lang.shape[0] // LANES, LANES), jnp.int32),
             pltpu.VMEM((tgt_lang.shape[0] // LANES, LANES), jnp.int32),
-            pltpu.VMEM((LANES, LANES), f32), pltpu.VMEM((columns, n_label), bf16), dma((plane,)),
+            pltpu.VMEM((LANES, LANES), f32), dma((4,)),
         ],
         offsets, src_lang.reshape(-1, LANES), tgt_lang.reshape(-1, LANES), src_emb, tgt_emb,
-        smem=1, in_hbm=range(1, 5), outs_in_hbm=(1,), flops=1, bytes_accessed=2**20,
-    )
-    mine = lax.all_to_all(tgt, PLANE, 0, 0)
+        smem=1, in_hbm=range(1, 5), flops=1, bytes_accessed=2**20,
+    )
+
+    def gather_axis(block, axis, at):
+        size = lax.axis_size(axis)
+        found = [
+            lax.ppermute(block, axis, [((i + k) % size, i) for i in range(size)]) for k in range(1, size)
+        ]
+        return call(
+            functools.partial(assemble_kernel, at),
+            [jax.ShapeDtypeStruct((size * block.shape[0], block.shape[1]), bf16)], [dma((size,))],
+            offsets, block, *found, smem=1, flops=1, bytes_accessed=2**20,
+        )[0]
+
     up, down = shift(own, 1), shift(own, -1)
     pairs = [(down, up)]
+    block = gather_axis(tgt, "y", 5)
+    block, up, down = lax.optimization_barrier((block, up, down))
+    up, down = shift(up, 1), shift(down, -1)
+    mine = gather_axis(block, "x", 4)
+    pairs.append((down, up))
     up, down = shift(up, 1), shift(down, -1)
     mine, up, down = lax.optimization_barrier((mine, up, down))
-    pairs.append((down, up))
     theirs = lax.ppermute(mine, "core", SWAP)
-    mine, theirs = (v.reshape(plane * columns, -1) for v in (mine, theirs))
-    up, down = shift(up, 1), shift(down, -1)
 
     order = pltpu.VMEM((8, LANES), f32)
     pots = jax.ShapeDtypeStruct((8, LANES), f32)
@@ -344,7 +379,7 @@
     *first, tgt_block = call(
         functools.partial(first_pair_kernel, scale),
         [*pair, pair_part, jax.ShapeDtypeStruct((n_tgt, n_label), bf16)], [dma((4,))],
-        *pairs[0], mine, theirs, in_hbm=range(3), **cost,
+        *pairs[0], mine, theirs, **cost,
     )
 
     def pair_logits(near, other, in_hbm):
@@ -354,18 +389,29 @@
             near, other, tgt_block, in_hbm=in_hbm, **cost,
         )
 
-    made = [list(first), list(pair_logits(*pairs[1], range(2)))]
-    made[0][3], made[1][3], up, down = lax.optimization_barrier((made[0][3], made[1][3], up, down))
+    made = [list(first), list(pair_logits(*pairs[1], ()))]
     made.append(pair_logits(down, up, ()))
     half = rows // 2
     far = [jax.ShapeDtypeStruct((half, n_label), bf16)] * 2
     up, down = call(halves_kernel, far, [dma((2,))], up, down, flops=1, bytes_accessed=1)
     far = shift(up, 1), shift(down, -1)
+    single = [
+        jax.ShapeDtypeStruct((rows, n_label), bf16),
+        jax.ShapeDtypeStruct((rows, n_tgt), f32),
+        jax.ShapeDtypeStruct((n_tgt, rows), f32),
+    ]
+    made.append(
+        call(
+            functools.partial(own_kernel, scale),
+            [*single, jax.ShapeDtypeStruct((1, LANES), f32)], [dma((1,))],
+            own, tgt_block, **cost,
+        )
+    )
     *last, part = call(
-        functools.partial(last_pair_kernel, scale),
-        [*pair, to_ring], [order, dma((3,))],
-        offsets, own, *far, tgt_block, *(m[3] for m in made),
-        smem=1, in_hbm=(1,), **cost,
+        functools.partial(far_kernel, scale),
+        [*single, to_ring], [order, dma((2,))],
+        offsets, *far, tgt_block, *(m[3] for m in made),
+        smem=1, **cost,
     )
     made.append(last)
     src_blocks, logits, logits_t = ([m[k] for m in made] for k in range(3))
@@ -387,19 +433,20 @@
             )
     term = jax.ShapeDtypeStruct((rows, depth), f32)
 
-    def src_terms(log_count, units, tgt_pots, kinds):
+    def src_terms(log_count, units, pieces, tgt_pots, kinds):
         return call(
-            functools.partial(src_kernel, log_count, 1.0 / total_tgt, units),
+            functools.partial(src_kernel, log_count, 1.0 / total_tgt, pieces),
             kinds, [order, wide_src],
             offsets, *(logits[u] for u in units), tgt_pots, src_pots, tgt_block,
-            smem=1, flops=len(units) * matmul // 4, bytes_accessed=2**22,
+            smem=1, flops=matmul // 4, bytes_accessed=2**22,
         )
 
     low = jax.ShapeDtypeStruct((rows, depth), bf16)
     far = [jax.ShapeDtypeStruct((half, depth), bf16)] * 2
-    own_term, up, down, tgt_pots = src_terms(math.log2(total_src), (3,), gathered, [term, *far, pots])
+    up, down, tgt_pots = src_terms(math.log2(total_src), (4,), [(0, rows, 7 * rows)], gathered, [*far, pots])
     up, down = shift(up, 1), shift(down, -1)
-    terms = src_terms(None, (0, 1, 2), tgt_pots, [term] * 6)
+    pieces = [(0, 2 * rows, 0), (0, 2 * rows, 2 * rows), (0, 2 * rows, 4 * rows), (0, rows, 6 * rows)]
+    *terms, own_term = src_terms(None, (0, 1, 2, 3), pieces, tgt_pots, [term] * 7)
     keep, give = call(
         functools.partial(tgt_kernel, 1.0 / total_src),
         [jax.ShapeDtypeStruct((n_tgt // 2, depth), f32), jax.ShapeDtypeStruct((n_tgt // 2, depth), bf16)],
@@ -408,7 +455,7 @@
         flops=matmul, bytes_accessed=2**23,
     )
     taken = lax.ppermute(give, "core", SWAP)
-    keep, taken, up, down, *terms = lax.optimization_barrier((keep, taken, up, down, *terms))
+    keep, taken, up, down, own_term, *terms = lax.optimization_barrier((keep, taken, up, down, own_term, *terms))
     shares = jax.ShapeDtypeStruct((n_tgt // 2, depth), bf16)
     (sent,) = call(
         add_cores_kernel, [shares], [pltpu.VMEM(shares.shape, bf16), dma((4,))],

time: 181 us -> 172 us (0.950)
  waiting for transfers between devices: 31 us -> 23.8 us
  Pallas kernels: 31.8 us -> 27.5 us
  starting transfers between devices: 41.9 us -> 45.4 us
    ppermute x16, waiting for transfers between devices: 31 us -> 14.2 us  [shift(): lax.ppermute(value, RING, [(i, (i + step) % size) for i in range(size)])]
    ppermute x0 -> x6, starting transfers between devices: none -> 10.6 us  [gather_axis(): lax.ppermute(block, axis, [((i + k) % size, i) for i in range(size)])]
    ppermute x0 -> x6, waiting for transfers between devices: none -> 9.59 us  [gather_axis(): lax.ppermute(block, axis, [((i + k) % size, i) for i in range(size)])]
    all_to_all x1 -> x0, starting transfers between devices: 7.49 us -> none  [shards(): mine = lax.all_to_all(tgt, PLANE, 0, 0)]
    pallas_call x18 -> x21, Pallas kernels: 31.8 us -> 27.5 us  [call(): pl.pallas_call(kernel, out_shape=outs, in_specs=specs, out_specs=[IN_HBM...]
  transfers between devices with their start and end apart: 20 -> 25, of which waited for: 9 -> 11; matrix products, arithmetic and copies ran while one was open for 1% -> 1% of each run, Pallas kernels for 6% -> 6%
where the time goes in v5:
time: 172 us; the launch traced here: 171 us
  blocking collectives  70.1 us (41%)
  starting transfers between devices  45.4 us (26%)
  Pallas kernels  27.5 us (16%)
  waiting for transfers between devices  23.8 us (14%)
  other arithmetic  3.51 us (2%)
    all_to_all x3, blocking collectives, shards(): gathered = lax.all_to_all(part, SPREAD, 0, 0)  35.7 us
    all_to_all x3, blocking collectives, shards(): gathered = lax.all_to_all(part, RING, 0, 0)  34.4 us
    ppermute x16, starting transfers between devices, shift(): lax.ppermute(value, RING, [(i, (i + step) % size) for i in range(size)])  29 us
    pallas_call x21, Pallas kernels, call(): pl.pallas_call(kernel, out_shape=outs, in_specs=specs, out_specs=[IN_HBM...  27.5 us
    ppermute x16, waiting for transfers between devices, shift(): lax.ppermute(value, RING, [(i, (i + step) % size) for i in range(size)])  14.2 us
    ppermute x6, starting transfers between devices, gather_axis(): lax.ppermute(block, axis, [((i + k) % size, i) for i in range(size)])  10.6 us
    ppermute x6, waiting for transfers between devices, gather_axis(): lax.ppermute(block, axis, [((i + k) % size, i) for i in range(size)])  9.59 us
    all_to_all x1, starting transfers between devices, shards(): parts = lax.all_to_all(sent.reshape(plane, columns, depth), PLANE, 0, 0)  5.55 us
  transfers between devices with their start and end apart: 25, of which 11 were waited for; matrix products, arithmetic and copies ran while one was open for 1% of the time, Pallas kernels for 6%

profile of v5, /device:TPU:2, one launch (start us, length us, event | category | flops | bytes accessed | tf_op | source)
XLA Modules:
  0.0 171.3 jit_solution(2054985477262217930)
XLA Ops:
  4.3 4.0 %collective-permute-start = (bf16[128,1152]{1,0:T(8,128)(2,1)S(1)}, bf16[128,1152]{1,0:T(8,128)(2,1)S(1)}, u32[]{:S(2)}, u32[]{:S(2)}) collective-permute-start(bf16[128,1152]{1,0:T(8,128)(2,1)S(1)} %get-tuple-element.70.own), channel_id=1, source_target_pairs={{0,52},{4,0},{16,4},{20,16},{32,20},{36,32},{48,36},{52,48},{1,53}... | collective-permute-start | bytes 884744 | tf_op jit(solution)/shard_map/ppermute | solution.py:63
  9.9 2.9 %collective-permute-start.3 = (bf16[32,1152]{1,0:T(8,128)(2,1)S(1)}, bf16[32,1152]{1,0:T(8,128)(2,1)S(1)}, u32[]{:S(2)}, u32[]{:S(2)}) collective-permute-start(bf16[32,1152]{1,0:T(8,128)(2,1)S(1)} %get-tuple-element.71.refs_0_), channel_id=1, source_target_pairs={{2,0},{3,1},{0,2},{1,3},{6,4},{7,5},{4,6},{5,7},{10,8},{11,9},{8,1... | collective-permute-start | bytes 221192 | tf_op jit(solution)/shard_map/ppermute | solution.py:347
  18.3 3.2 %collective-permute-start.10 = (bf16[128,1152]{1,0:T(8,128)(2,1)S(1)}, bf16[128,1152]{1,0:T(8,128)(2,1)S(1)}, u32[]{:S(2)}, u32[]{:S(2)}) collective-permute-start(bf16[128,1152]{1,0:T(8,128)(2,1)S(1)} %collective-permute-done.near), channel_id=1, source_target_pairs={{0,52},{4,0},{16,4},{20,16},{32,20},{36,32},{48,36},{52,48},{1,53}... | collective-permute-start | bytes 884744 | tf_op jit(solution)/shard_map/ppermute | solution.py:63
  24.1 2.2 %collective-permute-start.5 = (bf16[128,1152]{1,0:T(8,128)(2,1)S(1)}, bf16[128,1152]{1,0:T(8,128)(2,1)S(1)}, u32[]{:S(2)}, u32[]{:S(2)}) collective-permute-start(bf16[128,1152]{1,0:T(8,128)(2,1)S(1)} %shard_map.68.refs_0_), channel_id=1, source_target_pairs={{64,0},{128,64},{192,128},{0,192},{65,1},{129,65},{193,129},{1,193... | collective-permute-start | bytes 884744 | tf_op jit(solution)/shard_map/ppermute | solution.py:347
  26.9 3.2 %collective-permute-start.11 = (bf16[128,1152]{1,0:T(8,128)(2,1)S(1)}, bf16[128,1152]{1,0:T(8,128)(2,1)S(1)}, u32[]{:S(2)}, u32[]{:S(2)}) collective-permute-start(bf16[128,1152]{1,0:T(8,128)(2,1)S(1)} %collective-permute-done.10.near), channel_id=1, source_target_pairs={{0,52},{4,0},{16,4},{20,16},{32,20},{36,32},{48,36},{52,48},{1,53}... | collective-permute-start | bytes 884744 | tf_op jit(solution)/shard_map/ppermute | solution.py:63
  31.5 2.8 %collective-permute-done.6.refs_2_ = bf16[128,1152]{1,0:T(8,128)(2,1)S(1)} collective-permute-done((bf16[128,1152]{1,0:T(8,128)(2,1)S(1)}, bf16[128,1152]{1,0:T(8,128)(2,1)S(1)}, u32[]{:S(2)}, u32[]{:S(2)}) %collective-permute-start.6) | collective-permute-done | bytes 294944 | tf_op jit(solution)/shard_map/ppermute | solution.py:347
  34.3 2.4 %collective-permute-done.5.refs_1_ = bf16[128,1152]{1,0:T(8,128)(2,1)S(1)} collective-permute-done((bf16[128,1152]{1,0:T(8,128)(2,1)S(1)}, bf16[128,1152]{1,0:T(8,128)(2,1)S(1)}, u32[]{:S(2)}, u32[]{:S(2)}) %collective-permute-start.5) | collective-permute-done | bytes 294944 | tf_op jit(solution)/shard_map/ppermute | solution.py:347
  38.2 3.2 %collective-permute-start.14 = (bf16[64,1152]{1,0:T(8,128)(2,1)S(1)}, bf16[64,1152]{1,0:T(8,128)(2,1)S(1)}, u32[]{:S(2)}, u32[]{:S(2)}) collective-permute-start(bf16[64,1152]{1,0:T(8,128)(2,1)S(1)} %get-tuple-element.84), channel_id=1, source_target_pairs={{0,52},{4,0},{16,4},{20,16},{32,20},{36,32},{48,36},{52,48},{1,53}... | collective-permute-start | bytes 442376 | tf_op jit(solution)/shard_map/ppermute | solution.py:63
  48.4 13.6 %all_to_all.35.refs_5_ = f32[8,8,128]{2,1,0:T(8,128)S(1)} all-to-all(f32[8,8,128]{2,1,0:T(8,128)S(1)} %get-tuple-element.95), channel_id=1, replica_groups=mesh['x'=4,'zh'=4,'core'=2,'zl'=2,'y'=4] {'zh','zl'}, dimensions={0} | all-to-all | bytes 65536 | tf_op jit(solution)/shard_map/all_to_all | solution.py:421
  64.0 13.2 %all_to_all.36.refs_5_ = f32[32,8,128]{2,1,0:T(8,128)S(1)} all-to-all(f32[32,8,128]{2,1,0:T(8,128)S(1)} %get-tuple-element.96), channel_id=1, replica_groups=mesh['x'=4,'zh'=4,'core'=2,'zl'=2,'y'=4] {'x','y','core'}, dimensions={0} | all-to-all | bytes 262144 | tf_op jit(solution)/shard_map/all_to_all | solution.py:427
  78.9 10.4 %all_to_all.37.refs_5_ = f32[8,8,128]{2,1,0:T(8,128)S(1)} all-to-all(f32[8,8,128]{2,1,0:T(8,128)S(1)} %shard_map.77), channel_id=1, replica_groups=mesh['x'=4,'zh'=4,'core'=2,'zl'=2,'y'=4] {'zh','zl'}, dimensions={0} | all-to-all | bytes 65536 | tf_op jit(solution)/shard_map/all_to_all | solution.py:421
  91.3 11.3 %all_to_all.38.refs_5_ = f32[32,8,128]{2,1,0:T(8,128)S(1)} all-to-all(f32[32,8,128]{2,1,0:T(8,128)S(1)} %get-tuple-element.97), channel_id=1, replica_groups=mesh['x'=4,'zh'=4,'core'=2,'zl'=2,'y'=4] {'x','y','core'}, dimensions={0} | all-to-all | bytes 262144 | tf_op jit(solution)/shard_map/all_to_all | solution.py:427
  104.2 10.4 %all_to_all.39.refs_5_ = f32[8,8,128]{2,1,0:T(8,128)S(1)} all-to-all(f32[8,8,128]{2,1,0:T(8,128)S(1)} %shard_map.79), channel_id=1, replica_groups=mesh['x'=4,'zh'=4,'core'=2,'zl'=2,'y'=4] {'zh','zl'}, dimensions={0} | all-to-all | bytes 65536 | tf_op jit(solution)/shard_map/all_to_all | solution.py:421
  116.2 11.3 %all_to_all.40.refs_1_ = f32[32,8,128]{2,1,0:T(8,128)S(1)} all-to-all(f32[32,8,128]{2,1,0:T(8,128)S(1)} %get-tuple-element.98), channel_id=1, replica_groups=mesh['x'=4,'zh'=4,'core'=2,'zl'=2,'y'=4] {'x','y','core'}, dimensions={0} | all-to-all | bytes 262144 | tf_op jit(solution)/shard_map/all_to_all | solution.py:427
  128.7 2.5 %shard_map.82 = (f32[512,1024]{1,0:T(8,128)S(1)}, bf16[512,1024]{1,0:T(8,128)(2,1)S(1)}) custom-call(f32[1024,256]{1,0:T(8,128)S(1)} %get-tuple-element.76.refs_0_, f32[1024,256]{1,0:T(8,128)S(1)} %get-tuple-element.78.refs_1_, f32[1024,256]{1,0:T(8,128)S(1)} %get-tuple-element.81.refs_2_, f32[1024,128]{1,0:T(8,128)S(1)} %get-tuple-element.82.refs_3_, ...), custom_call_target="tpu_custom_call" | custom-call | flops 2147483648 | bytes 8388608 | tf_op jit(solution)/shard_map/pallas_call | solution.py:48
  131.9 2.7 %collective-permute-start.17 = (bf16[64,1024]{1,0:T(8,128)(2,1)S(1)}, bf16[64,1024]{1,0:T(8,128)(2,1)S(1)}, u32[]{:S(2)}, u32[]{:S(2)}) collective-permute-start(bf16[64,1024]{1,0:T(8,128)(2,1)S(1)} %get-tuple-element.109), channel_id=1, source_target_pairs={{0,52},{4,0},{16,4},{20,16},{32,20},{36,32},{48,36},{52,48},{1,53}... | collective-permute-start | bytes 393224 | tf_op jit(solution)/shard_map/ppermute | solution.py:63
  134.6 2.8 %shard_map.83 = (f32[128,1024]{1,0:T(8,128)S(1)}, f32[128,1024]{1,0:T(8,128)S(1)}, f32[128,1024]{1,0:T(8,128)S(1)}, f32[128,1024]{1,0:T(8,128)S(1)}, f32[128,102...) custom-call(s32[6]{0:T(128)S(1)} %stack.27.offsets, f32[256,1024]{1,0:T(8,128)S(1)} %get-tuple-element.91.refs_0_, ...), custom_call_target="tpu_custom_call" | custom-call | flops 536870912 | bytes 4194304 | tf_op jit(solution)/shard_map/pallas_call | solution.py:48
  139.5 5.5 %all-to-all-start.6 = ((bf16[16,32,1024]{2,1,0:T(8,128)(2,1)}), bf16[16,32,1024]{2,1,0:T(8,128)(2,1)}, u32[]{:S(2)}, u32[]{:S(2)}) async-start(bf16[16,32,1024]{2,1,0:T(8,128)(2,1)} %bitcast.9), calls=%async_computation.6 | async-start | bytes 2097152 | tf_op jit(solution)/shard_map/all_to_all | solution.py:464
  145.2 3.2 %collective-permute-start.19 = (bf16[128,1024]{1,0:T(8,128)(2,1)S(1)}, bf16[128,1024]{1,0:T(8,128)(2,1)S(1)}, u32[]{:S(2)}, u32[]{:S(2)}) collective-permute-start(bf16[128,1024]{1,0:T(8,128)(2,1)S(1)} %get-tuple-element.126), channel_id=1, source_target_pairs={{0,52},{4,0},{16,4},{20,16},{32,20},{36,32},{48,36},{52,48},{1,53}... | collective-permute-start | bytes 786440 | tf_op jit(solution)/shard_map/ppermute | solution.py:63
  148.4 5.5 %collective-permute-done.18.up = bf16[128,1024]{1,0:T(8,128)(2,1)S(1)} collective-permute-done((bf16[128,1024]{1,0:T(8,128)(2,1)S(1)}, bf16[128,1024]{1,0:T(8,128)(2,1)S(1)}, u32[]{:S(2)}, u32[]{:S(2)}) %collective-permute-start.18) | collective-permute-done | bytes 262176 | tf_op jit(solution)/shard_map/ppermute | solution.py:63
  154.1 3.2 %collective-permute-start.21 = (bf16[128,1024]{1,0:T(8,128)(2,1)S(1)}, bf16[128,1024]{1,0:T(8,128)(2,1)S(1)}, u32[]{:S(2)}, u32[]{:S(2)}) collective-permute-start(bf16[128,1024]{1,0:T(8,128)(2,1)S(1)} %get-tuple-element.130), channel_id=1, source_target_pairs={{0,52},{4,0},{16,4},{20,16},{32,20},{36,32},{48,36},{52,48},{1,53}... | collective-permute-start | bytes 786440 | tf_op jit(solution)/shard_map/ppermute | solution.py:63
  157.4 4.7 %collective-permute-done.20.up = bf16[128,1024]{1,0:T(8,128)(2,1)S(1)} collective-permute-done((bf16[128,1024]{1,0:T(8,128)(2,1)S(1)}, bf16[128,1024]{1,0:T(8,128)(2,1)S(1)}, u32[]{:S(2)}, u32[]{:S(2)}) %collective-permute-start.20) | collective-permute-done | bytes 262176 | tf_op jit(solution)/shard_map/ppermute | solution.py:63
  162.3 3.2 %collective-permute-start.23 = (bf16[128,1024]{1,0:T(8,128)(2,1)S(1)}, bf16[128,1024]{1,0:T(8,128)(2,1)S(1)}, u32[]{:S(2)}, u32[]{:S(2)}) collective-permute-start(bf16[128,1024]{1,0:T(8,128)(2,1)S(1)} %get-tuple-element.135), channel_id=1, source_target_pairs={{0,52},{4,0},{16,4},{20,16},{32,20},{36,32},{48,36},{52,48},{1,53}... | collective-permute-start | bytes 786440 | tf_op jit(solution)/shard_map/ppermute | solution.py:63
  167.6 2.3 %collective-permute-done.22 = bf16[128,1024]{1,0:T(8,128)(2,1)S(1)} collective-permute-done((bf16[128,1024]{1,0:T(8,128)(2,1)S(1)}, bf16[128,1024]{1,0:T(8,128)(2,1)S(1)}, u32[]{:S(2)}, u32[]{:S(2)}) %collective-permute-start.22) | collective-permute-done | bytes 262176 | tf_op jit(solution)/shard_map/ppermute | solution.py:63
  (63 shorter events, 40.7 us)
Async XLA Ops:
  2.3 15.8 %collective-permute-start.1 = (bf16[128,1152]{1,0:T(8,128)(2,1)S(1)}, bf16[128,1152]{1,0:T(8,128)(2,1)S(1)}, u32[]{:S(2)}, u32[]{:S(2)}) collective-permute-start(bf16[128,1152]{1,0:T(8,128)(2,1)S(1)} %get-tuple-element.70.own), channel_id=1, source_target_pairs={{0,4},{4,16},{16,20},{20,32},{32,36},{36,48},{48,52},{52,0},{1,5},... | collective-permute-start | bytes 884744 | tf_op jit(solution)/shard_map/ppermute | solution.py:63
  4.3 13.9 %collective-permute-start = (bf16[128,1152]{1,0:T(8,128)(2,1)S(1)}, bf16[128,1152]{1,0:T(8,128)(2,1)S(1)}, u32[]{:S(2)}, u32[]{:S(2)}) collective-permute-start(bf16[128,1152]{1,0:T(8,128)(2,1)S(1)} %get-tuple-element.70.own), channel_id=1, source_target_pairs={{0,52},{4,0},{16,4},{20,16},{32,20},{36,32},{48,36},{52,48},{1,53}... | collective-permute-start | bytes 884744 | tf_op jit(solution)/shard_map/ppermute | solution.py:63
  8.4 6.4 %collective-permute-start.4 = (bf16[32,1152]{1,0:T(8,128)(2,1)S(1)}, bf16[32,1152]{1,0:T(8,128)(2,1)S(1)}, u32[]{:S(2)}, u32[]{:S(2)}) collective-permute-start(bf16[32,1152]{1,0:T(8,128)(2,1)S(1)} %get-tuple-element.71.refs_0_), channel_id=1, source_target_pairs={{3,0},{0,1},{1,2},{2,3},{7,4},{4,5},{5,6},{6,7},{11,8},{8,9},{9,10... | collective-permute-start | bytes 221192 | tf_op jit(solution)/shard_map/ppermute | solution.py:347
  9.9 6.2 %collective-permute-start.3 = (bf16[32,1152]{1,0:T(8,128)(2,1)S(1)}, bf16[32,1152]{1,0:T(8,128)(2,1)S(1)}, u32[]{:S(2)}, u32[]{:S(2)}) collective-permute-start(bf16[32,1152]{1,0:T(8,128)(2,1)S(1)} %get-tuple-element.71.refs_0_), channel_id=1, source_target_pairs={{2,0},{3,1},{0,2},{1,3},{6,4},{7,5},{4,6},{5,7},{10,8},{11,9},{8,1... | collective-permute-start | bytes 221192 | tf_op jit(solution)/shard_map/ppermute | solution.py:347
  12.8 4.4 %collective-permute-start.2 = (bf16[32,1152]{1,0:T(8,128)(2,1)S(1)}, bf16[32,1152]{1,0:T(8,128)(2,1)S(1)}, u32[]{:S(2)}, u32[]{:S(2)}) collective-permute-start(bf16[32,1152]{1,0:T(8,128)(2,1)S(1)} %get-tuple-element.71.refs_0_), channel_id=1, source_target_pairs={{1,0},{2,1},{3,2},{0,3},{5,4},{6,5},{7,6},{4,7},{9,8},{10,9},{11,1... | collective-permute-start | bytes 221192 | tf_op jit(solution)/shard_map/ppermute | solution.py:347
  18.2 8.7 %collective-permute-start.8 = (bf16[128,1152]{1,0:T(8,128)(2,1)S(1)}, bf16[128,1152]{1,0:T(8,128)(2,1)S(1)}, u32[]{:S(2)}, u32[]{:S(2)}) collective-permute-start(bf16[128,1152]{1,0:T(8,128)(2,1)S(1)} %collective-permute-done.1.other), channel_id=1, source_target_pairs={{0,4},{4,16},{16,20},{20,32},{32,36},{36,48},{48,52},{52,0},{1,5},... | collective-permute-start | bytes 884744 | tf_op jit(solution)/shard_map/ppermute | solution.py:63
  18.3 8.6 %collective-permute-start.10 = (bf16[128,1152]{1,0:T(8,128)(2,1)S(1)}, bf16[128,1152]{1,0:T(8,128)(2,1)S(1)}, u32[]{:S(2)}, u32[]{:S(2)}) collective-permute-start(bf16[128,1152]{1,0:T(8,128)(2,1)S(1)} %collective-permute-done.near), channel_id=1, source_target_pairs={{0,52},{4,0},{16,4},{20,16},{32,20},{36,32},{48,36},{52,48},{1,53}... | collective-permute-start | bytes 884744 | tf_op jit(solution)/shard_map/ppermute | solution.py:63
  21.5 9.9 %collective-permute-start.7 = (bf16[128,1152]{1,0:T(8,128)(2,1)S(1)}, bf16[128,1152]{1,0:T(8,128)(2,1)S(1)}, u32[]{:S(2)}, u32[]{:S(2)}) collective-permute-start(bf16[128,1152]{1,0:T(8,128)(2,1)S(1)} %shard_map.68.refs_0_), channel_id=1, source_target_pairs={{192,0},{0,64},{64,128},{128,192},{193,1},{1,65},{65,129},{129,193... | collective-permute-start | bytes 884744 | tf_op jit(solution)/shard_map/ppermute | solution.py:347
  23.0 11.3 %collective-permute-start.6 = (bf16[128,1152]{1,0:T(8,128)(2,1)S(1)}, bf16[128,1152]{1,0:T(8,128)(2,1)S(1)}, u32[]{:S(2)}, u32[]{:S(2)}) collective-permute-start(bf16[128,1152]{1,0:T(8,128)(2,1)S(1)} %shard_map.68.refs_0_), channel_id=1, source_target_pairs={{128,0},{192,64},{0,128},{64,192},{129,1},{193,65},{1,129},{65,193... | collective-permute-start | bytes 884744 | tf_op jit(solution)/shard_map/ppermute | solution.py:347
  24.1 12.6 %collective-permute-start.5 = (bf16[128,1152]{1,0:T(8,128)(2,1)S(1)}, bf16[128,1152]{1,0:T(8,128)(2,1)S(1)}, u32[]{:S(2)}, u32[]{:S(2)}) collective-permute-start(bf16[128,1152]{1,0:T(8,128)(2,1)S(1)} %shard_map.68.refs_0_), channel_id=1, source_target_pairs={{64,0},{128,64},{192,128},{0,192},{65,1},{129,65},{193,129},{1,193... | collective-permute-start | bytes 884744 | tf_op jit(solution)/shard_map/ppermute | solution.py:347
  26.9 10.7 %collective-permute-start.9 = (bf16[128,1152]{1,0:T(8,128)(2,1)S(1)}, bf16[128,1152]{1,0:T(8,128)(2,1)S(1)}, u32[]{:S(2)}, u32[]{:S(2)}) collective-permute-start(bf16[128,1152]{1,0:T(8,128)(2,1)S(1)} %collective-permute-done.8.other), channel_id=1, source_target_pairs={{0,4},{4,16},{16,20},{20,32},{32,36},{36,48},{48,52},{52,0},{1,5},... | collective-permute-start | bytes 884744 | tf_op jit(solution)/shard_map/ppermute | solution.py:63
  26.9 10.7 %collective-permute-start.11 = (bf16[128,1152]{1,0:T(8,128)(2,1)S(1)}, bf16[128,1152]{1,0:T(8,128)(2,1)S(1)}, u32[]{:S(2)}, u32[]{:S(2)}) collective-permute-start(bf16[128,1152]{1,0:T(8,128)(2,1)S(1)} %collective-permute-done.10.near), channel_id=1, source_target_pairs={{0,52},{4,0},{16,4},{20,16},{32,20},{36,32},{48,36},{52,48},{1,53}... | collective-permute-start | bytes 884744 | tf_op jit(solution)/shard_map/ppermute | solution.py:63
  38.1 8.4 %collective-permute-start.13 = (bf16[64,1152]{1,0:T(8,128)(2,1)S(1)}, bf16[64,1152]{1,0:T(8,128)(2,1)S(1)}, u32[]{:S(2)}, u32[]{:S(2)}) collective-permute-start(bf16[64,1152]{1,0:T(8,128)(2,1)S(1)} %get-tuple-element.83), channel_id=1, source_target_pairs={{0,4},{4,16},{16,20},{20,32},{32,36},{36,48},{48,52},{52,0},{1,5},... | collective-permute-start | bytes 442376 | tf_op jit(solution)/shard_map/ppermute | solution.py:63
  38.2 8.3 %collective-permute-start.14 = (bf16[64,1152]{1,0:T(8,128)(2,1)S(1)}, bf16[64,1152]{1,0:T(8,128)(2,1)S(1)}, u32[]{:S(2)}, u32[]{:S(2)}) collective-permute-start(bf16[64,1152]{1,0:T(8,128)(2,1)S(1)} %get-tuple-element.84), channel_id=1, source_target_pairs={{0,52},{4,0},{16,4},{20,16},{32,20},{36,32},{48,36},{52,48},{1,53}... | collective-permute-start | bytes 442376 | tf_op jit(solution)/shard_map/ppermute | solution.py:63
  131.1 7.2 %collective-permute-start.15 = (bf16[512,1024]{1,0:T(8,128)(2,1)S(1)}, bf16[512,1024]{1,0:T(8,128)(2,1)S(1)}, u32[]{:S(2)}, u32[]{:S(2)}) collective-permute-start(bf16[512,1024]{1,0:T(8,128)(2,1)S(1)} %get-tuple-element.107), channel_id=1, source_target_pairs={{0,8},{8,0},{1,9},{9,1},{2,10},{10,2},{3,11},{11,3},{4,12},{12,4},... | collective-permute-start | bytes 3145736 | tf_op jit(solution)/shard_map/ppermute | solution.py:457
  131.3 7.0 %collective-permute-start.16 = (bf16[64,1024]{1,0:T(8,128)(2,1)S(1)}, bf16[64,1024]{1,0:T(8,128)(2,1)S(1)}, u32[]{:S(2)}, u32[]{:S(2)}) collective-permute-start(bf16[64,1024]{1,0:T(8,128)(2,1)S(1)} %get-tuple-element.108), channel_id=1, source_target_pairs={{0,4},{4,16},{16,20},{20,32},{32,36},{36,48},{48,52},{52,0},{1,5},... | collective-permute-start | bytes 393224 | tf_op jit(solution)/shard_map/ppermute | solution.py:63
  131.9 6.5 %collective-permute-start.17 = (bf16[64,1024]{1,0:T(8,128)(2,1)S(1)}, bf16[64,1024]{1,0:T(8,128)(2,1)S(1)}, u32[]{:S(2)}, u32[]{:S(2)}) collective-permute-start(bf16[64,1024]{1,0:T(8,128)(2,1)S(1)} %get-tuple-element.109), channel_id=1, source_target_pairs={{0,52},{4,0},{16,4},{20,16},{32,20},{36,32},{48,36},{52,48},{1,53}... | collective-permute-start | bytes 393224 | tf_op jit(solution)/shard_map/ppermute | solution.py:63
  139.5 22.7 %all-to-all-start.6 = ((bf16[16,32,1024]{2,1,0:T(8,128)(2,1)}), bf16[16,32,1024]{2,1,0:T(8,128)(2,1)}, u32[]{:S(2)}, u32[]{:S(2)}) async-start(bf16[16,32,1024]{2,1,0:T(8,128)(2,1)} %bitcast.9), calls=%async_computation.6 | async-start | bytes 2097152 | tf_op jit(solution)/shard_map/all_to_all | solution.py:464
  145.1 8.9 %collective-permute-start.18 = (bf16[128,1024]{1,0:T(8,128)(2,1)S(1)}, bf16[128,1024]{1,0:T(8,128)(2,1)S(1)}, u32[]{:S(2)}, u32[]{:S(2)}) collective-permute-start(bf16[128,1024]{1,0:T(8,128)(2,1)S(1)} %get-tuple-element.124), channel_id=1, source_target_pairs={{0,4},{4,16},{16,20},{20,32},{32,36},{36,48},{48,52},{52,0},{1,5},... | collective-permute-start | bytes 786440 | tf_op jit(solution)/shard_map/ppermute | solution.py:63
  145.2 8.7 %collective-permute-start.19 = (bf16[128,1024]{1,0:T(8,128)(2,1)S(1)}, bf16[128,1024]{1,0:T(8,128)(2,1)S(1)}, u32[]{:S(2)}, u32[]{:S(2)}) collective-permute-start(bf16[128,1024]{1,0:T(8,128)(2,1)S(1)} %get-tuple-element.126), channel_id=1, source_target_pairs={{0,52},{4,0},{16,4},{20,16},{32,20},{36,32},{48,36},{52,48},{1,53}... | collective-permute-start | bytes 786440 | tf_op jit(solution)/shard_map/ppermute | solution.py:63
  154.0 8.0 %collective-permute-start.20 = (bf16[128,1024]{1,0:T(8,128)(2,1)S(1)}, bf16[128,1024]{1,0:T(8,128)(2,1)S(1)}, u32[]{:S(2)}, u32[]{:S(2)}) collective-permute-start(bf16[128,1024]{1,0:T(8,128)(2,1)S(1)} %get-tuple-element.128), channel_id=1, source_target_pairs={{0,4},{4,16},{16,20},{20,32},{32,36},{36,48},{48,52},{52,0},{1,5},... | collective-permute-start | bytes 786440 | tf_op jit(solution)/shard_map/ppermute | solution.py:63
  154.1 8.0 %collective-permute-start.21 = (bf16[128,1024]{1,0:T(8,128)(2,1)S(1)}, bf16[128,1024]{1,0:T(8,128)(2,1)S(1)}, u32[]{:S(2)}, u32[]{:S(2)}) collective-permute-start(bf16[128,1024]{1,0:T(8,128)(2,1)S(1)} %get-tuple-element.130), channel_id=1, source_target_pairs={{0,52},{4,0},{16,4},{20,16},{32,20},{36,32},{48,36},{52,48},{1,53}... | collective-permute-start | bytes 786440 | tf_op jit(solution)/shard_map/ppermute | solution.py:63
  162.2 7.7 %collective-permute-start.22 = (bf16[128,1024]{1,0:T(8,128)(2,1)S(1)}, bf16[128,1024]{1,0:T(8,128)(2,1)S(1)}, u32[]{:S(2)}, u32[]{:S(2)}) collective-permute-start(bf16[128,1024]{1,0:T(8,128)(2,1)S(1)} %get-tuple-element.134), channel_id=1, source_target_pairs={{0,4},{4,16},{16,20},{20,32},{32,36},{36,48},{48,52},{52,0},{1,5},... | collective-permute-start | bytes 786440 | tf_op jit(solution)/shard_map/ppermute | solution.py:63
  162.3 7.6 %collective-permute-start.23 = (bf16[128,1024]{1,0:T(8,128)(2,1)S(1)}, bf16[128,1024]{1,0:T(8,128)(2,1)S(1)}, u32[]{:S(2)}, u32[]{:S(2)}) collective-permute-start(bf16[128,1024]{1,0:T(8,128)(2,1)S(1)} %get-tuple-element.135), channel_id=1, source_target_pairs={{0,52},{4,0},{16,4},{20,16},{32,20},{36,32},{48,36},{52,48},{1,53}... | collective-permute-start | bytes 786440 | tf_op jit(solution)/shard_map/ppermute | solution.py:63
  (4 other events, 55.3 us)

commit v6 on v5

--- a/solution.py
+++ b/solution.py
@@ -115,25 +115,29 @@
 def columns_sums(tables, added):
     tiles = tables[0].shape[1] // LANES
 
-    def blocks(t):
-        start = 0
+    def fold(start, join):
+        results, row = start, 0
         for table in tables:
             for c in range(table.shape[0] // LANES):
-                z = table[c * LANES : (c + 1) * LANES, t * LANES : (t + 1) * LANES]
-                if added is not None:
-                    z = z + added[start : start + LANES, :]
-                start += LANES
-                yield z.reshape(LANES // 8, 8, LANES)
-
-    tops, totals = [], []
-    for t in range(tiles):
-        top = functools.reduce(jnp.maximum, (jnp.max(z, axis=0) for z in blocks(t)))
-        top = jnp.max(top, axis=0, keepdims=True)
-        total = functools.reduce(
-            jnp.add, (jnp.sum(jnp.exp2(z - top[None]), axis=0) for z in blocks(t))
-        )
-        tops.append(top)
-        totals.append(jnp.sum(total, axis=0, keepdims=True))
+                add = None if added is None else added[row : row + LANES, :]
+                for t in range(tiles):
+                    z = table[c * LANES : (c + 1) * LANES, t * LANES : (t + 1) * LANES]
+                    z = (z if add is None else z + add).reshape(LANES // 8, 8, LANES)
+                    results[t] = join(t, results[t], z)
+                row += LANES
+        return results
+
+    def larger(t, top, z):
+        z = jnp.max(z, axis=0)
+        return z if top is None else jnp.maximum(top, z)
+
+    tops = [jnp.max(top, axis=0, keepdims=True) for top in fold([None] * tiles, larger)]
+
+    def total(t, so_far, z):
+        z = jnp.sum(jnp.exp2(z - tops[t][None]), axis=0)
+        return z if so_far is None else so_far + z
+
+    totals = [jnp.sum(v, axis=0, keepdims=True) for v in fold([None] * tiles, total)]
     return tops, totals
 
 
@@ -472,7 +476,7 @@
         up, down = shift(up, 1), shift(down, -1)
     tgt_pull = jnp.sum(parts.astype(f32), axis=0)
     src_pull = own_term + up.astype(f32) + down.astype(f32)
-    row_cost = jnp.sum(src_pull * src_emb.astype(f32), axis=1) * (-1.0 / math.sqrt(depth))
+    row_cost = jnp.sum(src_pull * (src_emb.astype(f32) * (-1.0 / math.sqrt(depth))), axis=1)
     return (src_pull, tgt_pull, row_cost)
 
 

time: 172 us -> 171 us (level)
  no operation moved by 1% of the time
where the time goes in v6:
time: 171 us
  blocking collectives  70.1 us (41%)
  starting transfers between devices  45.4 us (27%)
  Pallas kernels  26.7 us (16%)
  waiting for transfers between devices  23.8 us (14%)
  other arithmetic  3.52 us (2%)
    all_to_all x3, blocking collectives, shards(): gathered = lax.all_to_all(part, SPREAD, 0, 0)  35.7 us
    all_to_all x3, blocking collectives, shards(): gathered = lax.all_to_all(part, RING, 0, 0)  34.4 us
    ppermute x16, starting transfers between devices, shift(): lax.ppermute(value, RING, [(i, (i + step) % size) for i in range(size)])  29 us
    pallas_call x21, Pallas kernels, call(): pl.pallas_call(kernel, out_shape=outs, in_specs=specs, out_specs=[IN_HBM...  26.7 us
    ppermute x16, waiting for transfers between devices, shift(): lax.ppermute(value, RING, [(i, (i + step) % size) for i in range(size)])  14.2 us
    ppermute x6, starting transfers between devices, gather_axis(): lax.ppermute(block, axis, [((i + k) % size, i) for i in range(size)])  10.6 us
    ppermute x6, waiting for transfers between devices, gather_axis(): lax.ppermute(block, axis, [((i + k) % size, i) for i in range(size)])  9.59 us
    all_to_all x1, starting transfers between devices, shards(): parts = lax.all_to_all(sent.reshape(plane, columns, depth), PLANE, 0, 0)  5.55 us
  transfers between devices with their start and end apart: 25, of which 11 were waited for; matrix products, arithmetic and copies ran while one was open for 1% of the time, Pallas kernels for 6%

profile of v6, /device:TPU:2, one launch (start us, length us, event | category | flops | bytes accessed | tf_op | source)
XLA Modules:
  0.0 170.5 jit_solution(4673213647245141423)
XLA Ops:
  4.3 4.0 %collective-permute-start = (bf16[128,1152]{1,0:T(8,128)(2,1)S(1)}, bf16[128,1152]{1,0:T(8,128)(2,1)S(1)}, u32[]{:S(2)}, u32[]{:S(2)}) collective-permute-start(bf16[128,1152]{1,0:T(8,128)(2,1)S(1)} %get-tuple-element.70.own), channel_id=1, source_target_pairs={{0,52},{4,0},{16,4},{20,16},{32,20},{36,32},{48,36},{52,48},{1,53}... | collective-permute-start | bytes 884744 | tf_op jit(solution)/shard_map/ppermute | solution.py:63
  9.9 2.9 %collective-permute-start.3 = (bf16[32,1152]{1,0:T(8,128)(2,1)S(1)}, bf16[32,1152]{1,0:T(8,128)(2,1)S(1)}, u32[]{:S(2)}, u32[]{:S(2)}) collective-permute-start(bf16[32,1152]{1,0:T(8,128)(2,1)S(1)} %get-tuple-element.71.refs_0_), channel_id=1, source_target_pairs={{2,0},{3,1},{0,2},{1,3},{6,4},{7,5},{4,6},{5,7},{10,8},{11,9},{8,1... | collective-permute-start | bytes 221192 | tf_op jit(solution)/shard_map/ppermute | solution.py:351
  18.3 3.2 %collective-permute-start.10 = (bf16[128,1152]{1,0:T(8,128)(2,1)S(1)}, bf16[128,1152]{1,0:T(8,128)(2,1)S(1)}, u32[]{:S(2)}, u32[]{:S(2)}) collective-permute-start(bf16[128,1152]{1,0:T(8,128)(2,1)S(1)} %collective-permute-done.near), channel_id=1, source_target_pairs={{0,52},{4,0},{16,4},{20,16},{32,20},{36,32},{48,36},{52,48},{1,53}... | collective-permute-start | bytes 884744 | tf_op jit(solution)/shard_map/ppermute | solution.py:63
  24.1 2.2 %collective-permute-start.5 = (bf16[128,1152]{1,0:T(8,128)(2,1)S(1)}, bf16[128,1152]{1,0:T(8,128)(2,1)S(1)}, u32[]{:S(2)}, u32[]{:S(2)}) collective-permute-start(bf16[128,1152]{1,0:T(8,128)(2,1)S(1)} %shard_map.68.refs_0_), channel_id=1, source_target_pairs={{64,0},{128,64},{192,128},{0,192},{65,1},{129,65},{193,129},{1,193... | collective-permute-start | bytes 884744 | tf_op jit(solution)/shard_map/ppermute | solution.py:351
  26.9 3.2 %collective-permute-start.11 = (bf16[128,1152]{1,0:T(8,128)(2,1)S(1)}, bf16[128,1152]{1,0:T(8,128)(2,1)S(1)}, u32[]{:S(2)}, u32[]{:S(2)}) collective-permute-start(bf16[128,1152]{1,0:T(8,128)(2,1)S(1)} %collective-permute-done.10.near), channel_id=1, source_target_pairs={{0,52},{4,0},{16,4},{20,16},{32,20},{36,32},{48,36},{52,48},{1,53}... | collective-permute-start | bytes 884744 | tf_op jit(solution)/shard_map/ppermute | solution.py:63
  31.5 2.8 %collective-permute-done.6.refs_2_ = bf16[128,1152]{1,0:T(8,128)(2,1)S(1)} collective-permute-done((bf16[128,1152]{1,0:T(8,128)(2,1)S(1)}, bf16[128,1152]{1,0:T(8,128)(2,1)S(1)}, u32[]{:S(2)}, u32[]{:S(2)}) %collective-permute-start.6) | collective-permute-done | bytes 294944 | tf_op jit(solution)/shard_map/ppermute | solution.py:351
  34.3 2.4 %collective-permute-done.5.refs_1_ = bf16[128,1152]{1,0:T(8,128)(2,1)S(1)} collective-permute-done((bf16[128,1152]{1,0:T(8,128)(2,1)S(1)}, bf16[128,1152]{1,0:T(8,128)(2,1)S(1)}, u32[]{:S(2)}, u32[]{:S(2)}) %collective-permute-start.5) | collective-permute-done | bytes 294944 | tf_op jit(solution)/shard_map/ppermute | solution.py:351
  38.2 3.2 %collective-permute-start.14 = (bf16[64,1152]{1,0:T(8,128)(2,1)S(1)}, bf16[64,1152]{1,0:T(8,128)(2,1)S(1)}, u32[]{:S(2)}, u32[]{:S(2)}) collective-permute-start(bf16[64,1152]{1,0:T(8,128)(2,1)S(1)} %get-tuple-element.84), channel_id=1, source_target_pairs={{0,52},{4,0},{16,4},{20,16},{32,20},{36,32},{48,36},{52,48},{1,53}... | collective-permute-start | bytes 442376 | tf_op jit(solution)/shard_map/ppermute | solution.py:63
  48.4 13.6 %all_to_all.35.refs_5_ = f32[8,8,128]{2,1,0:T(8,128)S(1)} all-to-all(f32[8,8,128]{2,1,0:T(8,128)S(1)} %get-tuple-element.95), channel_id=1, replica_groups=mesh['x'=4,'zh'=4,'core'=2,'zl'=2,'y'=4] {'zh','zl'}, dimensions={0} | all-to-all | bytes 65536 | tf_op jit(solution)/shard_map/all_to_all | solution.py:425
  63.6 13.2 %all_to_all.36.refs_5_ = f32[32,8,128]{2,1,0:T(8,128)S(1)} all-to-all(f32[32,8,128]{2,1,0:T(8,128)S(1)} %get-tuple-element.96), channel_id=1, replica_groups=mesh['x'=4,'zh'=4,'core'=2,'zl'=2,'y'=4] {'x','y','core'}, dimensions={0} | all-to-all | bytes 262144 | tf_op jit(solution)/shard_map/all_to_all | solution.py:431
  78.5 10.4 %all_to_all.37.refs_5_ = f32[8,8,128]{2,1,0:T(8,128)S(1)} all-to-all(f32[8,8,128]{2,1,0:T(8,128)S(1)} %shard_map.77), channel_id=1, replica_groups=mesh['x'=4,'zh'=4,'core'=2,'zl'=2,'y'=4] {'zh','zl'}, dimensions={0} | all-to-all | bytes 65536 | tf_op jit(solution)/shard_map/all_to_all | solution.py:425
  90.5 11.3 %all_to_all.38.refs_5_ = f32[32,8,128]{2,1,0:T(8,128)S(1)} all-to-all(f32[32,8,128]{2,1,0:T(8,128)S(1)} %get-tuple-element.97), channel_id=1, replica_groups=mesh['x'=4,'zh'=4,'core'=2,'zl'=2,'y'=4] {'x','y','core'}, dimensions={0} | all-to-all | bytes 262144 | tf_op jit(solution)/shard_map/all_to_all | solution.py:431
  103.4 10.4 %all_to_all.39.refs_5_ = f32[8,8,128]{2,1,0:T(8,128)S(1)} all-to-all(f32[8,8,128]{2,1,0:T(8,128)S(1)} %shard_map.79), channel_id=1, replica_groups=mesh['x'=4,'zh'=4,'core'=2,'zl'=2,'y'=4] {'zh','zl'}, dimensions={0} | all-to-all | bytes 65536 | tf_op jit(solution)/shard_map/all_to_all | solution.py:425
  115.5 11.3 %all_to_all.40.refs_1_ = f32[32,8,128]{2,1,0:T(8,128)S(1)} all-to-all(f32[32,8,128]{2,1,0:T(8,128)S(1)} %get-tuple-element.98), channel_id=1, replica_groups=mesh['x'=4,'zh'=4,'core'=2,'zl'=2,'y'=4] {'x','y','core'}, dimensions={0} | all-to-all | bytes 262144 | tf_op jit(solution)/shard_map/all_to_all | solution.py:431
  127.9 2.5 %shard_map.82 = (f32[512,1024]{1,0:T(8,128)S(1)}, bf16[512,1024]{1,0:T(8,128)(2,1)S(1)}) custom-call(f32[1024,256]{1,0:T(8,128)S(1)} %get-tuple-element.76.refs_0_, f32[1024,256]{1,0:T(8,128)S(1)} %get-tuple-element.78.refs_1_, f32[1024,256]{1,0:T(8,128)S(1)} %get-tuple-element.81.refs_2_, f32[1024,128]{1,0:T(8,128)S(1)} %get-tuple-element.82.refs_3_, ...), custom_call_target="tpu_custom_call" | custom-call | flops 2147483648 | bytes 8388608 | tf_op jit(solution)/shard_map/pallas_call | solution.py:48
  131.1 2.7 %collective-permute-start.17 = (bf16[64,1024]{1,0:T(8,128)(2,1)S(1)}, bf16[64,1024]{1,0:T(8,128)(2,1)S(1)}, u32[]{:S(2)}, u32[]{:S(2)}) collective-permute-start(bf16[64,1024]{1,0:T(8,128)(2,1)S(1)} %get-tuple-element.109), channel_id=1, source_target_pairs={{0,52},{4,0},{16,4},{20,16},{32,20},{36,32},{48,36},{52,48},{1,53}... | collective-permute-start | bytes 393224 | tf_op jit(solution)/shard_map/ppermute | solution.py:63
  133.8 2.8 %shard_map.83 = (f32[128,1024]{1,0:T(8,128)S(1)}, f32[128,1024]{1,0:T(8,128)S(1)}, f32[128,1024]{1,0:T(8,128)S(1)}, f32[128,1024]{1,0:T(8,128)S(1)}, f32[128,102...) custom-call(s32[6]{0:T(128)S(1)} %stack.27.offsets, f32[256,1024]{1,0:T(8,128)S(1)} %get-tuple-element.91.refs_0_, ...), custom_call_target="tpu_custom_call" | custom-call | flops 536870912 | bytes 4194304 | tf_op jit(solution)/shard_map/pallas_call | solution.py:48
  138.7 5.5 %all-to-all-start.6 = ((bf16[16,32,1024]{2,1,0:T(8,128)(2,1)}), bf16[16,32,1024]{2,1,0:T(8,128)(2,1)}, u32[]{:S(2)}, u32[]{:S(2)}) async-start(bf16[16,32,1024]{2,1,0:T(8,128)(2,1)} %bitcast.9), calls=%async_computation.6 | async-start | bytes 2097152 | tf_op jit(solution)/shard_map/all_to_all | solution.py:468
  144.4 3.2 %collective-permute-start.19 = (bf16[128,1024]{1,0:T(8,128)(2,1)S(1)}, bf16[128,1024]{1,0:T(8,128)(2,1)S(1)}, u32[]{:S(2)}, u32[]{:S(2)}) collective-permute-start(bf16[128,1024]{1,0:T(8,128)(2,1)S(1)} %get-tuple-element.126), channel_id=1, source_target_pairs={{0,52},{4,0},{16,4},{20,16},{32,20},{36,32},{48,36},{52,48},{1,53}... | collective-permute-start | bytes 786440 | tf_op jit(solution)/shard_map/ppermute | solution.py:63
  147.6 5.5 %collective-permute-done.18.up = bf16[128,1024]{1,0:T(8,128)(2,1)S(1)} collective-permute-done((bf16[128,1024]{1,0:T(8,128)(2,1)S(1)}, bf16[128,1024]{1,0:T(8,128)(2,1)S(1)}, u32[]{:S(2)}, u32[]{:S(2)}) %collective-permute-start.18) | collective-permute-done | bytes 262176 | tf_op jit(solution)/shard_map/ppermute | solution.py:63
  153.4 3.2 %collective-permute-start.21 = (bf16[128,1024]{1,0:T(8,128)(2,1)S(1)}, bf16[128,1024]{1,0:T(8,128)(2,1)S(1)}, u32[]{:S(2)}, u32[]{:S(2)}) collective-permute-start(bf16[128,1024]{1,0:T(8,128)(2,1)S(1)} %get-tuple-element.130), channel_id=1, source_target_pairs={{0,52},{4,0},{16,4},{20,16},{32,20},{36,32},{48,36},{52,48},{1,53}... | collective-permute-start | bytes 786440 | tf_op jit(solution)/shard_map/ppermute | solution.py:63
  156.6 4.7 %collective-permute-done.20.up = bf16[128,1024]{1,0:T(8,128)(2,1)S(1)} collective-permute-done((bf16[128,1024]{1,0:T(8,128)(2,1)S(1)}, bf16[128,1024]{1,0:T(8,128)(2,1)S(1)}, u32[]{:S(2)}, u32[]{:S(2)}) %collective-permute-start.20) | collective-permute-done | bytes 262176 | tf_op jit(solution)/shard_map/ppermute | solution.py:63
  161.5 3.2 %collective-permute-start.23 = (bf16[128,1024]{1,0:T(8,128)(2,1)S(1)}, bf16[128,1024]{1,0:T(8,128)(2,1)S(1)}, u32[]{:S(2)}, u32[]{:S(2)}) collective-permute-start(bf16[128,1024]{1,0:T(8,128)(2,1)S(1)} %get-tuple-element.135), channel_id=1, source_target_pairs={{0,52},{4,0},{16,4},{20,16},{32,20},{36,32},{48,36},{52,48},{1,53}... | collective-permute-start | bytes 786440 | tf_op jit(solution)/shard_map/ppermute | solution.py:63
  166.8 2.3 %collective-permute-done.22 = bf16[128,1024]{1,0:T(8,128)(2,1)S(1)} collective-permute-done((bf16[128,1024]{1,0:T(8,128)(2,1)S(1)}, bf16[128,1024]{1,0:T(8,128)(2,1)S(1)}, u32[]{:S(2)}, u32[]{:S(2)}) %collective-permute-start.22) | collective-permute-done | bytes 262176 | tf_op jit(solution)/shard_map/ppermute | solution.py:63
  (62 shorter events, 39.9 us)
Async XLA Ops:
  2.3 15.8 %collective-permute-start.1 = (bf16[128,1152]{1,0:T(8,128)(2,1)S(1)}, bf16[128,1152]{1,0:T(8,128)(2,1)S(1)}, u32[]{:S(2)}, u32[]{:S(2)}) collective-permute-start(bf16[128,1152]{1,0:T(8,128)(2,1)S(1)} %get-tuple-element.70.own), channel_id=1, source_target_pairs={{0,4},{4,16},{16,20},{20,32},{32,36},{36,48},{48,52},{52,0},{1,5},... | collective-permute-start | bytes 884744 | tf_op jit(solution)/shard_map/ppermute | solution.py:63
  4.3 13.9 %collective-permute-start = (bf16[128,1152]{1,0:T(8,128)(2,1)S(1)}, bf16[128,1152]{1,0:T(8,128)(2,1)S(1)}, u32[]{:S(2)}, u32[]{:S(2)}) collective-permute-start(bf16[128,1152]{1,0:T(8,128)(2,1)S(1)} %get-tuple-element.70.own), channel_id=1, source_target_pairs={{0,52},{4,0},{16,4},{20,16},{32,20},{36,32},{48,36},{52,48},{1,53}... | collective-permute-start | bytes 884744 | tf_op jit(solution)/shard_map/ppermute | solution.py:63
  8.4 6.4 %collective-permute-start.4 = (bf16[32,1152]{1,0:T(8,128)(2,1)S(1)}, bf16[32,1152]{1,0:T(8,128)(2,1)S(1)}, u32[]{:S(2)}, u32[]{:S(2)}) collective-permute-start(bf16[32,1152]{1,0:T(8,128)(2,1)S(1)} %get-tuple-element.71.refs_0_), channel_id=1, source_target_pairs={{3,0},{0,1},{1,2},{2,3},{7,4},{4,5},{5,6},{6,7},{11,8},{8,9},{9,10... | collective-permute-start | bytes 221192 | tf_op jit(solution)/shard_map/ppermute | solution.py:351
  9.9 6.2 %collective-permute-start.3 = (bf16[32,1152]{1,0:T(8,128)(2,1)S(1)}, bf16[32,1152]{1,0:T(8,128)(2,1)S(1)}, u32[]{:S(2)}, u32[]{:S(2)}) collective-permute-start(bf16[32,1152]{1,0:T(8,128)(2,1)S(1)} %get-tuple-element.71.refs_0_), channel_id=1, source_target_pairs={{2,0},{3,1},{0,2},{1,3},{6,4},{7,5},{4,6},{5,7},{10,8},{11,9},{8,1... | collective-permute-start | bytes 221192 | tf_op jit(solution)/shard_map/ppermute | solution.py:351
  12.8 4.4 %collective-permute-start.2 = (bf16[32,1152]{1,0:T(8,128)(2,1)S(1)}, bf16[32,1152]{1,0:T(8,128)(2,1)S(1)}, u32[]{:S(2)}, u32[]{:S(2)}) collective-permute-start(bf16[32,1152]{1,0:T(8,128)(2,1)S(1)} %get-tuple-element.71.refs_0_), channel_id=1, source_target_pairs={{1,0},{2,1},{3,2},{0,3},{5,4},{6,5},{7,6},{4,7},{9,8},{10,9},{11,1... | collective-permute-start | bytes 221192 | tf_op jit(solution)/shard_map/ppermute | solution.py:351
  18.2 8.7 %collective-permute-start.8 = (bf16[128,1152]{1,0:T(8,128)(2,1)S(1)}, bf16[128,1152]{1,0:T(8,128)(2,1)S(1)}, u32[]{:S(2)}, u32[]{:S(2)}) collective-permute-start(bf16[128,1152]{1,0:T(8,128)(2,1)S(1)} %collective-permute-done.1.other), channel_id=1, source_target_pairs={{0,4},{4,16},{16,20},{20,32},{32,36},{36,48},{48,52},{52,0},{1,5},... | collective-permute-start | bytes 884744 | tf_op jit(solution)/shard_map/ppermute | solution.py:63
  18.3 8.6 %collective-permute-start.10 = (bf16[128,1152]{1,0:T(8,128)(2,1)S(1)}, bf16[128,1152]{1,0:T(8,128)(2,1)S(1)}, u32[]{:S(2)}, u32[]{:S(2)}) collective-permute-start(bf16[128,1152]{1,0:T(8,128)(2,1)S(1)} %collective-permute-done.near), channel_id=1, source_target_pairs={{0,52},{4,0},{16,4},{20,16},{32,20},{36,32},{48,36},{52,48},{1,53}... | collective-permute-start | bytes 884744 | tf_op jit(solution)/shard_map/ppermute | solution.py:63
  21.5 9.9 %collective-permute-start.7 = (bf16[128,1152]{1,0:T(8,128)(2,1)S(1)}, bf16[128,1152]{1,0:T(8,128)(2,1)S(1)}, u32[]{:S(2)}, u32[]{:S(2)}) collective-permute-start(bf16[128,1152]{1,0:T(8,128)(2,1)S(1)} %shard_map.68.refs_0_), channel_id=1, source_target_pairs={{192,0},{0,64},{64,128},{128,192},{193,1},{1,65},{65,129},{129,193... | collective-permute-start | bytes 884744 | tf_op jit(solution)/shard_map/ppermute | solution.py:351
  23.0 11.3 %collective-permute-start.6 = (bf16[128,1152]{1,0:T(8,128)(2,1)S(1)}, bf16[128,1152]{1,0:T(8,128)(2,1)S(1)}, u32[]{:S(2)}, u32[]{:S(2)}) collective-permute-start(bf16[128,1152]{1,0:T(8,128)(2,1)S(1)} %shard_map.68.refs_0_), channel_id=1, source_target_pairs={{128,0},{192,64},{0,128},{64,192},{129,1},{193,65},{1,129},{65,193... | collective-permute-start | bytes 884744 | tf_op jit(solution)/shard_map/ppermute | solution.py:351
  24.1 12.6 %collective-permute-start.5 = (bf16[128,1152]{1,0:T(8,128)(2,1)S(1)}, bf16[128,1152]{1,0:T(8,128)(2,1)S(1)}, u32[]{:S(2)}, u32[]{:S(2)}) collective-permute-start(bf16[128,1152]{1,0:T(8,128)(2,1)S(1)} %shard_map.68.refs_0_), channel_id=1, source_target_pairs={{64,0},{128,64},{192,128},{0,192},{65,1},{129,65},{193,129},{1,193... | collective-permute-start | bytes 884744 | tf_op jit(solution)/shard_map/ppermute | solution.py:351
  26.9 10.7 %collective-permute-start.9 = (bf16[128,1152]{1,0:T(8,128)(2,1)S(1)}, bf16[128,1152]{1,0:T(8,128)(2,1)S(1)}, u32[]{:S(2)}, u32[]{:S(2)}) collective-permute-start(bf16[128,1152]{1,0:T(8,128)(2,1)S(1)} %collective-permute-done.8.other), channel_id=1, source_target_pairs={{0,4},{4,16},{16,20},{20,32},{32,36},{36,48},{48,52},{52,0},{1,5},... | collective-permute-start | bytes 884744 | tf_op jit(solution)/shard_map/ppermute | solution.py:63
  26.9 10.7 %collective-permute-start.11 = (bf16[128,1152]{1,0:T(8,128)(2,1)S(1)}, bf16[128,1152]{1,0:T(8,128)(2,1)S(1)}, u32[]{:S(2)}, u32[]{:S(2)}) collective-permute-start(bf16[128,1152]{1,0:T(8,128)(2,1)S(1)} %collective-permute-done.10.near), channel_id=1, source_target_pairs={{0,52},{4,0},{16,4},{20,16},{32,20},{36,32},{48,36},{52,48},{1,53}... | collective-permute-start | bytes 884744 | tf_op jit(solution)/shard_map/ppermute | solution.py:63
  38.1 8.4 %collective-permute-start.13 = (bf16[64,1152]{1,0:T(8,128)(2,1)S(1)}, bf16[64,1152]{1,0:T(8,128)(2,1)S(1)}, u32[]{:S(2)}, u32[]{:S(2)}) collective-permute-start(bf16[64,1152]{1,0:T(8,128)(2,1)S(1)} %get-tuple-element.83), channel_id=1, source_target_pairs={{0,4},{4,16},{16,20},{20,32},{32,36},{36,48},{48,52},{52,0},{1,5},... | collective-permute-start | bytes 442376 | tf_op jit(solution)/shard_map/ppermute | solution.py:63
  38.2 8.3 %collective-permute-start.14 = (bf16[64,1152]{1,0:T(8,128)(2,1)S(1)}, bf16[64,1152]{1,0:T(8,128)(2,1)S(1)}, u32[]{:S(2)}, u32[]{:S(2)}) collective-permute-start(bf16[64,1152]{1,0:T(8,128)(2,1)S(1)} %get-tuple-element.84), channel_id=1, source_target_pairs={{0,52},{4,0},{16,4},{20,16},{32,20},{36,32},{48,36},{52,48},{1,53}... | collective-permute-start | bytes 442376 | tf_op jit(solution)/shard_map/ppermute | solution.py:63
  130.4 7.2 %collective-permute-start.15 = (bf16[512,1024]{1,0:T(8,128)(2,1)S(1)}, bf16[512,1024]{1,0:T(8,128)(2,1)S(1)}, u32[]{:S(2)}, u32[]{:S(2)}) collective-permute-start(bf16[512,1024]{1,0:T(8,128)(2,1)S(1)} %get-tuple-element.107), channel_id=1, source_target_pairs={{0,8},{8,0},{1,9},{9,1},{2,10},{10,2},{3,11},{11,3},{4,12},{12,4},... | collective-permute-start | bytes 3145736 | tf_op jit(solution)/shard_map/ppermute | solution.py:461
  130.6 7.0 %collective-permute-start.16 = (bf16[64,1024]{1,0:T(8,128)(2,1)S(1)}, bf16[64,1024]{1,0:T(8,128)(2,1)S(1)}, u32[]{:S(2)}, u32[]{:S(2)}) collective-permute-start(bf16[64,1024]{1,0:T(8,128)(2,1)S(1)} %get-tuple-element.108), channel_id=1, source_target_pairs={{0,4},{4,16},{16,20},{20,32},{32,36},{36,48},{48,52},{52,0},{1,5},... | collective-permute-start | bytes 393224 | tf_op jit(solution)/shard_map/ppermute | solution.py:63
  131.1 6.5 %collective-permute-start.17 = (bf16[64,1024]{1,0:T(8,128)(2,1)S(1)}, bf16[64,1024]{1,0:T(8,128)(2,1)S(1)}, u32[]{:S(2)}, u32[]{:S(2)}) collective-permute-start(bf16[64,1024]{1,0:T(8,128)(2,1)S(1)} %get-tuple-element.109), channel_id=1, source_target_pairs={{0,52},{4,0},{16,4},{20,16},{32,20},{36,32},{48,36},{52,48},{1,53}... | collective-permute-start | bytes 393224 | tf_op jit(solution)/shard_map/ppermute | solution.py:63
  138.7 22.7 %all-to-all-start.6 = ((bf16[16,32,1024]{2,1,0:T(8,128)(2,1)}), bf16[16,32,1024]{2,1,0:T(8,128)(2,1)}, u32[]{:S(2)}, u32[]{:S(2)}) async-start(bf16[16,32,1024]{2,1,0:T(8,128)(2,1)} %bitcast.9), calls=%async_computation.6 | async-start | bytes 2097152 | tf_op jit(solution)/shard_map/all_to_all | solution.py:468
  144.3 8.9 %collective-permute-start.18 = (bf16[128,1024]{1,0:T(8,128)(2,1)S(1)}, bf16[128,1024]{1,0:T(8,128)(2,1)S(1)}, u32[]{:S(2)}, u32[]{:S(2)}) collective-permute-start(bf16[128,1024]{1,0:T(8,128)(2,1)S(1)} %get-tuple-element.124), channel_id=1, source_target_pairs={{0,4},{4,16},{16,20},{20,32},{32,36},{36,48},{48,52},{52,0},{1,5},... | collective-permute-start | bytes 786440 | tf_op jit(solution)/shard_map/ppermute | solution.py:63
  144.4 8.7 %collective-permute-start.19 = (bf16[128,1024]{1,0:T(8,128)(2,1)S(1)}, bf16[128,1024]{1,0:T(8,128)(2,1)S(1)}, u32[]{:S(2)}, u32[]{:S(2)}) collective-permute-start(bf16[128,1024]{1,0:T(8,128)(2,1)S(1)} %get-tuple-element.126), channel_id=1, source_target_pairs={{0,52},{4,0},{16,4},{20,16},{32,20},{36,32},{48,36},{52,48},{1,53}... | collective-permute-start | bytes 786440 | tf_op jit(solution)/shard_map/ppermute | solution.py:63
  153.3 8.0 %collective-permute-start.20 = (bf16[128,1024]{1,0:T(8,128)(2,1)S(1)}, bf16[128,1024]{1,0:T(8,128)(2,1)S(1)}, u32[]{:S(2)}, u32[]{:S(2)}) collective-permute-start(bf16[128,1024]{1,0:T(8,128)(2,1)S(1)} %get-tuple-element.128), channel_id=1, source_target_pairs={{0,4},{4,16},{16,20},{20,32},{32,36},{36,48},{48,52},{52,0},{1,5},... | collective-permute-start | bytes 786440 | tf_op jit(solution)/shard_map/ppermute | solution.py:63
  153.4 8.0 %collective-permute-start.21 = (bf16[128,1024]{1,0:T(8,128)(2,1)S(1)}, bf16[128,1024]{1,0:T(8,128)(2,1)S(1)}, u32[]{:S(2)}, u32[]{:S(2)}) collective-permute-start(bf16[128,1024]{1,0:T(8,128)(2,1)S(1)} %get-tuple-element.130), channel_id=1, source_target_pairs={{0,52},{4,0},{16,4},{20,16},{32,20},{36,32},{48,36},{52,48},{1,53}... | collective-permute-start | bytes 786440 | tf_op jit(solution)/shard_map/ppermute | solution.py:63
  161.4 7.7 %collective-permute-start.22 = (bf16[128,1024]{1,0:T(8,128)(2,1)S(1)}, bf16[128,1024]{1,0:T(8,128)(2,1)S(1)}, u32[]{:S(2)}, u32[]{:S(2)}) collective-permute-start(bf16[128,1024]{1,0:T(8,128)(2,1)S(1)} %get-tuple-element.134), channel_id=1, source_target_pairs={{0,4},{4,16},{16,20},{20,32},{32,36},{36,48},{48,52},{52,0},{1,5},... | collective-permute-start | bytes 786440 | tf_op jit(solution)/shard_map/ppermute | solution.py:63
  161.5 7.6 %collective-permute-start.23 = (bf16[128,1024]{1,0:T(8,128)(2,1)S(1)}, bf16[128,1024]{1,0:T(8,128)(2,1)S(1)}, u32[]{:S(2)}, u32[]{:S(2)}) collective-permute-start(bf16[128,1024]{1,0:T(8,128)(2,1)S(1)} %get-tuple-element.135), channel_id=1, source_target_pairs={{0,52},{4,0},{16,4},{20,16},{32,20},{36,32},{48,36},{52,48},{1,53}... | collective-permute-start | bytes 786440 | tf_op jit(solution)/shard_map/ppermute | solution.py:63
  (4 other events, 55.3 us)

commit v7 on v6

--- a/solution.py
+++ b/solution.py
@@ -110,6 +110,23 @@
         [(block, out.at[pl.ds(pl.multiple_of(at, rows), rows)]) for block, at in zip(blocks, places)],
         sems,
     )
+
+
+def assemble_relayed_kernel(offsets, own, first, second, third, relayed, out, sems):
+    rows = own.shape[0]
+    places = [
+        out.at[pl.ds(pl.multiple_of(lax.rem(offsets[4] + k, 4) * rows, rows), rows)] for k in range(4)
+    ]
+
+    @pl.when(offsets[1] == 0)
+    def _():
+        copy_all([(second, places[2])], sems)
+
+    @pl.when(offsets[1] != 0)
+    def _():
+        copy_all([(relayed, places[2])], sems)
+
+    copy_all([(own, places[0]), (first, places[1]), (third, places[3])], sems)
 
 
 def columns_sums(tables, added):
@@ -361,7 +378,14 @@
     block = gather_axis(tgt, "y", 5)
     block, up, down = lax.optimization_barrier((block, up, down))
     up, down = shift(up, 1), shift(down, -1)
-    mine = gather_axis(block, "x", 4)
+    first, third = (lax.ppermute(block, "x", [((i + k) % 4, i) for i in range(4)]) for k in (1, 3))
+    pairs_of = lambda step, c: [(((i + step) % 4) * 2 + c, i * 2 + c) for i in range(4)]
+    second = lax.ppermute(block, ("x", "core"), pairs_of(2, 0))
+    relayed = lax.ppermute(third, ("x", "core"), pairs_of(3, 1))
+    (mine,) = call(
+        assemble_relayed_kernel, [jax.ShapeDtypeStruct((plane * columns, n_label), bf16)], [dma((3,))],
+        offsets, block, first, second, third, relayed, smem=1, flops=1, bytes_accessed=2**20,
+    )
     pairs.append((down, up))
     up, down = shift(up, 1), shift(down, -1)
     mine, up, down = lax.optimization_barrier((mine, up, down))

time: 171 us -> 170 us (level)
  waiting for transfers between devices: 23.8 us -> 20.4 us
  starting transfers between devices: 45.4 us -> 48.4 us
    ppermute x0 -> x4, starting transfers between devices: none -> 7.48 us  [the longest x2 3.8 us: shards(): lax.ppermute(block, 'x', [((i + k) % 4, i) for i in range(4)])]
    ppermute x6 -> x3, waiting for transfers between devices: 9.59 us -> 3 us  [gather_axis(): lax.ppermute(block, axis, [((i + k) % size, i) for i in range(size)])]
    ppermute x6 -> x3, starting transfers between devices: 10.6 us -> 5.83 us  [gather_axis(): lax.ppermute(block, axis, [((i + k) % size, i) for i in range(size)])]
    ppermute x0 -> x4, waiting for transfers between devices: none -> 3.73 us  [the longest x2 2.76 us: shards(): lax.ppermute(block, 'x', [((i + k) % 4, i) for i in range(4)])]
  transfers between devices with their start and end apart: 25 -> 26, of which waited for: 11 -> 10; matrix products, arithmetic and copies ran while one was open for 1% -> 1% of each run, Pallas kernels for 6% -> 6%
where the time goes in v7:
time: 170 us
  blocking collectives  69.5 us (41%)
  starting transfers between devices  48.4 us (28%)
  Pallas kernels  26.7 us (16%)
  waiting for transfers between devices  20.4 us (12%)
  other arithmetic  3.52 us (2%)
    all_to_all x3, blocking collectives, shards(): gathered = lax.all_to_all(part, SPREAD, 0, 0)  35.2 us
    all_to_all x3, blocking collectives, shards(): gathered = lax.all_to_all(part, RING, 0, 0)  34.4 us
    ppermute x16, starting transfers between devices, shift(): lax.ppermute(value, RING, [(i, (i + step) % size) for i in range(size)])  29.3 us
    pallas_call x21, Pallas kernels, call(): pl.pallas_call(kernel, out_shape=outs, in_specs=specs, out_specs=[IN_HBM...  26.7 us
    ppermute x16, waiting for transfers between devices, shift(): lax.ppermute(value, RING, [(i, (i + step) % size) for i in range(size)])  13.6 us
    ppermute x3, starting transfers between devices, gather_axis(): lax.ppermute(block, axis, [((i + k) % size, i) for i in range(size)])  5.83 us
    all_to_all x1, starting transfers between devices, shards(): parts = lax.all_to_all(sent.reshape(plane, columns, depth), PLANE, 0, 0)  5.58 us
    ppermute x2, starting transfers between devices, shards(): lax.ppermute(block, 'x', [((i + k) % 4, i) for i in range(4)])  3.8 us
  transfers between devices with their start and end apart: 26, of which 10 were waited for; matrix products, arithmetic and copies ran while one was open for 1% of the time, Pallas kernels for 6%

profile of v7, /device:TPU:2, one launch (start us, length us, event | category | flops | bytes accessed | tf_op | source)
XLA Modules:
  0.0 169.5 jit_solution(12334218495942057950)
XLA Ops:
  4.3 4.0 %collective-permute-start = (bf16[128,1152]{1,0:T(8,128)(2,1)S(1)}, bf16[128,1152]{1,0:T(8,128)(2,1)S(1)}, u32[]{:S(2)}, u32[]{:S(2)}) collective-permute-start(bf16[128,1152]{1,0:T(8,128)(2,1)S(1)} %get-tuple-element.70.own), channel_id=1, source_target_pairs={{0,52},{4,0},{16,4},{20,16},{32,20},{36,32},{48,36},{52,48},{1,53}... | collective-permute-start | bytes 884744 | tf_op jit(solution)/shard_map/ppermute | solution.py:63
  9.9 2.9 %collective-permute-start.3 = (bf16[32,1152]{1,0:T(8,128)(2,1)S(1)}, bf16[32,1152]{1,0:T(8,128)(2,1)S(1)}, u32[]{:S(2)}, u32[]{:S(2)}) collective-permute-start(bf16[32,1152]{1,0:T(8,128)(2,1)S(1)} %get-tuple-element.71.refs_0_), channel_id=1, source_target_pairs={{2,0},{3,1},{0,2},{1,3},{6,4},{7,5},{4,6},{5,7},{10,8},{11,9},{8,1... | collective-permute-start | bytes 221192 | tf_op jit(solution)/shard_map/ppermute | solution.py:368
  19.8 3.2 %collective-permute-start.11 = (bf16[128,1152]{1,0:T(8,128)(2,1)S(1)}, bf16[128,1152]{1,0:T(8,128)(2,1)S(1)}, u32[]{:S(2)}, u32[]{:S(2)}) collective-permute-start(bf16[128,1152]{1,0:T(8,128)(2,1)S(1)} %collective-permute-done.near), channel_id=1, source_target_pairs={{0,52},{4,0},{16,4},{20,16},{32,20},{36,32},{48,36},{52,48},{1,53}... | collective-permute-start | bytes 884744 | tf_op jit(solution)/shard_map/ppermute | solution.py:63
  23.0 3.0 %collective-permute-start.6 = (bf16[128,1152]{1,0:T(8,128)(2,1)S(1)}, bf16[128,1152]{1,0:T(8,128)(2,1)S(1)}, u32[]{:S(2)}, u32[]{:S(2)}) collective-permute-start(bf16[128,1152]{1,0:T(8,128)(2,1)S(1)} %shard_map.68.own), channel_id=1, source_target_pairs={{128,0},{192,64},{0,128},{64,192},{129,1},{193,65},{1,129},{65,193... | collective-permute-start | bytes 884744 | tf_op jit(solution)/shard_map/ppermute | solution.py:383
  26.0 2.2 %collective-permute-start.5 = (bf16[128,1152]{1,0:T(8,128)(2,1)S(1)}, bf16[128,1152]{1,0:T(8,128)(2,1)S(1)}, u32[]{:S(2)}, u32[]{:S(2)}) collective-permute-start(bf16[128,1152]{1,0:T(8,128)(2,1)S(1)} %shard_map.68.own), channel_id=1, source_target_pairs={{64,0},{128,64},{192,128},{0,192},{65,1},{129,65},{193,129},{1,193... | collective-permute-start | bytes 884744 | tf_op jit(solution)/shard_map/ppermute | solution.py:381
  29.0 3.2 %collective-permute-start.12 = (bf16[128,1152]{1,0:T(8,128)(2,1)S(1)}, bf16[128,1152]{1,0:T(8,128)(2,1)S(1)}, u32[]{:S(2)}, u32[]{:S(2)}) collective-permute-start(bf16[128,1152]{1,0:T(8,128)(2,1)S(1)} %collective-permute-done.11.near), channel_id=1, source_target_pairs={{0,52},{4,0},{16,4},{20,16},{32,20},{36,32},{48,36},{52,48},{1,53}... | collective-permute-start | bytes 884744 | tf_op jit(solution)/shard_map/ppermute | solution.py:63
  33.2 2.8 %collective-permute-done.5.first = bf16[128,1152]{1,0:T(8,128)(2,1)S(1)} collective-permute-done((bf16[128,1152]{1,0:T(8,128)(2,1)S(1)}, bf16[128,1152]{1,0:T(8,128)(2,1)S(1)}, u32[]{:S(2)}, u32[]{:S(2)}) %collective-permute-start.5) | collective-permute-done | bytes 294944 | tf_op jit(solution)/shard_map/ppermute | solution.py:381
  37.5 3.5 %collective-permute-start.15 = (bf16[64,1152]{1,0:T(8,128)(2,1)S(1)}, bf16[64,1152]{1,0:T(8,128)(2,1)S(1)}, u32[]{:S(2)}, u32[]{:S(2)}) collective-permute-start(bf16[64,1152]{1,0:T(8,128)(2,1)S(1)} %get-tuple-element.84), channel_id=1, source_target_pairs={{0,52},{4,0},{16,4},{20,16},{32,20},{36,32},{48,36},{52,48},{1,53}... | collective-permute-start | bytes 442376 | tf_op jit(solution)/shard_map/ppermute | solution.py:63
  47.9 13.6 %all_to_all.35.refs_5_ = f32[8,8,128]{2,1,0:T(8,128)S(1)} all-to-all(f32[8,8,128]{2,1,0:T(8,128)S(1)} %get-tuple-element.95), channel_id=1, replica_groups=mesh['x'=4,'zh'=4,'core'=2,'zl'=2,'y'=4] {'zh','zl'}, dimensions={0} | all-to-all | bytes 65536 | tf_op jit(solution)/shard_map/all_to_all | solution.py:449
  63.2 12.6 %all_to_all.36.refs_5_ = f32[32,8,128]{2,1,0:T(8,128)S(1)} all-to-all(f32[32,8,128]{2,1,0:T(8,128)S(1)} %get-tuple-element.96), channel_id=1, replica_groups=mesh['x'=4,'zh'=4,'core'=2,'zl'=2,'y'=4] {'x','y','core'}, dimensions={0} | all-to-all | bytes 262144 | tf_op jit(solution)/shard_map/all_to_all | solution.py:455
  77.4 10.4 %all_to_all.37.refs_5_ = f32[8,8,128]{2,1,0:T(8,128)S(1)} all-to-all(f32[8,8,128]{2,1,0:T(8,128)S(1)} %shard_map.77), channel_id=1, replica_groups=mesh['x'=4,'zh'=4,'core'=2,'zl'=2,'y'=4] {'zh','zl'}, dimensions={0} | all-to-all | bytes 65536 | tf_op jit(solution)/shard_map/all_to_all | solution.py:449
  89.5 11.3 %all_to_all.38.refs_5_ = f32[32,8,128]{2,1,0:T(8,128)S(1)} all-to-all(f32[32,8,128]{2,1,0:T(8,128)S(1)} %get-tuple-element.97), channel_id=1, replica_groups=mesh['x'=4,'zh'=4,'core'=2,'zl'=2,'y'=4] {'x','y','core'}, dimensions={0} | all-to-all | bytes 262144 | tf_op jit(solution)/shard_map/all_to_all | solution.py:455
  102.4 10.4 %all_to_all.39.refs_5_ = f32[8,8,128]{2,1,0:T(8,128)S(1)} all-to-all(f32[8,8,128]{2,1,0:T(8,128)S(1)} %shard_map.79), channel_id=1, replica_groups=mesh['x'=4,'zh'=4,'core'=2,'zl'=2,'y'=4] {'zh','zl'}, dimensions={0} | all-to-all | bytes 65536 | tf_op jit(solution)/shard_map/all_to_all | solution.py:449
  114.4 11.3 %all_to_all.40.refs_1_ = f32[32,8,128]{2,1,0:T(8,128)S(1)} all-to-all(f32[32,8,128]{2,1,0:T(8,128)S(1)} %get-tuple-element.98), channel_id=1, replica_groups=mesh['x'=4,'zh'=4,'core'=2,'zl'=2,'y'=4] {'x','y','core'}, dimensions={0} | all-to-all | bytes 262144 | tf_op jit(solution)/shard_map/all_to_all | solution.py:455
  126.9 2.5 %shard_map.82 = (f32[512,1024]{1,0:T(8,128)S(1)}, bf16[512,1024]{1,0:T(8,128)(2,1)S(1)}) custom-call(f32[1024,256]{1,0:T(8,128)S(1)} %get-tuple-element.76.refs_0_, f32[1024,256]{1,0:T(8,128)S(1)} %get-tuple-element.78.refs_1_, f32[1024,256]{1,0:T(8,128)S(1)} %get-tuple-element.81.refs_2_, f32[1024,128]{1,0:T(8,128)S(1)} %get-tuple-element.82.refs_3_, ...), custom_call_target="tpu_custom_call" | custom-call | flops 2147483648 | bytes 8388608 | tf_op jit(solution)/shard_map/pallas_call | solution.py:48
  130.1 2.7 %collective-permute-start.18 = (bf16[64,1024]{1,0:T(8,128)(2,1)S(1)}, bf16[64,1024]{1,0:T(8,128)(2,1)S(1)}, u32[]{:S(2)}, u32[]{:S(2)}) collective-permute-start(bf16[64,1024]{1,0:T(8,128)(2,1)S(1)} %get-tuple-element.109), channel_id=1, source_target_pairs={{0,52},{4,0},{16,4},{20,16},{32,20},{36,32},{48,36},{52,48},{1,53}... | collective-permute-start | bytes 393224 | tf_op jit(solution)/shard_map/ppermute | solution.py:63
  132.8 2.8 %shard_map.83 = (f32[128,1024]{1,0:T(8,128)S(1)}, f32[128,1024]{1,0:T(8,128)S(1)}, f32[128,1024]{1,0:T(8,128)S(1)}, f32[128,1024]{1,0:T(8,128)S(1)}, f32[128,102...) custom-call(s32[6]{0:T(128)S(1)} %stack.27.offsets, f32[256,1024]{1,0:T(8,128)S(1)} %get-tuple-element.91.refs_0_, ...), custom_call_target="tpu_custom_call" | custom-call | flops 536870912 | bytes 4194304 | tf_op jit(solution)/shard_map/pallas_call | solution.py:48
  137.6 5.6 %all-to-all-start.6 = ((bf16[16,32,1024]{2,1,0:T(8,128)(2,1)}), bf16[16,32,1024]{2,1,0:T(8,128)(2,1)}, u32[]{:S(2)}, u32[]{:S(2)}) async-start(bf16[16,32,1024]{2,1,0:T(8,128)(2,1)} %bitcast.9), calls=%async_computation.6 | async-start | bytes 2097152 | tf_op jit(solution)/shard_map/all_to_all | solution.py:492
  143.4 3.2 %collective-permute-start.20 = (bf16[128,1024]{1,0:T(8,128)(2,1)S(1)}, bf16[128,1024]{1,0:T(8,128)(2,1)S(1)}, u32[]{:S(2)}, u32[]{:S(2)}) collective-permute-start(bf16[128,1024]{1,0:T(8,128)(2,1)S(1)} %get-tuple-element.126), channel_id=1, source_target_pairs={{0,52},{4,0},{16,4},{20,16},{32,20},{36,32},{48,36},{52,48},{1,53}... | collective-permute-start | bytes 786440 | tf_op jit(solution)/shard_map/ppermute | solution.py:63
  146.6 5.5 %collective-permute-done.19.up = bf16[128,1024]{1,0:T(8,128)(2,1)S(1)} collective-permute-done((bf16[128,1024]{1,0:T(8,128)(2,1)S(1)}, bf16[128,1024]{1,0:T(8,128)(2,1)S(1)}, u32[]{:S(2)}, u32[]{:S(2)}) %collective-permute-start.19) | collective-permute-done | bytes 262176 | tf_op jit(solution)/shard_map/ppermute | solution.py:63
  152.3 3.2 %collective-permute-start.22 = (bf16[128,1024]{1,0:T(8,128)(2,1)S(1)}, bf16[128,1024]{1,0:T(8,128)(2,1)S(1)}, u32[]{:S(2)}, u32[]{:S(2)}) collective-permute-start(bf16[128,1024]{1,0:T(8,128)(2,1)S(1)} %get-tuple-element.130), channel_id=1, source_target_pairs={{0,52},{4,0},{16,4},{20,16},{32,20},{36,32},{48,36},{52,48},{1,53}... | collective-permute-start | bytes 786440 | tf_op jit(solution)/shard_map/ppermute | solution.py:63
  155.6 4.7 %collective-permute-done.21.up = bf16[128,1024]{1,0:T(8,128)(2,1)S(1)} collective-permute-done((bf16[128,1024]{1,0:T(8,128)(2,1)S(1)}, bf16[128,1024]{1,0:T(8,128)(2,1)S(1)}, u32[]{:S(2)}, u32[]{:S(2)}) %collective-permute-start.21) | collective-permute-done | bytes 262176 | tf_op jit(solution)/shard_map/ppermute | solution.py:63
  160.5 3.2 %collective-permute-start.24 = (bf16[128,1024]{1,0:T(8,128)(2,1)S(1)}, bf16[128,1024]{1,0:T(8,128)(2,1)S(1)}, u32[]{:S(2)}, u32[]{:S(2)}) collective-permute-start(bf16[128,1024]{1,0:T(8,128)(2,1)S(1)} %get-tuple-element.135), channel_id=1, source_target_pairs={{0,52},{4,0},{16,4},{20,16},{32,20},{36,32},{48,36},{52,48},{1,53}... | collective-permute-start | bytes 786440 | tf_op jit(solution)/shard_map/ppermute | solution.py:63
  165.8 2.3 %collective-permute-done.23 = bf16[128,1024]{1,0:T(8,128)(2,1)S(1)} collective-permute-done((bf16[128,1024]{1,0:T(8,128)(2,1)S(1)}, bf16[128,1024]{1,0:T(8,128)(2,1)S(1)}, u32[]{:S(2)}, u32[]{:S(2)}) %collective-permute-start.23) | collective-permute-done | bytes 262176 | tf_op jit(solution)/shard_map/ppermute | solution.py:63
  (64 shorter events, 38.5 us)
Async XLA Ops:
  2.3 15.8 %collective-permute-start.1 = (bf16[128,1152]{1,0:T(8,128)(2,1)S(1)}, bf16[128,1152]{1,0:T(8,128)(2,1)S(1)}, u32[]{:S(2)}, u32[]{:S(2)}) collective-permute-start(bf16[128,1152]{1,0:T(8,128)(2,1)S(1)} %get-tuple-element.70.own), channel_id=1, source_target_pairs={{0,4},{4,16},{16,20},{20,32},{32,36},{36,48},{48,52},{52,0},{1,5},... | collective-permute-start | bytes 884744 | tf_op jit(solution)/shard_map/ppermute | solution.py:63
  4.3 13.9 %collective-permute-start = (bf16[128,1152]{1,0:T(8,128)(2,1)S(1)}, bf16[128,1152]{1,0:T(8,128)(2,1)S(1)}, u32[]{:S(2)}, u32[]{:S(2)}) collective-permute-start(bf16[128,1152]{1,0:T(8,128)(2,1)S(1)} %get-tuple-element.70.own), channel_id=1, source_target_pairs={{0,52},{4,0},{16,4},{20,16},{32,20},{36,32},{48,36},{52,48},{1,53}... | collective-permute-start | bytes 884744 | tf_op jit(solution)/shard_map/ppermute | solution.py:63
  8.4 6.4 %collective-permute-start.4 = (bf16[32,1152]{1,0:T(8,128)(2,1)S(1)}, bf16[32,1152]{1,0:T(8,128)(2,1)S(1)}, u32[]{:S(2)}, u32[]{:S(2)}) collective-permute-start(bf16[32,1152]{1,0:T(8,128)(2,1)S(1)} %get-tuple-element.71.refs_0_), channel_id=1, source_target_pairs={{3,0},{0,1},{1,2},{2,3},{7,4},{4,5},{5,6},{6,7},{11,8},{8,9},{9,10... | collective-permute-start | bytes 221192 | tf_op jit(solution)/shard_map/ppermute | solution.py:368
  9.9 6.2 %collective-permute-start.3 = (bf16[32,1152]{1,0:T(8,128)(2,1)S(1)}, bf16[32,1152]{1,0:T(8,128)(2,1)S(1)}, u32[]{:S(2)}, u32[]{:S(2)}) collective-permute-start(bf16[32,1152]{1,0:T(8,128)(2,1)S(1)} %get-tuple-element.71.refs_0_), channel_id=1, source_target_pairs={{2,0},{3,1},{0,2},{1,3},{6,4},{7,5},{4,6},{5,7},{10,8},{11,9},{8,1... | collective-permute-start | bytes 221192 | tf_op jit(solution)/shard_map/ppermute | solution.py:368
  18.2 10.1 %collective-permute-start.7 = (bf16[128,1152]{1,0:T(8,128)(2,1)S(1)}, bf16[128,1152]{1,0:T(8,128)(2,1)S(1)}, u32[]{:S(2)}, u32[]{:S(2)}) collective-permute-start(bf16[128,1152]{1,0:T(8,128)(2,1)S(1)} %shard_map.68.own), channel_id=1, source_target_pairs={{192,0},{0,64},{64,128},{128,192},{193,1},{1,65},{65,129},{129,193... | collective-permute-start | bytes 884744 | tf_op jit(solution)/shard_map/ppermute | solution.py:381
  19.8 9.2 %collective-permute-start.9 = (bf16[128,1152]{1,0:T(8,128)(2,1)S(1)}, bf16[128,1152]{1,0:T(8,128)(2,1)S(1)}, u32[]{:S(2)}, u32[]{:S(2)}) collective-permute-start(bf16[128,1152]{1,0:T(8,128)(2,1)S(1)} %collective-permute-done.1.other), channel_id=1, source_target_pairs={{0,4},{4,16},{16,20},{20,32},{32,36},{36,48},{48,52},{52,0},{1,5},... | collective-permute-start | bytes 884744 | tf_op jit(solution)/shard_map/ppermute | solution.py:63
  19.8 9.3 %collective-permute-start.11 = (bf16[128,1152]{1,0:T(8,128)(2,1)S(1)}, bf16[128,1152]{1,0:T(8,128)(2,1)S(1)}, u32[]{:S(2)}, u32[]{:S(2)}) collective-permute-start(bf16[128,1152]{1,0:T(8,128)(2,1)S(1)} %collective-permute-done.near), channel_id=1, source_target_pairs={{0,52},{4,0},{16,4},{20,16},{32,20},{36,32},{48,36},{52,48},{1,53}... | collective-permute-start | bytes 884744 | tf_op jit(solution)/shard_map/ppermute | solution.py:63
  23.0 10.2 %collective-permute-start.6 = (bf16[128,1152]{1,0:T(8,128)(2,1)S(1)}, bf16[128,1152]{1,0:T(8,128)(2,1)S(1)}, u32[]{:S(2)}, u32[]{:S(2)}) collective-permute-start(bf16[128,1152]{1,0:T(8,128)(2,1)S(1)} %shard_map.68.own), channel_id=1, source_target_pairs={{128,0},{192,64},{0,128},{64,192},{129,1},{193,65},{1,129},{65,193... | collective-permute-start | bytes 884744 | tf_op jit(solution)/shard_map/ppermute | solution.py:383
  26.0 10.0 %collective-permute-start.5 = (bf16[128,1152]{1,0:T(8,128)(2,1)S(1)}, bf16[128,1152]{1,0:T(8,128)(2,1)S(1)}, u32[]{:S(2)}, u32[]{:S(2)}) collective-permute-start(bf16[128,1152]{1,0:T(8,128)(2,1)S(1)} %shard_map.68.own), channel_id=1, source_target_pairs={{64,0},{128,64},{192,128},{0,192},{65,1},{129,65},{193,129},{1,193... | collective-permute-start | bytes 884744 | tf_op jit(solution)/shard_map/ppermute | solution.py:381
  28.2 7.7 %collective-permute-start.8 = (bf16[128,1152]{1,0:T(8,128)(2,1)S(1)}, bf16[128,1152]{1,0:T(8,128)(2,1)S(1)}, u32[]{:S(2)}, u32[]{:S(2)}) collective-permute-start(bf16[128,1152]{1,0:T(8,128)(2,1)S(1)} %collective-permute-done.7.third), channel_id=1, source_target_pairs={{200,8},{8,72},{72,136},{136,200},{201,9},{9,73},{73,137},{137,201... | collective-permute-start | bytes 884744 | tf_op jit(solution)/shard_map/ppermute | solution.py:384
  28.9 8.0 %collective-permute-start.10 = (bf16[128,1152]{1,0:T(8,128)(2,1)S(1)}, bf16[128,1152]{1,0:T(8,128)(2,1)S(1)}, u32[]{:S(2)}, u32[]{:S(2)}) collective-permute-start(bf16[128,1152]{1,0:T(8,128)(2,1)S(1)} %collective-permute-done.9.other), channel_id=1, source_target_pairs={{0,4},{4,16},{16,20},{20,32},{32,36},{36,48},{48,52},{52,0},{1,5},... | collective-permute-start | bytes 884744 | tf_op jit(solution)/shard_map/ppermute | solution.py:63
  29.0 7.9 %collective-permute-start.12 = (bf16[128,1152]{1,0:T(8,128)(2,1)S(1)}, bf16[128,1152]{1,0:T(8,128)(2,1)S(1)}, u32[]{:S(2)}, u32[]{:S(2)}) collective-permute-start(bf16[128,1152]{1,0:T(8,128)(2,1)S(1)} %collective-permute-done.11.near), channel_id=1, source_target_pairs={{0,52},{4,0},{16,4},{20,16},{32,20},{36,32},{48,36},{52,48},{1,53}... | collective-permute-start | bytes 884744 | tf_op jit(solution)/shard_map/ppermute | solution.py:63
  37.4 8.7 %collective-permute-start.14 = (bf16[64,1152]{1,0:T(8,128)(2,1)S(1)}, bf16[64,1152]{1,0:T(8,128)(2,1)S(1)}, u32[]{:S(2)}, u32[]{:S(2)}) collective-permute-start(bf16[64,1152]{1,0:T(8,128)(2,1)S(1)} %get-tuple-element.83), channel_id=1, source_target_pairs={{0,4},{4,16},{16,20},{20,32},{32,36},{36,48},{48,52},{52,0},{1,5},... | collective-permute-start | bytes 442376 | tf_op jit(solution)/shard_map/ppermute | solution.py:63
  37.5 8.6 %collective-permute-start.15 = (bf16[64,1152]{1,0:T(8,128)(2,1)S(1)}, bf16[64,1152]{1,0:T(8,128)(2,1)S(1)}, u32[]{:S(2)}, u32[]{:S(2)}) collective-permute-start(bf16[64,1152]{1,0:T(8,128)(2,1)S(1)} %get-tuple-element.84), channel_id=1, source_target_pairs={{0,52},{4,0},{16,4},{20,16},{32,20},{36,32},{48,36},{52,48},{1,53}... | collective-permute-start | bytes 442376 | tf_op jit(solution)/shard_map/ppermute | solution.py:63
  129.3 7.2 %collective-permute-start.16 = (bf16[512,1024]{1,0:T(8,128)(2,1)S(1)}, bf16[512,1024]{1,0:T(8,128)(2,1)S(1)}, u32[]{:S(2)}, u32[]{:S(2)}) collective-permute-start(bf16[512,1024]{1,0:T(8,128)(2,1)S(1)} %get-tuple-element.107), channel_id=1, source_target_pairs={{0,8},{8,0},{1,9},{9,1},{2,10},{10,2},{3,11},{11,3},{4,12},{12,4},... | collective-permute-start | bytes 3145736 | tf_op jit(solution)/shard_map/ppermute | solution.py:485
  129.5 7.0 %collective-permute-start.17 = (bf16[64,1024]{1,0:T(8,128)(2,1)S(1)}, bf16[64,1024]{1,0:T(8,128)(2,1)S(1)}, u32[]{:S(2)}, u32[]{:S(2)}) collective-permute-start(bf16[64,1024]{1,0:T(8,128)(2,1)S(1)} %get-tuple-element.108), channel_id=1, source_target_pairs={{0,4},{4,16},{16,20},{20,32},{32,36},{36,48},{48,52},{52,0},{1,5},... | collective-permute-start | bytes 393224 | tf_op jit(solution)/shard_map/ppermute | solution.py:63
  130.1 6.4 %collective-permute-start.18 = (bf16[64,1024]{1,0:T(8,128)(2,1)S(1)}, bf16[64,1024]{1,0:T(8,128)(2,1)S(1)}, u32[]{:S(2)}, u32[]{:S(2)}) collective-permute-start(bf16[64,1024]{1,0:T(8,128)(2,1)S(1)} %get-tuple-element.109), channel_id=1, source_target_pairs={{0,52},{4,0},{16,4},{20,16},{32,20},{36,32},{48,36},{52,48},{1,53}... | collective-permute-start | bytes 393224 | tf_op jit(solution)/shard_map/ppermute | solution.py:63
  137.6 22.8 %all-to-all-start.6 = ((bf16[16,32,1024]{2,1,0:T(8,128)(2,1)}), bf16[16,32,1024]{2,1,0:T(8,128)(2,1)}, u32[]{:S(2)}, u32[]{:S(2)}) async-start(bf16[16,32,1024]{2,1,0:T(8,128)(2,1)} %bitcast.9), calls=%async_computation.6 | async-start | bytes 2097152 | tf_op jit(solution)/shard_map/all_to_all | solution.py:492
  143.3 8.9 %collective-permute-start.19 = (bf16[128,1024]{1,0:T(8,128)(2,1)S(1)}, bf16[128,1024]{1,0:T(8,128)(2,1)S(1)}, u32[]{:S(2)}, u32[]{:S(2)}) collective-permute-start(bf16[128,1024]{1,0:T(8,128)(2,1)S(1)} %get-tuple-element.124), channel_id=1, source_target_pairs={{0,4},{4,16},{16,20},{20,32},{32,36},{36,48},{48,52},{52,0},{1,5},... | collective-permute-start | bytes 786440 | tf_op jit(solution)/shard_map/ppermute | solution.py:63
  143.4 8.7 %collective-permute-start.20 = (bf16[128,1024]{1,0:T(8,128)(2,1)S(1)}, bf16[128,1024]{1,0:T(8,128)(2,1)S(1)}, u32[]{:S(2)}, u32[]{:S(2)}) collective-permute-start(bf16[128,1024]{1,0:T(8,128)(2,1)S(1)} %get-tuple-element.126), channel_id=1, source_target_pairs={{0,52},{4,0},{16,4},{20,16},{32,20},{36,32},{48,36},{52,48},{1,53}... | collective-permute-start | bytes 786440 | tf_op jit(solution)/shard_map/ppermute | solution.py:63
  152.3 8.0 %collective-permute-start.21 = (bf16[128,1024]{1,0:T(8,128)(2,1)S(1)}, bf16[128,1024]{1,0:T(8,128)(2,1)S(1)}, u32[]{:S(2)}, u32[]{:S(2)}) collective-permute-start(bf16[128,1024]{1,0:T(8,128)(2,1)S(1)} %get-tuple-element.128), channel_id=1, source_target_pairs={{0,4},{4,16},{16,20},{20,32},{32,36},{36,48},{48,52},{52,0},{1,5},... | collective-permute-start | bytes 786440 | tf_op jit(solution)/shard_map/ppermute | solution.py:63
  152.3 8.0 %collective-permute-start.22 = (bf16[128,1024]{1,0:T(8,128)(2,1)S(1)}, bf16[128,1024]{1,0:T(8,128)(2,1)S(1)}, u32[]{:S(2)}, u32[]{:S(2)}) collective-permute-start(bf16[128,1024]{1,0:T(8,128)(2,1)S(1)} %get-tuple-element.130), channel_id=1, source_target_pairs={{0,52},{4,0},{16,4},{20,16},{32,20},{36,32},{48,36},{52,48},{1,53}... | collective-permute-start | bytes 786440 | tf_op jit(solution)/shard_map/ppermute | solution.py:63
  160.4 7.7 %collective-permute-start.23 = (bf16[128,1024]{1,0:T(8,128)(2,1)S(1)}, bf16[128,1024]{1,0:T(8,128)(2,1)S(1)}, u32[]{:S(2)}, u32[]{:S(2)}) collective-permute-start(bf16[128,1024]{1,0:T(8,128)(2,1)S(1)} %get-tuple-element.134), channel_id=1, source_target_pairs={{0,4},{4,16},{16,20},{20,32},{32,36},{36,48},{48,52},{52,0},{1,5},... | collective-permute-start | bytes 786440 | tf_op jit(solution)/shard_map/ppermute | solution.py:63
  160.5 7.6 %collective-permute-start.24 = (bf16[128,1024]{1,0:T(8,128)(2,1)S(1)}, bf16[128,1024]{1,0:T(8,128)(2,1)S(1)}, u32[]{:S(2)}, u32[]{:S(2)}) collective-permute-start(bf16[128,1024]{1,0:T(8,128)(2,1)S(1)} %get-tuple-element.135), channel_id=1, source_target_pairs={{0,52},{4,0},{16,4},{20,16},{32,20},{36,32},{48,36},{52,48},{1,53}... | collective-permute-start | bytes 786440 | tf_op jit(solution)/shard_map/ppermute | solution.py:63
  (5 other events, 59.8 us)

commit v8 on v7

--- a/solution.py
+++ b/solution.py
@@ -118,15 +118,24 @@
         out.at[pl.ds(pl.multiple_of(lax.rem(offsets[4] + k, 4) * rows, rows), rows)] for k in range(4)
     ]
 
+    rest = [
+        pltpu.make_async_copy(block, places[k], sems.at[n])
+        for n, (k, block) in enumerate(((0, own), (1, first), (3, third)))
+    ]
+    for copy in rest:
+        copy.start()
+
     @pl.when(offsets[1] == 0)
     def _():
-        copy_all([(second, places[2])], sems)
+        pltpu.make_async_copy(second, places[2], sems.at[3]).start()
 
     @pl.when(offsets[1] != 0)
     def _():
-        copy_all([(relayed, places[2])], sems)
-
-    copy_all([(own, places[0]), (first, places[1]), (third, places[3])], sems)
+        pltpu.make_async_copy(relayed, places[2], sems.at[3]).start()
+
+    for copy in rest:
+        copy.wait()
+    pltpu.make_async_copy(second, places[2], sems.at[3]).wait()
 
 
 def columns_sums(tables, added):
@@ -176,9 +185,9 @@
     return jnp.concatenate([order[pl.ds(lax.rem(at + offset, 8), 1), :] for at in table])
 
 
-def spread(pots, wide):
+def spread(pots, wide, lines=range(8)):
     columns = pots.T
-    for c in range(8):
+    for c in lines:
         wide[c * LANES : (c + 1) * LANES, :] = jnp.broadcast_to(
             columns[:, c : c + 1], (LANES, LANES)
         )
@@ -263,7 +272,8 @@
         tgt = merge(tgt_pots, log_count, offsets[1], range(8), order)
         outs[-1][...] = tgt
         outs = outs[:-1]
-    spread(src_pots[...], wide)
+    lines = [c for _, n_rows, at in pieces for c in range(at // LANES, (at + n_rows) // LANES)]
+    spread(src_pots[...], wide, lines)
     outs = list(outs)
     for (first, rows, place), table in zip(pieces, tables):
         at = slice(place, place + rows)
@@ -383,7 +393,7 @@
     second = lax.ppermute(block, ("x", "core"), pairs_of(2, 0))
     relayed = lax.ppermute(third, ("x", "core"), pairs_of(3, 1))
     (mine,) = call(
-        assemble_relayed_kernel, [jax.ShapeDtypeStruct((plane * columns, n_label), bf16)], [dma((3,))],
+        assemble_relayed_kernel, [jax.ShapeDtypeStruct((plane * columns, n_label), bf16)], [dma((4,))],
         offsets, block, first, second, third, relayed, smem=1, flops=1, bytes_accessed=2**20,
     )
     pairs.append((down, up))

time: 170 us -> 170 us (level)
  no operation moved by 1% of the time
where the time goes in v8:
time: 170 us
  blocking collectives  69.5 us (41%)
  starting transfers between devices  48.4 us (28%)
  Pallas kernels  26.7 us (16%)
  waiting for transfers between devices  20.4 us (12%)
  other arithmetic  3.52 us (2%)
    all_to_all x3, blocking collectives, shards(): gathered = lax.all_to_all(part, SPREAD, 0, 0)  35.2 us
    all_to_all x3, blocking collectives, shards(): gathered = lax.all_to_all(part, RING, 0, 0)  34.4 us
    ppermute x16, starting transfers between devices, shift(): lax.ppermute(value, RING, [(i, (i + step) % size) for i in range(size)])  29.3 us
    pallas_call x21, Pallas kernels, call(): pl.pallas_call(kernel, out_shape=outs, in_specs=specs, out_specs=[IN_HBM...  26.7 us
    ppermute x16, waiting for transfers between devices, shift(): lax.ppermute(value, RING, [(i, (i + step) % size) for i in range(size)])  13.6 us
    ppermute x3, starting transfers between devices, gather_axis(): lax.ppermute(block, axis, [((i + k) % size, i) for i in range(size)])  5.83 us
    all_to_all x1, starting transfers between devices, shards(): parts = lax.all_to_all(sent.reshape(plane, columns, depth), PLANE, 0, 0)  5.58 us
    ppermute x2, starting transfers between devices, shards(): lax.ppermute(block, 'x', [((i + k) % 4, i) for i in range(4)])  3.8 us
  transfers between devices with their start and end apart: 26, of which 10 were waited for; matrix products, arithmetic and copies ran while one was open for 1% of the time, Pallas kernels for 6%

profile of v8, /device:TPU:2, one launch (start us, length us, event | category | flops | bytes accessed | tf_op | source)
XLA Modules:
  0.0 169.5 jit_solution(12481309062437213579)
XLA Ops:
  4.3 4.0 %collective-permute-start = (bf16[128,1152]{1,0:T(8,128)(2,1)S(1)}, bf16[128,1152]{1,0:T(8,128)(2,1)S(1)}, u32[]{:S(2)}, u32[]{:S(2)}) collective-permute-start(bf16[128,1152]{1,0:T(8,128)(2,1)S(1)} %get-tuple-element.70.own), channel_id=1, source_target_pairs={{0,52},{4,0},{16,4},{20,16},{32,20},{36,32},{48,36},{52,48},{1,53}... | collective-permute-start | bytes 884744 | tf_op jit(solution)/shard_map/ppermute | solution.py:63
  9.9 2.9 %collective-permute-start.3 = (bf16[32,1152]{1,0:T(8,128)(2,1)S(1)}, bf16[32,1152]{1,0:T(8,128)(2,1)S(1)}, u32[]{:S(2)}, u32[]{:S(2)}) collective-permute-start(bf16[32,1152]{1,0:T(8,128)(2,1)S(1)} %get-tuple-element.71.refs_0_), channel_id=1, source_target_pairs={{2,0},{3,1},{0,2},{1,3},{6,4},{7,5},{4,6},{5,7},{10,8},{11,9},{8,1... | collective-permute-start | bytes 221192 | tf_op jit(solution)/shard_map/ppermute | solution.py:378
  19.8 3.2 %collective-permute-start.11 = (bf16[128,1152]{1,0:T(8,128)(2,1)S(1)}, bf16[128,1152]{1,0:T(8,128)(2,1)S(1)}, u32[]{:S(2)}, u32[]{:S(2)}) collective-permute-start(bf16[128,1152]{1,0:T(8,128)(2,1)S(1)} %collective-permute-done.near), channel_id=1, source_target_pairs={{0,52},{4,0},{16,4},{20,16},{32,20},{36,32},{48,36},{52,48},{1,53}... | collective-permute-start | bytes 884744 | tf_op jit(solution)/shard_map/ppermute | solution.py:63
  23.0 3.0 %collective-permute-start.6 = (bf16[128,1152]{1,0:T(8,128)(2,1)S(1)}, bf16[128,1152]{1,0:T(8,128)(2,1)S(1)}, u32[]{:S(2)}, u32[]{:S(2)}) collective-permute-start(bf16[128,1152]{1,0:T(8,128)(2,1)S(1)} %shard_map.68.own), channel_id=1, source_target_pairs={{128,0},{192,64},{0,128},{64,192},{129,1},{193,65},{1,129},{65,193... | collective-permute-start | bytes 884744 | tf_op jit(solution)/shard_map/ppermute | solution.py:393
  26.0 2.2 %collective-permute-start.5 = (bf16[128,1152]{1,0:T(8,128)(2,1)S(1)}, bf16[128,1152]{1,0:T(8,128)(2,1)S(1)}, u32[]{:S(2)}, u32[]{:S(2)}) collective-permute-start(bf16[128,1152]{1,0:T(8,128)(2,1)S(1)} %shard_map.68.own), channel_id=1, source_target_pairs={{64,0},{128,64},{192,128},{0,192},{65,1},{129,65},{193,129},{1,193... | collective-permute-start | bytes 884744 | tf_op jit(solution)/shard_map/ppermute | solution.py:391
  29.0 3.2 %collective-permute-start.12 = (bf16[128,1152]{1,0:T(8,128)(2,1)S(1)}, bf16[128,1152]{1,0:T(8,128)(2,1)S(1)}, u32[]{:S(2)}, u32[]{:S(2)}) collective-permute-start(bf16[128,1152]{1,0:T(8,128)(2,1)S(1)} %collective-permute-done.11.near), channel_id=1, source_target_pairs={{0,52},{4,0},{16,4},{20,16},{32,20},{36,32},{48,36},{52,48},{1,53}... | collective-permute-start | bytes 884744 | tf_op jit(solution)/shard_map/ppermute | solution.py:63
  33.2 2.8 %collective-permute-done.5.first = bf16[128,1152]{1,0:T(8,128)(2,1)S(1)} collective-permute-done((bf16[128,1152]{1,0:T(8,128)(2,1)S(1)}, bf16[128,1152]{1,0:T(8,128)(2,1)S(1)}, u32[]{:S(2)}, u32[]{:S(2)}) %collective-permute-start.5) | collective-permute-done | bytes 294944 | tf_op jit(solution)/shard_map/ppermute | solution.py:391
  37.5 3.5 %collective-permute-start.15 = (bf16[64,1152]{1,0:T(8,128)(2,1)S(1)}, bf16[64,1152]{1,0:T(8,128)(2,1)S(1)}, u32[]{:S(2)}, u32[]{:S(2)}) collective-permute-start(bf16[64,1152]{1,0:T(8,128)(2,1)S(1)} %get-tuple-element.84), channel_id=1, source_target_pairs={{0,52},{4,0},{16,4},{20,16},{32,20},{36,32},{48,36},{52,48},{1,53}... | collective-permute-start | bytes 442376 | tf_op jit(solution)/shard_map/ppermute | solution.py:63
  47.9 13.6 %all_to_all.35.refs_5_ = f32[8,8,128]{2,1,0:T(8,128)S(1)} all-to-all(f32[8,8,128]{2,1,0:T(8,128)S(1)} %get-tuple-element.95), channel_id=1, replica_groups=mesh['x'=4,'zh'=4,'core'=2,'zl'=2,'y'=4] {'zh','zl'}, dimensions={0} | all-to-all | bytes 65536 | tf_op jit(solution)/shard_map/all_to_all | solution.py:459
  63.2 12.6 %all_to_all.36.refs_5_ = f32[32,8,128]{2,1,0:T(8,128)S(1)} all-to-all(f32[32,8,128]{2,1,0:T(8,128)S(1)} %get-tuple-element.96), channel_id=1, replica_groups=mesh['x'=4,'zh'=4,'core'=2,'zl'=2,'y'=4] {'x','y','core'}, dimensions={0} | all-to-all | bytes 262144 | tf_op jit(solution)/shard_map/all_to_all | solution.py:465
  77.4 10.4 %all_to_all.37.refs_5_ = f32[8,8,128]{2,1,0:T(8,128)S(1)} all-to-all(f32[8,8,128]{2,1,0:T(8,128)S(1)} %shard_map.77), channel_id=1, replica_groups=mesh['x'=4,'zh'=4,'core'=2,'zl'=2,'y'=4] {'zh','zl'}, dimensions={0} | all-to-all | bytes 65536 | tf_op jit(solution)/shard_map/all_to_all | solution.py:459
  89.5 11.3 %all_to_all.38.refs_5_ = f32[32,8,128]{2,1,0:T(8,128)S(1)} all-to-all(f32[32,8,128]{2,1,0:T(8,128)S(1)} %get-tuple-element.97), channel_id=1, replica_groups=mesh['x'=4,'zh'=4,'core'=2,'zl'=2,'y'=4] {'x','y','core'}, dimensions={0} | all-to-all | bytes 262144 | tf_op jit(solution)/shard_map/all_to_all | solution.py:465
  102.4 10.4 %all_to_all.39.refs_5_ = f32[8,8,128]{2,1,0:T(8,128)S(1)} all-to-all(f32[8,8,128]{2,1,0:T(8,128)S(1)} %shard_map.79), channel_id=1, replica_groups=mesh['x'=4,'zh'=4,'core'=2,'zl'=2,'y'=4] {'zh','zl'}, dimensions={0} | all-to-all | bytes 65536 | tf_op jit(solution)/shard_map/all_to_all | solution.py:459
  114.4 11.3 %all_to_all.40.refs_1_ = f32[32,8,128]{2,1,0:T(8,128)S(1)} all-to-all(f32[32,8,128]{2,1,0:T(8,128)S(1)} %get-tuple-element.98), channel_id=1, replica_groups=mesh['x'=4,'zh'=4,'core'=2,'zl'=2,'y'=4] {'x','y','core'}, dimensions={0} | all-to-all | bytes 262144 | tf_op jit(solution)/shard_map/all_to_all | solution.py:465
  126.9 2.5 %shard_map.82 = (f32[512,1024]{1,0:T(8,128)S(1)}, bf16[512,1024]{1,0:T(8,128)(2,1)S(1)}) custom-call(f32[1024,256]{1,0:T(8,128)S(1)} %get-tuple-element.76.refs_0_, f32[1024,256]{1,0:T(8,128)S(1)} %get-tuple-element.78.refs_1_, f32[1024,256]{1,0:T(8,128)S(1)} %get-tuple-element.81.refs_2_, f32[1024,128]{1,0:T(8,128)S(1)} %get-tuple-element.82.refs_3_, ...), custom_call_target="tpu_custom_call" | custom-call | flops 2147483648 | bytes 8388608 | tf_op jit(solution)/shard_map/pallas_call | solution.py:48
  130.1 2.7 %collective-permute-start.18 = (bf16[64,1024]{1,0:T(8,128)(2,1)S(1)}, bf16[64,1024]{1,0:T(8,128)(2,1)S(1)}, u32[]{:S(2)}, u32[]{:S(2)}) collective-permute-start(bf16[64,1024]{1,0:T(8,128)(2,1)S(1)} %get-tuple-element.109), channel_id=1, source_target_pairs={{0,52},{4,0},{16,4},{20,16},{32,20},{36,32},{48,36},{52,48},{1,53}... | collective-permute-start | bytes 393224 | tf_op jit(solution)/shard_map/ppermute | solution.py:63
  132.8 2.8 %shard_map.83 = (f32[128,1024]{1,0:T(8,128)S(1)}, f32[128,1024]{1,0:T(8,128)S(1)}, f32[128,1024]{1,0:T(8,128)S(1)}, f32[128,1024]{1,0:T(8,128)S(1)}, f32[128,102...) custom-call(s32[6]{0:T(128)S(1)} %stack.27.offsets, f32[256,1024]{1,0:T(8,128)S(1)} %get-tuple-element.91.refs_0_, ...), custom_call_target="tpu_custom_call" | custom-call | flops 536870912 | bytes 4194304 | tf_op jit(solution)/shard_map/pallas_call | solution.py:48
  137.6 5.6 %all-to-all-start.6 = ((bf16[16,32,1024]{2,1,0:T(8,128)(2,1)}), bf16[16,32,1024]{2,1,0:T(8,128)(2,1)}, u32[]{:S(2)}, u32[]{:S(2)}) async-start(bf16[16,32,1024]{2,1,0:T(8,128)(2,1)} %bitcast.9), calls=%async_computation.6 | async-start | bytes 2097152 | tf_op jit(solution)/shard_map/all_to_all | solution.py:502
  143.4 3.2 %collective-permute-start.20 = (bf16[128,1024]{1,0:T(8,128)(2,1)S(1)}, bf16[128,1024]{1,0:T(8,128)(2,1)S(1)}, u32[]{:S(2)}, u32[]{:S(2)}) collective-permute-start(bf16[128,1024]{1,0:T(8,128)(2,1)S(1)} %get-tuple-element.126), channel_id=1, source_target_pairs={{0,52},{4,0},{16,4},{20,16},{32,20},{36,32},{48,36},{52,48},{1,53}... | collective-permute-start | bytes 786440 | tf_op jit(solution)/shard_map/ppermute | solution.py:63
  146.6 5.5 %collective-permute-done.19.up = bf16[128,1024]{1,0:T(8,128)(2,1)S(1)} collective-permute-done((bf16[128,1024]{1,0:T(8,128)(2,1)S(1)}, bf16[128,1024]{1,0:T(8,128)(2,1)S(1)}, u32[]{:S(2)}, u32[]{:S(2)}) %collective-permute-start.19) | collective-permute-done | bytes 262176 | tf_op jit(solution)/shard_map/ppermute | solution.py:63
  152.3 3.2 %collective-permute-start.22 = (bf16[128,1024]{1,0:T(8,128)(2,1)S(1)}, bf16[128,1024]{1,0:T(8,128)(2,1)S(1)}, u32[]{:S(2)}, u32[]{:S(2)}) collective-permute-start(bf16[128,1024]{1,0:T(8,128)(2,1)S(1)} %get-tuple-element.130), channel_id=1, source_target_pairs={{0,52},{4,0},{16,4},{20,16},{32,20},{36,32},{48,36},{52,48},{1,53}... | collective-permute-start | bytes 786440 | tf_op jit(solution)/shard_map/ppermute | solution.py:63
  155.6 4.7 %collective-permute-done.21.up = bf16[128,1024]{1,0:T(8,128)(2,1)S(1)} collective-permute-done((bf16[128,1024]{1,0:T(8,128)(2,1)S(1)}, bf16[128,1024]{1,0:T(8,128)(2,1)S(1)}, u32[]{:S(2)}, u32[]{:S(2)}) %collective-permute-start.21) | collective-permute-done | bytes 262176 | tf_op jit(solution)/shard_map/ppermute | solution.py:63
  160.5 3.2 %collective-permute-start.24 = (bf16[128,1024]{1,0:T(8,128)(2,1)S(1)}, bf16[128,1024]{1,0:T(8,128)(2,1)S(1)}, u32[]{:S(2)}, u32[]{:S(2)}) collective-permute-start(bf16[128,1024]{1,0:T(8,128)(2,1)S(1)} %get-tuple-element.135), channel_id=1, source_target_pairs={{0,52},{4,0},{16,4},{20,16},{32,20},{36,32},{48,36},{52,48},{1,53}... | collective-permute-start | bytes 786440 | tf_op jit(solution)/shard_map/ppermute | solution.py:63
  165.8 2.3 %collective-permute-done.23 = bf16[128,1024]{1,0:T(8,128)(2,1)S(1)} collective-permute-done((bf16[128,1024]{1,0:T(8,128)(2,1)S(1)}, bf16[128,1024]{1,0:T(8,128)(2,1)S(1)}, u32[]{:S(2)}, u32[]{:S(2)}) %collective-permute-start.23) | collective-permute-done | bytes 262176 | tf_op jit(solution)/shard_map/ppermute | solution.py:63
  (64 shorter events, 38.5 us)
Async XLA Ops:
  2.3 15.8 %collective-permute-start.1 = (bf16[128,1152]{1,0:T(8,128)(2,1)S(1)}, bf16[128,1152]{1,0:T(8,128)(2,1)S(1)}, u32[]{:S(2)}, u32[]{:S(2)}) collective-permute-start(bf16[128,1152]{1,0:T(8,128)(2,1)S(1)} %get-tuple-element.70.own), channel_id=1, source_target_pairs={{0,4},{4,16},{16,20},{20,32},{32,36},{36,48},{48,52},{52,0},{1,5},... | collective-permute-start | bytes 884744 | tf_op jit(solution)/shard_map/ppermute | solution.py:63
  4.3 13.9 %collective-permute-start = (bf16[128,1152]{1,0:T(8,128)(2,1)S(1)}, bf16[128,1152]{1,0:T(8,128)(2,1)S(1)}, u32[]{:S(2)}, u32[]{:S(2)}) collective-permute-start(bf16[128,1152]{1,0:T(8,128)(2,1)S(1)} %get-tuple-element.70.own), channel_id=1, source_target_pairs={{0,52},{4,0},{16,4},{20,16},{32,20},{36,32},{48,36},{52,48},{1,53}... | collective-permute-start | bytes 884744 | tf_op jit(solution)/shard_map/ppermute | solution.py:63
  8.4 6.4 %collective-permute-start.4 = (bf16[32,1152]{1,0:T(8,128)(2,1)S(1)}, bf16[32,1152]{1,0:T(8,128)(2,1)S(1)}, u32[]{:S(2)}, u32[]{:S(2)}) collective-permute-start(bf16[32,1152]{1,0:T(8,128)(2,1)S(1)} %get-tuple-element.71.refs_0_), channel_id=1, source_target_pairs={{3,0},{0,1},{1,2},{2,3},{7,4},{4,5},{5,6},{6,7},{11,8},{8,9},{9,10... | collective-permute-start | bytes 221192 | tf_op jit(solution)/shard_map/ppermute | solution.py:378
  9.9 6.2 %collective-permute-start.3 = (bf16[32,1152]{1,0:T(8,128)(2,1)S(1)}, bf16[32,1152]{1,0:T(8,128)(2,1)S(1)}, u32[]{:S(2)}, u32[]{:S(2)}) collective-permute-start(bf16[32,1152]{1,0:T(8,128)(2,1)S(1)} %get-tuple-element.71.refs_0_), channel_id=1, source_target_pairs={{2,0},{3,1},{0,2},{1,3},{6,4},{7,5},{4,6},{5,7},{10,8},{11,9},{8,1... | collective-permute-start | bytes 221192 | tf_op jit(solution)/shard_map/ppermute | solution.py:378
  18.2 10.1 %collective-permute-start.7 = (bf16[128,1152]{1,0:T(8,128)(2,1)S(1)}, bf16[128,1152]{1,0:T(8,128)(2,1)S(1)}, u32[]{:S(2)}, u32[]{:S(2)}) collective-permute-start(bf16[128,1152]{1,0:T(8,128)(2,1)S(1)} %shard_map.68.own), channel_id=1, source_target_pairs={{192,0},{0,64},{64,128},{128,192},{193,1},{1,65},{65,129},{129,193... | collective-permute-start | bytes 884744 | tf_op jit(solution)/shard_map/ppermute | solution.py:391
  19.8 9.2 %collective-permute-start.9 = (bf16[128,1152]{1,0:T(8,128)(2,1)S(1)}, bf16[128,1152]{1,0:T(8,128)(2,1)S(1)}, u32[]{:S(2)}, u32[]{:S(2)}) collective-permute-start(bf16[128,1152]{1,0:T(8,128)(2,1)S(1)} %collective-permute-done.1.other), channel_id=1, source_target_pairs={{0,4},{4,16},{16,20},{20,32},{32,36},{36,48},{48,52},{52,0},{1,5},... | collective-permute-start | bytes 884744 | tf_op jit(solution)/shard_map/ppermute | solution.py:63
  19.8 9.3 %collective-permute-start.11 = (bf16[128,1152]{1,0:T(8,128)(2,1)S(1)}, bf16[128,1152]{1,0:T(8,128)(2,1)S(1)}, u32[]{:S(2)}, u32[]{:S(2)}) collective-permute-start(bf16[128,1152]{1,0:T(8,128)(2,1)S(1)} %collective-permute-done.near), channel_id=1, source_target_pairs={{0,52},{4,0},{16,4},{20,16},{32,20},{36,32},{48,36},{52,48},{1,53}... | collective-permute-start | bytes 884744 | tf_op jit(solution)/shard_map/ppermute | solution.py:63
  23.0 10.2 %collective-permute-start.6 = (bf16[128,1152]{1,0:T(8,128)(2,1)S(1)}, bf16[128,1152]{1,0:T(8,128)(2,1)S(1)}, u32[]{:S(2)}, u32[]{:S(2)}) collective-permute-start(bf16[128,1152]{1,0:T(8,128)(2,1)S(1)} %shard_map.68.own), channel_id=1, source_target_pairs={{128,0},{192,64},{0,128},{64,192},{129,1},{193,65},{1,129},{65,193... | collective-permute-start | bytes 884744 | tf_op jit(solution)/shard_map/ppermute | solution.py:393
  26.0 10.0 %collective-permute-start.5 = (bf16[128,1152]{1,0:T(8,128)(2,1)S(1)}, bf16[128,1152]{1,0:T(8,128)(2,1)S(1)}, u32[]{:S(2)}, u32[]{:S(2)}) collective-permute-start(bf16[128,1152]{1,0:T(8,128)(2,1)S(1)} %shard_map.68.own), channel_id=1, source_target_pairs={{64,0},{128,64},{192,128},{0,192},{65,1},{129,65},{193,129},{1,193... | collective-permute-start | bytes 884744 | tf_op jit(solution)/shard_map/ppermute | solution.py:391
  28.2 7.7 %collective-permute-start.8 = (bf16[128,1152]{1,0:T(8,128)(2,1)S(1)}, bf16[128,1152]{1,0:T(8,128)(2,1)S(1)}, u32[]{:S(2)}, u32[]{:S(2)}) collective-permute-start(bf16[128,1152]{1,0:T(8,128)(2,1)S(1)} %collective-permute-done.7.third), channel_id=1, source_target_pairs={{200,8},{8,72},{72,136},{136,200},{201,9},{9,73},{73,137},{137,201... | collective-permute-start | bytes 884744 | tf_op jit(solution)/shard_map/ppermute | solution.py:394
  28.9 8.0 %collective-permute-start.10 = (bf16[128,1152]{1,0:T(8,128)(2,1)S(1)}, bf16[128,1152]{1,0:T(8,128)(2,1)S(1)}, u32[]{:S(2)}, u32[]{:S(2)}) collective-permute-start(bf16[128,1152]{1,0:T(8,128)(2,1)S(1)} %collective-permute-done.9.other), channel_id=1, source_target_pairs={{0,4},{4,16},{16,20},{20,32},{32,36},{36,48},{48,52},{52,0},{1,5},... | collective-permute-start | bytes 884744 | tf_op jit(solution)/shard_map/ppermute | solution.py:63
  29.0 7.9 %collective-permute-start.12 = (bf16[128,1152]{1,0:T(8,128)(2,1)S(1)}, bf16[128,1152]{1,0:T(8,128)(2,1)S(1)}, u32[]{:S(2)}, u32[]{:S(2)}) collective-permute-start(bf16[128,1152]{1,0:T(8,128)(2,1)S(1)} %collective-permute-done.11.near), channel_id=1, source_target_pairs={{0,52},{4,0},{16,4},{20,16},{32,20},{36,32},{48,36},{52,48},{1,53}... | collective-permute-start | bytes 884744 | tf_op jit(solution)/shard_map/ppermute | solution.py:63
  37.4 8.7 %collective-permute-start.14 = (bf16[64,1152]{1,0:T(8,128)(2,1)S(1)}, bf16[64,1152]{1,0:T(8,128)(2,1)S(1)}, u32[]{:S(2)}, u32[]{:S(2)}) collective-permute-start(bf16[64,1152]{1,0:T(8,128)(2,1)S(1)} %get-tuple-element.83), channel_id=1, source_target_pairs={{0,4},{4,16},{16,20},{20,32},{32,36},{36,48},{48,52},{52,0},{1,5},... | collective-permute-start | bytes 442376 | tf_op jit(solution)/shard_map/ppermute | solution.py:63
  37.5 8.6 %collective-permute-start.15 = (bf16[64,1152]{1,0:T(8,128)(2,1)S(1)}, bf16[64,1152]{1,0:T(8,128)(2,1)S(1)}, u32[]{:S(2)}, u32[]{:S(2)}) collective-permute-start(bf16[64,1152]{1,0:T(8,128)(2,1)S(1)} %get-tuple-element.84), channel_id=1, source_target_pairs={{0,52},{4,0},{16,4},{20,16},{32,20},{36,32},{48,36},{52,48},{1,53}... | collective-permute-start | bytes 442376 | tf_op jit(solution)/shard_map/ppermute | solution.py:63
  129.3 7.2 %collective-permute-start.16 = (bf16[512,1024]{1,0:T(8,128)(2,1)S(1)}, bf16[512,1024]{1,0:T(8,128)(2,1)S(1)}, u32[]{:S(2)}, u32[]{:S(2)}) collective-permute-start(bf16[512,1024]{1,0:T(8,128)(2,1)S(1)} %get-tuple-element.107), channel_id=1, source_target_pairs={{0,8},{8,0},{1,9},{9,1},{2,10},{10,2},{3,11},{11,3},{4,12},{12,4},... | collective-permute-start | bytes 3145736 | tf_op jit(solution)/shard_map/ppermute | solution.py:495
  129.5 7.0 %collective-permute-start.17 = (bf16[64,1024]{1,0:T(8,128)(2,1)S(1)}, bf16[64,1024]{1,0:T(8,128)(2,1)S(1)}, u32[]{:S(2)}, u32[]{:S(2)}) collective-permute-start(bf16[64,1024]{1,0:T(8,128)(2,1)S(1)} %get-tuple-element.108), channel_id=1, source_target_pairs={{0,4},{4,16},{16,20},{20,32},{32,36},{36,48},{48,52},{52,0},{1,5},... | collective-permute-start | bytes 393224 | tf_op jit(solution)/shard_map/ppermute | solution.py:63
  130.1 6.4 %collective-permute-start.18 = (bf16[64,1024]{1,0:T(8,128)(2,1)S(1)}, bf16[64,1024]{1,0:T(8,128)(2,1)S(1)}, u32[]{:S(2)}, u32[]{:S(2)}) collective-permute-start(bf16[64,1024]{1,0:T(8,128)(2,1)S(1)} %get-tuple-element.109), channel_id=1, source_target_pairs={{0,52},{4,0},{16,4},{20,16},{32,20},{36,32},{48,36},{52,48},{1,53}... | collective-permute-start | bytes 393224 | tf_op jit(solution)/shard_map/ppermute | solution.py:63
  137.6 22.8 %all-to-all-start.6 = ((bf16[16,32,1024]{2,1,0:T(8,128)(2,1)}), bf16[16,32,1024]{2,1,0:T(8,128)(2,1)}, u32[]{:S(2)}, u32[]{:S(2)}) async-start(bf16[16,32,1024]{2,1,0:T(8,128)(2,1)} %bitcast.9), calls=%async_computation.6 | async-start | bytes 2097152 | tf_op jit(solution)/shard_map/all_to_all | solution.py:502
  143.3 8.9 %collective-permute-start.19 = (bf16[128,1024]{1,0:T(8,128)(2,1)S(1)}, bf16[128,1024]{1,0:T(8,128)(2,1)S(1)}, u32[]{:S(2)}, u32[]{:S(2)}) collective-permute-start(bf16[128,1024]{1,0:T(8,128)(2,1)S(1)} %get-tuple-element.124), channel_id=1, source_target_pairs={{0,4},{4,16},{16,20},{20,32},{32,36},{36,48},{48,52},{52,0},{1,5},... | collective-permute-start | bytes 786440 | tf_op jit(solution)/shard_map/ppermute | solution.py:63
  143.4 8.7 %collective-permute-start.20 = (bf16[128,1024]{1,0:T(8,128)(2,1)S(1)}, bf16[128,1024]{1,0:T(8,128)(2,1)S(1)}, u32[]{:S(2)}, u32[]{:S(2)}) collective-permute-start(bf16[128,1024]{1,0:T(8,128)(2,1)S(1)} %get-tuple-element.126), channel_id=1, source_target_pairs={{0,52},{4,0},{16,4},{20,16},{32,20},{36,32},{48,36},{52,48},{1,53}... | collective-permute-start | bytes 786440 | tf_op jit(solution)/shard_map/ppermute | solution.py:63
  152.3 8.0 %collective-permute-start.21 = (bf16[128,1024]{1,0:T(8,128)(2,1)S(1)}, bf16[128,1024]{1,0:T(8,128)(2,1)S(1)}, u32[]{:S(2)}, u32[]{:S(2)}) collective-permute-start(bf16[128,1024]{1,0:T(8,128)(2,1)S(1)} %get-tuple-element.128), channel_id=1, source_target_pairs={{0,4},{4,16},{16,20},{20,32},{32,36},{36,48},{48,52},{52,0},{1,5},... | collective-permute-start | bytes 786440 | tf_op jit(solution)/shard_map/ppermute | solution.py:63
  152.3 8.0 %collective-permute-start.22 = (bf16[128,1024]{1,0:T(8,128)(2,1)S(1)}, bf16[128,1024]{1,0:T(8,128)(2,1)S(1)}, u32[]{:S(2)}, u32[]{:S(2)}) collective-permute-start(bf16[128,1024]{1,0:T(8,128)(2,1)S(1)} %get-tuple-element.130), channel_id=1, source_target_pairs={{0,52},{4,0},{16,4},{20,16},{32,20},{36,32},{48,36},{52,48},{1,53}... | collective-permute-start | bytes 786440 | tf_op jit(solution)/shard_map/ppermute | solution.py:63
  160.4 7.7 %collective-permute-start.23 = (bf16[128,1024]{1,0:T(8,128)(2,1)S(1)}, bf16[128,1024]{1,0:T(8,128)(2,1)S(1)}, u32[]{:S(2)}, u32[]{:S(2)}) collective-permute-start(bf16[128,1024]{1,0:T(8,128)(2,1)S(1)} %get-tuple-element.134), channel_id=1, source_target_pairs={{0,4},{4,16},{16,20},{20,32},{32,36},{36,48},{48,52},{52,0},{1,5},... | collective-permute-start | bytes 786440 | tf_op jit(solution)/shard_map/ppermute | solution.py:63
  160.5 7.6 %collective-permute-start.24 = (bf16[128,1024]{1,0:T(8,128)(2,1)S(1)}, bf16[128,1024]{1,0:T(8,128)(2,1)S(1)}, u32[]{:S(2)}, u32[]{:S(2)}) collective-permute-start(bf16[128,1024]{1,0:T(8,128)(2,1)S(1)} %get-tuple-element.135), channel_id=1, source_target_pairs={{0,52},{4,0},{16,4},{20,16},{32,20},{36,32},{48,36},{52,48},{1,53}... | collective-permute-start | bytes 786440 | tf_op jit(solution)/shard_map/ppermute | solution.py:63
  (5 other events, 59.8 us)

commit v9 on v7

--- a/solution.py
+++ b/solution.py
@@ -226,6 +226,12 @@
     copy_all([(own, src)], sems)
     make_logits(scale, src, tgt, logits, logits_t)
     part[...] = jnp.concatenate(columns_lse([logits_t], None))
+
+
+def pair_own_kernel(scale, near, other, own, tgt, *refs):
+    sems = refs[8]
+    pair_kernel(scale, near, other, tgt, *refs[:4], sems)
+    own_kernel(scale, own, tgt, *refs[4:8], sems)
 
 
 def far_kernel(scale, offsets, far_up, far_down, tgt, *refs):
@@ -418,7 +424,7 @@
         )
 
     made = [list(first), list(pair_logits(*pairs[1], ()))]
-    made.append(pair_logits(down, up, ()))
+    near, other = down, up
     half = rows // 2
     far = [jax.ShapeDtypeStruct((half, n_label), bf16)] * 2
     up, down = call(halves_kernel, far, [dma((2,))], up, down, flops=1, bytes_accessed=1)
@@ -428,13 +434,12 @@
         jax.ShapeDtypeStruct((rows, n_tgt), f32),
         jax.ShapeDtypeStruct((n_tgt, rows), f32),
     ]
-    made.append(
-        call(
-            functools.partial(own_kernel, scale),
-            [*single, jax.ShapeDtypeStruct((1, LANES), f32)], [dma((1,))],
-            own, tgt_block, **cost,
-        )
-    )
+    both = call(
+        functools.partial(pair_own_kernel, scale),
+        [*pair, pair_part, *single, jax.ShapeDtypeStruct((1, LANES), f32)], [dma((2,))],
+        near, other, own, tgt_block, **cost,
+    )
+    made += [both[:4], both[4:]]
     *last, part = call(
         functools.partial(far_kernel, scale),
         [*single, to_ring], [order, dma((2,))],

time: 170 us -> 170 us (level)
    pallas_call x21 -> x20, Pallas kernels: 26.7 us -> 26.7 us  [call(): pl.pallas_call(kernel, out_shape=outs, in_specs=specs, out_specs=[IN_HBM...]
where the time goes in v9:
time: 170 us
  blocking collectives  69.6 us (41%)
  starting transfers between devices  48.4 us (28%)
  Pallas kernels  26.7 us (16%)
  waiting for transfers between devices  20.4 us (12%)
  other arithmetic  3.52 us (2%)
    all_to_all x3, blocking collectives, shards(): gathered = lax.all_to_all(part, SPREAD, 0, 0)  35.2 us
    all_to_all x3, blocking collectives, shards(): gathered = lax.all_to_all(part, RING, 0, 0)  34.4 us
    ppermute x16, starting transfers between devices, shift(): lax.ppermute(value, RING, [(i, (i + step) % size) for i in range(size)])  29.3 us
    pallas_call x20, Pallas kernels, call(): pl.pallas_call(kernel, out_shape=outs, in_specs=specs, out_specs=[IN_HBM...  26.7 us
    ppermute x16, waiting for transfers between devices, shift(): lax.ppermute(value, RING, [(i, (i + step) % size) for i in range(size)])  13.6 us
    ppermute x3, starting transfers between devices, gather_axis(): lax.ppermute(block, axis, [((i + k) % size, i) for i in range(size)])  5.83 us
    all_to_all x1, starting transfers between devices, shards(): parts = lax.all_to_all(sent.reshape(plane, columns, depth), PLANE, 0, 0)  5.58 us
    ppermute x2, starting transfers between devices, shards(): lax.ppermute(block, 'x', [((i + k) % 4, i) for i in range(4)])  3.8 us
  transfers between devices with their start and end apart: 26, of which 10 were waited for; matrix products, arithmetic and copies ran while one was open for 1% of the time, Pallas kernels for 6%

profile of v9, /device:TPU:2, one launch (start us, length us, event | category | flops | bytes accessed | tf_op | source)
XLA Modules:
  0.0 169.5 jit_solution(4572882851055308290)
XLA Ops:
  4.3 4.0 %collective-permute-start = (bf16[128,1152]{1,0:T(8,128)(2,1)S(1)}, bf16[128,1152]{1,0:T(8,128)(2,1)S(1)}, u32[]{:S(2)}, u32[]{:S(2)}) collective-permute-start(bf16[128,1152]{1,0:T(8,128)(2,1)S(1)} %get-tuple-element.70.own), channel_id=1, source_target_pairs={{0,52},{4,0},{16,4},{20,16},{32,20},{36,32},{48,36},{52,48},{1,53}... | collective-permute-start | bytes 884744 | tf_op jit(solution)/shard_map/ppermute | solution.py:63
  9.9 2.9 %collective-permute-start.3 = (bf16[32,1152]{1,0:T(8,128)(2,1)S(1)}, bf16[32,1152]{1,0:T(8,128)(2,1)S(1)}, u32[]{:S(2)}, u32[]{:S(2)}) collective-permute-start(bf16[32,1152]{1,0:T(8,128)(2,1)S(1)} %get-tuple-element.71.refs_0_), channel_id=1, source_target_pairs={{2,0},{3,1},{0,2},{1,3},{6,4},{7,5},{4,6},{5,7},{10,8},{11,9},{8,1... | collective-permute-start | bytes 221192 | tf_op jit(solution)/shard_map/ppermute | solution.py:374
  19.8 3.2 %collective-permute-start.11 = (bf16[128,1152]{1,0:T(8,128)(2,1)S(1)}, bf16[128,1152]{1,0:T(8,128)(2,1)S(1)}, u32[]{:S(2)}, u32[]{:S(2)}) collective-permute-start(bf16[128,1152]{1,0:T(8,128)(2,1)S(1)} %collective-permute-done.near), channel_id=1, source_target_pairs={{0,52},{4,0},{16,4},{20,16},{32,20},{36,32},{48,36},{52,48},{1,53}... | collective-permute-start | bytes 884744 | tf_op jit(solution)/shard_map/ppermute | solution.py:63
  23.0 3.0 %collective-permute-start.6 = (bf16[128,1152]{1,0:T(8,128)(2,1)S(1)}, bf16[128,1152]{1,0:T(8,128)(2,1)S(1)}, u32[]{:S(2)}, u32[]{:S(2)}) collective-permute-start(bf16[128,1152]{1,0:T(8,128)(2,1)S(1)} %shard_map.68.own), channel_id=1, source_target_pairs={{128,0},{192,64},{0,128},{64,192},{129,1},{193,65},{1,129},{65,193... | collective-permute-start | bytes 884744 | tf_op jit(solution)/shard_map/ppermute | solution.py:389
  26.0 2.2 %collective-permute-start.5 = (bf16[128,1152]{1,0:T(8,128)(2,1)S(1)}, bf16[128,1152]{1,0:T(8,128)(2,1)S(1)}, u32[]{:S(2)}, u32[]{:S(2)}) collective-permute-start(bf16[128,1152]{1,0:T(8,128)(2,1)S(1)} %shard_map.68.own), channel_id=1, source_target_pairs={{64,0},{128,64},{192,128},{0,192},{65,1},{129,65},{193,129},{1,193... | collective-permute-start | bytes 884744 | tf_op jit(solution)/shard_map/ppermute | solution.py:387
  29.0 3.2 %collective-permute-start.12 = (bf16[128,1152]{1,0:T(8,128)(2,1)S(1)}, bf16[128,1152]{1,0:T(8,128)(2,1)S(1)}, u32[]{:S(2)}, u32[]{:S(2)}) collective-permute-start(bf16[128,1152]{1,0:T(8,128)(2,1)S(1)} %collective-permute-done.11.near), channel_id=1, source_target_pairs={{0,52},{4,0},{16,4},{20,16},{32,20},{36,32},{48,36},{52,48},{1,53}... | collective-permute-start | bytes 884744 | tf_op jit(solution)/shard_map/ppermute | solution.py:63
  33.2 2.8 %collective-permute-done.5.first = bf16[128,1152]{1,0:T(8,128)(2,1)S(1)} collective-permute-done((bf16[128,1152]{1,0:T(8,128)(2,1)S(1)}, bf16[128,1152]{1,0:T(8,128)(2,1)S(1)}, u32[]{:S(2)}, u32[]{:S(2)}) %collective-permute-start.5) | collective-permute-done | bytes 294944 | tf_op jit(solution)/shard_map/ppermute | solution.py:387
  37.5 3.5 %collective-permute-start.15 = (bf16[64,1152]{1,0:T(8,128)(2,1)S(1)}, bf16[64,1152]{1,0:T(8,128)(2,1)S(1)}, u32[]{:S(2)}, u32[]{:S(2)}) collective-permute-start(bf16[64,1152]{1,0:T(8,128)(2,1)S(1)} %get-tuple-element.84), channel_id=1, source_target_pairs={{0,52},{4,0},{16,4},{20,16},{32,20},{36,32},{48,36},{52,48},{1,53}... | collective-permute-start | bytes 442376 | tf_op jit(solution)/shard_map/ppermute | solution.py:63
  47.9 13.6 %all_to_all.35.refs_5_ = f32[8,8,128]{2,1,0:T(8,128)S(1)} all-to-all(f32[8,8,128]{2,1,0:T(8,128)S(1)} %get-tuple-element.95), channel_id=1, replica_groups=mesh['x'=4,'zh'=4,'core'=2,'zl'=2,'y'=4] {'zh','zl'}, dimensions={0} | all-to-all | bytes 65536 | tf_op jit(solution)/shard_map/all_to_all | solution.py:454
  63.1 12.7 %all_to_all.36.refs_5_ = f32[32,8,128]{2,1,0:T(8,128)S(1)} all-to-all(f32[32,8,128]{2,1,0:T(8,128)S(1)} %get-tuple-element.96), channel_id=1, replica_groups=mesh['x'=4,'zh'=4,'core'=2,'zl'=2,'y'=4] {'x','y','core'}, dimensions={0} | all-to-all | bytes 262144 | tf_op jit(solution)/shard_map/all_to_all | solution.py:460
  77.4 10.4 %all_to_all.37.refs_5_ = f32[8,8,128]{2,1,0:T(8,128)S(1)} all-to-all(f32[8,8,128]{2,1,0:T(8,128)S(1)} %shard_map.76), channel_id=1, replica_groups=mesh['x'=4,'zh'=4,'core'=2,'zl'=2,'y'=4] {'zh','zl'}, dimensions={0} | all-to-all | bytes 65536 | tf_op jit(solution)/shard_map/all_to_all | solution.py:454
  89.5 11.3 %all_to_all.38.refs_5_ = f32[32,8,128]{2,1,0:T(8,128)S(1)} all-to-all(f32[32,8,128]{2,1,0:T(8,128)S(1)} %get-tuple-element.97), channel_id=1, replica_groups=mesh['x'=4,'zh'=4,'core'=2,'zl'=2,'y'=4] {'x','y','core'}, dimensions={0} | all-to-all | bytes 262144 | tf_op jit(solution)/shard_map/all_to_all | solution.py:460
  102.4 10.4 %all_to_all.39.refs_5_ = f32[8,8,128]{2,1,0:T(8,128)S(1)} all-to-all(f32[8,8,128]{2,1,0:T(8,128)S(1)} %shard_map.78), channel_id=1, replica_groups=mesh['x'=4,'zh'=4,'core'=2,'zl'=2,'y'=4] {'zh','zl'}, dimensions={0} | all-to-all | bytes 65536 | tf_op jit(solution)/shard_map/all_to_all | solution.py:454
  114.4 11.3 %all_to_all.40.refs_1_ = f32[32,8,128]{2,1,0:T(8,128)S(1)} all-to-all(f32[32,8,128]{2,1,0:T(8,128)S(1)} %get-tuple-element.98), channel_id=1, replica_groups=mesh['x'=4,'zh'=4,'core'=2,'zl'=2,'y'=4] {'x','y','core'}, dimensions={0} | all-to-all | bytes 262144 | tf_op jit(solution)/shard_map/all_to_all | solution.py:460
  126.9 2.5 %shard_map.81 = (f32[512,1024]{1,0:T(8,128)S(1)}, bf16[512,1024]{1,0:T(8,128)(2,1)S(1)}) custom-call(f32[1024,256]{1,0:T(8,128)S(1)} %get-tuple-element.76.refs_0_, f32[1024,256]{1,0:T(8,128)S(1)} %get-tuple-element.78.refs_1_, f32[1024,256]{1,0:T(8,128)S(1)} %get-tuple-element.81.refs_2_, f32[1024,128]{1,0:T(8,128)S(1)} %get-tuple-element.82.refs_3_, ...), custom_call_target="tpu_custom_call" | custom-call | flops 2147483648 | bytes 8388608 | tf_op jit(solution)/shard_map/pallas_call | solution.py:48
  130.1 2.7 %collective-permute-start.18 = (bf16[64,1024]{1,0:T(8,128)(2,1)S(1)}, bf16[64,1024]{1,0:T(8,128)(2,1)S(1)}, u32[]{:S(2)}, u32[]{:S(2)}) collective-permute-start(bf16[64,1024]{1,0:T(8,128)(2,1)S(1)} %get-tuple-element.109), channel_id=1, source_target_pairs={{0,52},{4,0},{16,4},{20,16},{32,20},{36,32},{48,36},{52,48},{1,53}... | collective-permute-start | bytes 393224 | tf_op jit(solution)/shard_map/ppermute | solution.py:63
  132.8 2.8 %shard_map.82 = (f32[128,1024]{1,0:T(8,128)S(1)}, f32[128,1024]{1,0:T(8,128)S(1)}, f32[128,1024]{1,0:T(8,128)S(1)}, f32[128,1024]{1,0:T(8,128)S(1)}, f32[128,102...) custom-call(s32[6]{0:T(128)S(1)} %stack.27.offsets, f32[256,1024]{1,0:T(8,128)S(1)} %get-tuple-element.91.refs_0_, ...), custom_call_target="tpu_custom_call" | custom-call | flops 536870912 | bytes 4194304 | tf_op jit(solution)/shard_map/pallas_call | solution.py:48
  137.6 5.6 %all-to-all-start.6 = ((bf16[16,32,1024]{2,1,0:T(8,128)(2,1)}), bf16[16,32,1024]{2,1,0:T(8,128)(2,1)}, u32[]{:S(2)}, u32[]{:S(2)}) async-start(bf16[16,32,1024]{2,1,0:T(8,128)(2,1)} %bitcast.9), calls=%async_computation.6 | async-start | bytes 2097152 | tf_op jit(solution)/shard_map/all_to_all | solution.py:497
  143.4 3.2 %collective-permute-start.20 = (bf16[128,1024]{1,0:T(8,128)(2,1)S(1)}, bf16[128,1024]{1,0:T(8,128)(2,1)S(1)}, u32[]{:S(2)}, u32[]{:S(2)}) collective-permute-start(bf16[128,1024]{1,0:T(8,128)(2,1)S(1)} %get-tuple-element.126), channel_id=1, source_target_pairs={{0,52},{4,0},{16,4},{20,16},{32,20},{36,32},{48,36},{52,48},{1,53}... | collective-permute-start | bytes 786440 | tf_op jit(solution)/shard_map/ppermute | solution.py:63
  146.6 5.5 %collective-permute-done.19.up = bf16[128,1024]{1,0:T(8,128)(2,1)S(1)} collective-permute-done((bf16[128,1024]{1,0:T(8,128)(2,1)S(1)}, bf16[128,1024]{1,0:T(8,128)(2,1)S(1)}, u32[]{:S(2)}, u32[]{:S(2)}) %collective-permute-start.19) | collective-permute-done | bytes 262176 | tf_op jit(solution)/shard_map/ppermute | solution.py:63
  152.3 3.2 %collective-permute-start.22 = (bf16[128,1024]{1,0:T(8,128)(2,1)S(1)}, bf16[128,1024]{1,0:T(8,128)(2,1)S(1)}, u32[]{:S(2)}, u32[]{:S(2)}) collective-permute-start(bf16[128,1024]{1,0:T(8,128)(2,1)S(1)} %get-tuple-element.130), channel_id=1, source_target_pairs={{0,52},{4,0},{16,4},{20,16},{32,20},{36,32},{48,36},{52,48},{1,53}... | collective-permute-start | bytes 786440 | tf_op jit(solution)/shard_map/ppermute | solution.py:63
  155.6 4.7 %collective-permute-done.21.up = bf16[128,1024]{1,0:T(8,128)(2,1)S(1)} collective-permute-done((bf16[128,1024]{1,0:T(8,128)(2,1)S(1)}, bf16[128,1024]{1,0:T(8,128)(2,1)S(1)}, u32[]{:S(2)}, u32[]{:S(2)}) %collective-permute-start.21) | collective-permute-done | bytes 262176 | tf_op jit(solution)/shard_map/ppermute | solution.py:63
  160.5 3.2 %collective-permute-start.24 = (bf16[128,1024]{1,0:T(8,128)(2,1)S(1)}, bf16[128,1024]{1,0:T(8,128)(2,1)S(1)}, u32[]{:S(2)}, u32[]{:S(2)}) collective-permute-start(bf16[128,1024]{1,0:T(8,128)(2,1)S(1)} %get-tuple-element.135), channel_id=1, source_target_pairs={{0,52},{4,0},{16,4},{20,16},{32,20},{36,32},{48,36},{52,48},{1,53}... | collective-permute-start | bytes 786440 | tf_op jit(solution)/shard_map/ppermute | solution.py:63
  165.8 2.3 %collective-permute-done.23 = bf16[128,1024]{1,0:T(8,128)(2,1)S(1)} collective-permute-done((bf16[128,1024]{1,0:T(8,128)(2,1)S(1)}, bf16[128,1024]{1,0:T(8,128)(2,1)S(1)}, u32[]{:S(2)}, u32[]{:S(2)}) %collective-permute-start.23) | collective-permute-done | bytes 262176 | tf_op jit(solution)/shard_map/ppermute | solution.py:63
  (63 shorter events, 38.5 us)
Async XLA Ops:
  2.3 15.8 %collective-permute-start.1 = (bf16[128,1152]{1,0:T(8,128)(2,1)S(1)}, bf16[128,1152]{1,0:T(8,128)(2,1)S(1)}, u32[]{:S(2)}, u32[]{:S(2)}) collective-permute-start(bf16[128,1152]{1,0:T(8,128)(2,1)S(1)} %get-tuple-element.70.own), channel_id=1, source_target_pairs={{0,4},{4,16},{16,20},{20,32},{32,36},{36,48},{48,52},{52,0},{1,5},... | collective-permute-start | bytes 884744 | tf_op jit(solution)/shard_map/ppermute | solution.py:63
  4.3 13.9 %collective-permute-start = (bf16[128,1152]{1,0:T(8,128)(2,1)S(1)}, bf16[128,1152]{1,0:T(8,128)(2,1)S(1)}, u32[]{:S(2)}, u32[]{:S(2)}) collective-permute-start(bf16[128,1152]{1,0:T(8,128)(2,1)S(1)} %get-tuple-element.70.own), channel_id=1, source_target_pairs={{0,52},{4,0},{16,4},{20,16},{32,20},{36,32},{48,36},{52,48},{1,53}... | collective-permute-start | bytes 884744 | tf_op jit(solution)/shard_map/ppermute | solution.py:63
  8.4 6.4 %collective-permute-start.4 = (bf16[32,1152]{1,0:T(8,128)(2,1)S(1)}, bf16[32,1152]{1,0:T(8,128)(2,1)S(1)}, u32[]{:S(2)}, u32[]{:S(2)}) collective-permute-start(bf16[32,1152]{1,0:T(8,128)(2,1)S(1)} %get-tuple-element.71.refs_0_), channel_id=1, source_target_pairs={{3,0},{0,1},{1,2},{2,3},{7,4},{4,5},{5,6},{6,7},{11,8},{8,9},{9,10... | collective-permute-start | bytes 221192 | tf_op jit(solution)/shard_map/ppermute | solution.py:374
  9.9 6.2 %collective-permute-start.3 = (bf16[32,1152]{1,0:T(8,128)(2,1)S(1)}, bf16[32,1152]{1,0:T(8,128)(2,1)S(1)}, u32[]{:S(2)}, u32[]{:S(2)}) collective-permute-start(bf16[32,1152]{1,0:T(8,128)(2,1)S(1)} %get-tuple-element.71.refs_0_), channel_id=1, source_target_pairs={{2,0},{3,1},{0,2},{1,3},{6,4},{7,5},{4,6},{5,7},{10,8},{11,9},{8,1... | collective-permute-start | bytes 221192 | tf_op jit(solution)/shard_map/ppermute | solution.py:374
  18.2 10.1 %collective-permute-start.7 = (bf16[128,1152]{1,0:T(8,128)(2,1)S(1)}, bf16[128,1152]{1,0:T(8,128)(2,1)S(1)}, u32[]{:S(2)}, u32[]{:S(2)}) collective-permute-start(bf16[128,1152]{1,0:T(8,128)(2,1)S(1)} %shard_map.68.own), channel_id=1, source_target_pairs={{192,0},{0,64},{64,128},{128,192},{193,1},{1,65},{65,129},{129,193... | collective-permute-start | bytes 884744 | tf_op jit(solution)/shard_map/ppermute | solution.py:387
  19.8 9.2 %collective-permute-start.9 = (bf16[128,1152]{1,0:T(8,128)(2,1)S(1)}, bf16[128,1152]{1,0:T(8,128)(2,1)S(1)}, u32[]{:S(2)}, u32[]{:S(2)}) collective-permute-start(bf16[128,1152]{1,0:T(8,128)(2,1)S(1)} %collective-permute-done.1.other), channel_id=1, source_target_pairs={{0,4},{4,16},{16,20},{20,32},{32,36},{36,48},{48,52},{52,0},{1,5},... | collective-permute-start | bytes 884744 | tf_op jit(solution)/shard_map/ppermute | solution.py:63
  19.8 9.3 %collective-permute-start.11 = (bf16[128,1152]{1,0:T(8,128)(2,1)S(1)}, bf16[128,1152]{1,0:T(8,128)(2,1)S(1)}, u32[]{:S(2)}, u32[]{:S(2)}) collective-permute-start(bf16[128,1152]{1,0:T(8,128)(2,1)S(1)} %collective-permute-done.near), channel_id=1, source_target_pairs={{0,52},{4,0},{16,4},{20,16},{32,20},{36,32},{48,36},{52,48},{1,53}... | collective-permute-start | bytes 884744 | tf_op jit(solution)/shard_map/ppermute | solution.py:63
  23.0 10.2 %collective-permute-start.6 = (bf16[128,1152]{1,0:T(8,128)(2,1)S(1)}, bf16[128,1152]{1,0:T(8,128)(2,1)S(1)}, u32[]{:S(2)}, u32[]{:S(2)}) collective-permute-start(bf16[128,1152]{1,0:T(8,128)(2,1)S(1)} %shard_map.68.own), channel_id=1, source_target_pairs={{128,0},{192,64},{0,128},{64,192},{129,1},{193,65},{1,129},{65,193... | collective-permute-start | bytes 884744 | tf_op jit(solution)/shard_map/ppermute | solution.py:389
  26.0 10.0 %collective-permute-start.5 = (bf16[128,1152]{1,0:T(8,128)(2,1)S(1)}, bf16[128,1152]{1,0:T(8,128)(2,1)S(1)}, u32[]{:S(2)}, u32[]{:S(2)}) collective-permute-start(bf16[128,1152]{1,0:T(8,128)(2,1)S(1)} %shard_map.68.own), channel_id=1, source_target_pairs={{64,0},{128,64},{192,128},{0,192},{65,1},{129,65},{193,129},{1,193... | collective-permute-start | bytes 884744 | tf_op jit(solution)/shard_map/ppermute | solution.py:387
  28.2 7.7 %collective-permute-start.8 = (bf16[128,1152]{1,0:T(8,128)(2,1)S(1)}, bf16[128,1152]{1,0:T(8,128)(2,1)S(1)}, u32[]{:S(2)}, u32[]{:S(2)}) collective-permute-start(bf16[128,1152]{1,0:T(8,128)(2,1)S(1)} %collective-permute-done.7.third), channel_id=1, source_target_pairs={{200,8},{8,72},{72,136},{136,200},{201,9},{9,73},{73,137},{137,201... | collective-permute-start | bytes 884744 | tf_op jit(solution)/shard_map/ppermute | solution.py:390
  28.9 8.0 %collective-permute-start.10 = (bf16[128,1152]{1,0:T(8,128)(2,1)S(1)}, bf16[128,1152]{1,0:T(8,128)(2,1)S(1)}, u32[]{:S(2)}, u32[]{:S(2)}) collective-permute-start(bf16[128,1152]{1,0:T(8,128)(2,1)S(1)} %collective-permute-done.9.other), channel_id=1, source_target_pairs={{0,4},{4,16},{16,20},{20,32},{32,36},{36,48},{48,52},{52,0},{1,5},... | collective-permute-start | bytes 884744 | tf_op jit(solution)/shard_map/ppermute | solution.py:63
  29.0 7.9 %collective-permute-start.12 = (bf16[128,1152]{1,0:T(8,128)(2,1)S(1)}, bf16[128,1152]{1,0:T(8,128)(2,1)S(1)}, u32[]{:S(2)}, u32[]{:S(2)}) collective-permute-start(bf16[128,1152]{1,0:T(8,128)(2,1)S(1)} %collective-permute-done.11.near), channel_id=1, source_target_pairs={{0,52},{4,0},{16,4},{20,16},{32,20},{36,32},{48,36},{52,48},{1,53}... | collective-permute-start | bytes 884744 | tf_op jit(solution)/shard_map/ppermute | solution.py:63
  37.4 8.7 %collective-permute-start.14 = (bf16[64,1152]{1,0:T(8,128)(2,1)S(1)}, bf16[64,1152]{1,0:T(8,128)(2,1)S(1)}, u32[]{:S(2)}, u32[]{:S(2)}) collective-permute-start(bf16[64,1152]{1,0:T(8,128)(2,1)S(1)} %get-tuple-element.83), channel_id=1, source_target_pairs={{0,4},{4,16},{16,20},{20,32},{32,36},{36,48},{48,52},{52,0},{1,5},... | collective-permute-start | bytes 442376 | tf_op jit(solution)/shard_map/ppermute | solution.py:63
  37.5 8.6 %collective-permute-start.15 = (bf16[64,1152]{1,0:T(8,128)(2,1)S(1)}, bf16[64,1152]{1,0:T(8,128)(2,1)S(1)}, u32[]{:S(2)}, u32[]{:S(2)}) collective-permute-start(bf16[64,1152]{1,0:T(8,128)(2,1)S(1)} %get-tuple-element.84), channel_id=1, source_target_pairs={{0,52},{4,0},{16,4},{20,16},{32,20},{36,32},{48,36},{52,48},{1,53}... | collective-permute-start | bytes 442376 | tf_op jit(solution)/shard_map/ppermute | solution.py:63
  129.3 7.2 %collective-permute-start.16 = (bf16[512,1024]{1,0:T(8,128)(2,1)S(1)}, bf16[512,1024]{1,0:T(8,128)(2,1)S(1)}, u32[]{:S(2)}, u32[]{:S(2)}) collective-permute-start(bf16[512,1024]{1,0:T(8,128)(2,1)S(1)} %get-tuple-element.107), channel_id=1, source_target_pairs={{0,8},{8,0},{1,9},{9,1},{2,10},{10,2},{3,11},{11,3},{4,12},{12,4},... | collective-permute-start | bytes 3145736 | tf_op jit(solution)/shard_map/ppermute | solution.py:490
  129.5 7.0 %collective-permute-start.17 = (bf16[64,1024]{1,0:T(8,128)(2,1)S(1)}, bf16[64,1024]{1,0:T(8,128)(2,1)S(1)}, u32[]{:S(2)}, u32[]{:S(2)}) collective-permute-start(bf16[64,1024]{1,0:T(8,128)(2,1)S(1)} %get-tuple-element.108), channel_id=1, source_target_pairs={{0,4},{4,16},{16,20},{20,32},{32,36},{36,48},{48,52},{52,0},{1,5},... | collective-permute-start | bytes 393224 | tf_op jit(solution)/shard_map/ppermute | solution.py:63
  130.1 6.4 %collective-permute-start.18 = (bf16[64,1024]{1,0:T(8,128)(2,1)S(1)}, bf16[64,1024]{1,0:T(8,128)(2,1)S(1)}, u32[]{:S(2)}, u32[]{:S(2)}) collective-permute-start(bf16[64,1024]{1,0:T(8,128)(2,1)S(1)} %get-tuple-element.109), channel_id=1, source_target_pairs={{0,52},{4,0},{16,4},{20,16},{32,20},{36,32},{48,36},{52,48},{1,53}... | collective-permute-start | bytes 393224 | tf_op jit(solution)/shard_map/ppermute | solution.py:63
  137.6 22.8 %all-to-all-start.6 = ((bf16[16,32,1024]{2,1,0:T(8,128)(2,1)}), bf16[16,32,1024]{2,1,0:T(8,128)(2,1)}, u32[]{:S(2)}, u32[]{:S(2)}) async-start(bf16[16,32,1024]{2,1,0:T(8,128)(2,1)} %bitcast.9), calls=%async_computation.6 | async-start | bytes 2097152 | tf_op jit(solution)/shard_map/all_to_all | solution.py:497
  143.3 8.9 %collective-permute-start.19 = (bf16[128,1024]{1,0:T(8,128)(2,1)S(1)}, bf16[128,1024]{1,0:T(8,128)(2,1)S(1)}, u32[]{:S(2)}, u32[]{:S(2)}) collective-permute-start(bf16[128,1024]{1,0:T(8,128)(2,1)S(1)} %get-tuple-element.124), channel_id=1, source_target_pairs={{0,4},{4,16},{16,20},{20,32},{32,36},{36,48},{48,52},{52,0},{1,5},... | collective-permute-start | bytes 786440 | tf_op jit(solution)/shard_map/ppermute | solution.py:63
  143.4 8.7 %collective-permute-start.20 = (bf16[128,1024]{1,0:T(8,128)(2,1)S(1)}, bf16[128,1024]{1,0:T(8,128)(2,1)S(1)}, u32[]{:S(2)}, u32[]{:S(2)}) collective-permute-start(bf16[128,1024]{1,0:T(8,128)(2,1)S(1)} %get-tuple-element.126), channel_id=1, source_target_pairs={{0,52},{4,0},{16,4},{20,16},{32,20},{36,32},{48,36},{52,48},{1,53}... | collective-permute-start | bytes 786440 | tf_op jit(solution)/shard_map/ppermute | solution.py:63
  152.2 8.0 %collective-permute-start.21 = (bf16[128,1024]{1,0:T(8,128)(2,1)S(1)}, bf16[128,1024]{1,0:T(8,128)(2,1)S(1)}, u32[]{:S(2)}, u32[]{:S(2)}) collective-permute-start(bf16[128,1024]{1,0:T(8,128)(2,1)S(1)} %get-tuple-element.128), channel_id=1, source_target_pairs={{0,4},{4,16},{16,20},{20,32},{32,36},{36,48},{48,52},{52,0},{1,5},... | collective-permute-start | bytes 786440 | tf_op jit(solution)/shard_map/ppermute | solution.py:63
  152.3 8.0 %collective-permute-start.22 = (bf16[128,1024]{1,0:T(8,128)(2,1)S(1)}, bf16[128,1024]{1,0:T(8,128)(2,1)S(1)}, u32[]{:S(2)}, u32[]{:S(2)}) collective-permute-start(bf16[128,1024]{1,0:T(8,128)(2,1)S(1)} %get-tuple-element.130), channel_id=1, source_target_pairs={{0,52},{4,0},{16,4},{20,16},{32,20},{36,32},{48,36},{52,48},{1,53}... | collective-permute-start | bytes 786440 | tf_op jit(solution)/shard_map/ppermute | solution.py:63
  160.4 7.7 %collective-permute-start.23 = (bf16[128,1024]{1,0:T(8,128)(2,1)S(1)}, bf16[128,1024]{1,0:T(8,128)(2,1)S(1)}, u32[]{:S(2)}, u32[]{:S(2)}) collective-permute-start(bf16[128,1024]{1,0:T(8,128)(2,1)S(1)} %get-tuple-element.134), channel_id=1, source_target_pairs={{0,4},{4,16},{16,20},{20,32},{32,36},{36,48},{48,52},{52,0},{1,5},... | collective-permute-start | bytes 786440 | tf_op jit(solution)/shard_map/ppermute | solution.py:63
  160.5 7.6 %collective-permute-start.24 = (bf16[128,1024]{1,0:T(8,128)(2,1)S(1)}, bf16[128,1024]{1,0:T(8,128)(2,1)S(1)}, u32[]{:S(2)}, u32[]{:S(2)}) collective-permute-start(bf16[128,1024]{1,0:T(8,128)(2,1)S(1)} %get-tuple-element.135), channel_id=1, source_target_pairs={{0,52},{4,0},{16,4},{20,16},{32,20},{36,32},{48,36},{52,48},{1,53}... | collective-permute-start | bytes 786440 | tf_op jit(solution)/shard_map/ppermute | solution.py:63
  (5 other events, 59.8 us)
